TPU v7x, 512 devices: a whole 4x8x8 slice. The times are simulated.
512 devices in a mesh: head: 8 (over z), vocab: 64 (over x, y, core).
Axes of the slice: x: 4, y: 8, z: 8, core: 2. Of those that a mesh axis runs over, the one named last changes fastest.
Arguments:
- heads_out: bfloat16 [1024, 64, 128], P('vocab', 'head'), may hold values from -240 to 240, as said below
- unembed: bfloat16 [64, 128, 65536], P('head', None, 'vocab'), may hold values from -0.5 to 0.5
- targets: int32 [1024], replicated, may hold values from 0 to 65535
Outputs:
- log_probs: bfloat16 [1024, 65536], P('head', 'vocab')
- attribution: float32 [1024, 64], P(None, 'head')
Inputs may be any that keep to these rules, and one draw needn't show every extreme that they name: heads_out is real-valued, each token scaled by its own positive factor.
All inputs are finite; a program needn't handle non-finite values.
Results may differ from a plain program's by a relative error of at most 0.001.
Values may be sent and summed in bfloat16 or wider, within the bound.
No kernel may reach another device: no remote copies, remote signals or barrier semaphores. Data moves between devices by JAX's collectives and lax.ppermute only.
A program may use at most 64 MiB of HBM per device.

v0:
```python
import jax
import jax.numpy as jnp
from jax import lax
from jax.sharding import PartitionSpec as P


def partial_logits(rows, unembed):
    return lax.dot_general(
        rows, unembed, (((1, 2), (0, 1)), ((), ())), preferred_element_type=jnp.float32
    )


def on_device(heads_out, unembed, targets):
    slab_width = unembed.shape[2]
    gathered = lax.all_gather(heads_out, "vocab", axis=0, tiled=True)
    slab_start = lax.axis_index("vocab") * slab_width
    local_ids = targets - slab_start
    inside = (local_ids >= 0) & (local_ids < slab_width)
    safe_ids = jnp.clip(local_ids, 0, slab_width - 1)
    picked = jnp.take(unembed, safe_ids, axis=2)
    own_terms = jnp.einsum("thd,hdt->th", gathered, picked, preferred_element_type=jnp.float32)
    own_terms = jnp.where(inside[:, None], own_terms, 0.0)
    attribution = lax.psum(own_terms, "vocab")
    logits = lax.psum_scatter(
        partial_logits(gathered, unembed), "head", scatter_dimension=0, tiled=True
    )
    local_top = jnp.max(logits, axis=1, keepdims=True)
    top = lax.pmax(local_top, "vocab")
    total = lax.psum(jnp.sum(jnp.exp(logits - top), axis=1, keepdims=True), "vocab")
    log_probs = (logits - top - jnp.log(total)).astype(jnp.bfloat16)
    return (log_probs, attribution)


def solution(mesh):
    in_specs = (P("vocab", "head", None), P("head", None, "vocab"), P())
    out_specs = (P("head", "vocab"), P(None, "head"))
    return jax.shard_map(
        on_device, mesh=mesh, in_specs=in_specs, out_specs=out_specs, check_vma=False
    )
```

profile of v0, /device:TPU:1, one launch (start us, length us, event | category | flops | bytes accessed | tf_op | source)
XLA Modules:
  0.0 540.5 jit_solution(15151555867465054311)
XLA Ops:
  7.2 0.0 all-gather.2.cloned.1.call-start
  7.2 1.4 copy.6
  8.6 0.0 all-gather.2.cloned.1.call-update
  8.6 0.0 reduce-scatter.2.cloned.1.call-start
  8.7 86.6 %all-gather.2.cloned.1.call-done = bf16[1024,8,128]{2,0,1:T(8,128)(2,1)} async-done(((bf16[16,8,128]{2,0,1:T(8,128)(2,1)}), bf16[1024,8,128]{2,0,1:T(8,128)(2,1)}) %all-gather.2.cloned.1.call-update) | async-done | bytes 2097168 | tf_op jit(solution)/shard_map/all_gather | solution.py:15
  95.3 6.5 %convolution_bitcast_fusion = f32[1024,1024]{1,0:T(8,128)} fusion(bf16[1024,8,128]{2,0,1:T(8,128)(2,1)} %all-gather.2.cloned.1.call-done, bf16[8,128,1024]{2,1,0:T(8,128)(2,1)} %param.4), kind=kOutput, calls=%fused_computation.2 | convolution fusion | flops 2147483648 | bytes 8388608 | tf_op jit(solution)/shard_map/dot_general | solution.py:8
  101.8 0.0 reduce-scatter.2.cloned.1.call-update
  101.8 0.0 copy-start.1
  101.8 3.4 copy.7
  105.2 0.0 copy-done.1
  105.2 7.6 %gather_fusion = bf16[1024,8,128]{2,1,0:T(8,128)(2,1)} fusion(bf16[8,128,1024]{1,0,2:T(8,128)(2,1)S(1)} %copy.7, s32[1024]{0:T(1024)S(1)} %fusion), kind=kCustom, calls=%fused_computation | custom fusion | bytes 4198400 | tf_op jit(solution)/shard_map/jit(_take)/gather | solution.py:20
  112.8 0.0 copy-start
  112.8 5.7 %select_convert_fusion = f32[1024,8,128]{2,1,0:T(8,128)S(1)} fusion(bf16[1024,8,128]{2,1,0:T(8,128)(2,1)} %gather_fusion, pred[1024]{0:T(1024)(128)(4,1)S(1)} %get-tuple-element.5), kind=kLoop, calls=%fused_computation.3 | loop fusion | flops 2097152 | bytes 6292480
  118.5 0.0 copy-done
  118.5 1.5 multiply_reduce_fusion
  120.0 39.7 %reduce-scatter.2.cloned.1.call-done = f32[128,1024]{1,0:T(8,128)} async-done(((f32[1024,1024]{1,0:T(8,128)}), f32[128,1024]{1,0:T(8,128)}) %reduce-scatter.2.cloned.1.call-update) | async-done | bytes 524304 | tf_op jit(solution)/shard_map/reduce_scatter | solution.py:24
  159.7 1.2 reduce_max.9
  160.9 124.0 %pmax.7 = f32[128]{0:T(128)S(1)} all-reduce(f32[128]{0:T(128)S(1)} %reduce_max.9), channel_id=1, replica_groups=mesh['head'=8,'vocab'=64] {'vocab'}, use_global_device_ids=true, to_apply=%region_2.3 | all-reduce | flops 128 | bytes 1024 | tf_op jit(solution)/shard_map/pmax | solution.py:28
  284.9 1.3 exponential_reduce_fusion
  286.2 245.6 %all-reduce = (f32[128,1]{0,1:T(1,128)S(1)}, f32[1024,8]{0,1:T(8,128)}) all-reduce(f32[128,1]{0,1:T(1,128)S(1)} %bitcast.10, f32[1024,8]{0,1:T(8,128)S(1)} %broadcast_select_fusion), channel_id=1, replica_groups=mesh['head'=8,'vocab'=64] {'vocab'}, use_global_device_ids=true, to_apply=%region_4.5 | all-reduce | flops 8320 | bytes 66560 | tf_op jit(solution)/shard_map/psum | solution.py:29
  531.7 1.9 subtract_convert_fusion
  (4 shorter events, 0.0 us)
Async XLA Ops:
  7.2 88.1 %all-gather.2.cloned.1.call-start = ((), (), s32[]{:S(2)}) async-start(), calls=%async_computation.1 | async-start | bytes 2129920 | tf_op jit(solution)/shard_map/all_gather | solution.py:15
  8.6 151.1 %reduce-scatter.2.cloned.1.call-start = ((), (), s32[]{:S(2)}) async-start(), calls=%async_computation.2 | async-start | bytes 4718592 | tf_op jit(solution)/shard_map/reduce_scatter | solution.py:24
  101.8 3.4 copy-start.1
  112.8 5.7 %copy-start = (bf16[1024,8,128]{2,0,1:T(8,128)(2,1)S(1)}, bf16[1024,8,128]{2,0,1:T(8,128)(2,1)}, u32[]{:S(2)}) copy-start(bf16[1024,8,128]{2,0,1:T(8,128)(2,1)} %all-gather.2.cloned.1.call-done) | copy-start | bytes 6291460
Sparse Core Ops, SparseCore 0:
  11.7 83.5 all-gather.1
  101.9 57.7 reduce-scatter.1
where the time goes:
time: 542 us; the launch traced here: 540 us
  blocking collectives  370 us (68%)
  waiting for transfers between devices  126 us (23%)
  between operations  14.1 us (3%)
  local copies, waits for them, and re-layouts  12.4 us (2%)
  other arithmetic  11.5 us (2%)
  matrix products  6.48 us (1%)
    psum x1, blocking collectives, on_device(): lax.psum(jnp.sum(jnp.exp(logits - top), axis=1, keepdims=True), 'vocab')  246 us
    pmax x1, blocking collectives, on_device(): top = lax.pmax(local_top, 'vocab')  124 us
    all_gather x1, waiting for transfers between devices, on_device(): gathered = lax.all_gather(heads_out, 'vocab', axis=0, tiled=True)  86.6 us
    reduce_scatter x1, waiting for transfers between devices, on_device(): lax.psum_scatter(partial_logits(gathered, unembed), 'head', scatter_dimen...  39.7 us
  transfers between devices with their start and end apart: 2, of which 2 were waited for; matrix products, arithmetic and copies ran while one was open for 3% of the time, Pallas kernels for 0%

commit v1 on v0

v1 whole, which is shorter than its diff:
```python
import jax
import jax.numpy as jnp
from jax import lax
from jax.sharding import PartitionSpec as P

NX, NY, NC, NZ = 4, 8, 2, 8
SCALE = 0.125


def vocab_index(x, y, c):
    return (x * NY + y) * NC + c


Y_GROUPS = [[vocab_index(x, y, c) for y in range(NY)] for x in range(NX) for c in range(NC)]
X_GROUPS = [[vocab_index(x, y, c) for x in range(NX)] for y in range(NY) for c in range(NC)]
CORE_SWAP = [(v, v ^ 1) for v in range(NX * NY * NC)]
UP = [(z, (z + 1) % NZ) for z in range(NZ)]
DOWN = [(z, (z - 1) % NZ) for z in range(NZ)]


def share(block, groups, count):
    copies = jnp.broadcast_to(block[None], (count,) + block.shape)
    return lax.all_to_all(copies, "vocab", 0, 0, axis_index_groups=groups, tiled=True)


def coded(values):
    return (values * SCALE).astype(jnp.float16)


def decoded(values):
    return values.astype(jnp.float32) * (1.0 / SCALE)


def cores_in_order(values, core):
    pair = values.reshape((NC, -1) + values.shape[1:])
    return jnp.where(core == 0, pair, pair[::-1]).reshape(values.shape)


def on_device(heads_out, unembed, targets):
    per_device, heads, hd = heads_out.shape
    depth = heads * hd
    slab = unembed.shape[2]
    half = slab // 2
    weights = unembed.reshape(depth, slab)
    vocab_id = lax.axis_index("vocab")
    z = lax.axis_index("head")
    core = vocab_id % NC

    column = share(heads_out.reshape(per_device, depth), Y_GROUPS, NY)
    own = share(column, X_GROUPS, NX)
    other = lax.ppermute(own, "vocab", CORE_SWAP)
    rows = jnp.stack([own, other])
    rows = rows.reshape(2, NZ, NY // 2 * per_device, depth)

    def partial_logits(target):
        part = lax.dynamic_slice_in_dim(rows, target % NZ, 1, axis=1)[:, 0]
        return lax.dot_general(
            part.reshape(-1, depth), weights, (((1,), (0,)), ((), ())), preferred_element_type=jnp.float32
        )

    far = coded(partial_logits(z + 4))
    up = lax.ppermute(far[:, :half], "head", UP)
    down = lax.ppermute(far[:, half:], "head", DOWN)
    nothing = jnp.zeros((far.shape[0], half), jnp.float32)
    up = jnp.concatenate([decoded(up), nothing], axis=1)
    down = jnp.concatenate([nothing, decoded(down)], axis=1)
    for distance in (3, 2, 1):
        up = lax.ppermute(coded(partial_logits(z + distance) + up), "head", UP)
        down = lax.ppermute(coded(partial_logits(z - distance + NZ) + down), "head", DOWN)
        up, down = decoded(up), decoded(down)
    logits = partial_logits(z) + up + down

    ids = targets.reshape(NX, NY, NC, per_device)
    ids = jnp.where(core == 0, ids, ids[:, :, ::-1])
    ids = ids.transpose(2, 0, 1, 3).reshape(-1) - vocab_id * slab
    chosen = (ids[:, None] == jnp.arange(slab)[None, :]).astype(jnp.bfloat16)
    picked = lax.dot_general(chosen, weights, (((1,), (1,)), ((), ())), preferred_element_type=jnp.float32)
    terms = rows.reshape(-1, heads, hd).astype(jnp.float32) * picked.reshape(-1, heads, hd)
    terms = jnp.sum(terms, axis=-1).reshape(NC, NX, NY, per_device * heads)
    terms = jnp.where(core == 0, terms, terms[::-1])
    terms = terms.transpose(1, 2, 0, 3).reshape(NX * NY * NC, per_device * heads)
    own_terms = jnp.sum(lax.all_to_all(terms, "vocab", 0, 0, tiled=True), axis=0)

    top = jnp.max(logits, axis=1, keepdims=True)
    lse = top[:, 0] + jnp.log(jnp.sum(jnp.exp(logits - top), axis=1))
    message = jnp.stack([cores_in_order(lse, core), own_terms])
    messages = share(message, None, NX * NY * NC)
    every_lse, attribution = messages[:, 0], messages[:, 1]
    top = jnp.max(every_lse, axis=0)
    lse = top + jnp.log(jnp.sum(jnp.exp(every_lse - top[None]), axis=0))
    lse = cores_in_order(lse, core)
    log_probs = cores_in_order((logits - lse[:, None]).astype(jnp.bfloat16), core)
    log_probs = log_probs.reshape(NC, NY // 2, per_device, slab)
    log_probs = log_probs.transpose(1, 0, 2, 3).reshape(-1, slab)
    return (log_probs, attribution.reshape(-1, heads))


def solution(mesh):
    in_specs = (P("vocab", "head", None), P("head", None, "vocab"), P())
    out_specs = (P("head", "vocab"), P(None, "head"))
    return jax.shard_map(
        on_device, mesh=mesh, in_specs=in_specs, out_specs=out_specs, check_vma=False
    )
```

time: 542 us -> 142 us (0.26)
  blocking collectives: 370 us -> 63.9 us
  waiting for transfers between devices: 126 us -> 6.41 us
  starting transfers between devices: 0.08 us -> 37.4 us
  between operations: 14.1 us -> 1.12 us
    psum x1 -> x0, blocking collectives: 246 us -> none  [on_device(): lax.psum(jnp.sum(jnp.exp(logits - top), axis=1, keepdims=True), 'vocab')]
    pmax x1 -> x0, blocking collectives: 124 us -> none  [on_device(): top = lax.pmax(local_top, 'vocab')]
    all_gather x1 -> x0, waiting for transfers between devices: 86.6 us -> none  [on_device(): gathered = lax.all_gather(heads_out, 'vocab', axis=0, tiled=True)]
    all_to_all x0 -> x4, blocking collectives: none -> 63.9 us  [the longest x3 47.5 us: share(): lax.all_to_all(copies, 'vocab', 0, 0, axis_index_groups=groups, tiled=True)]
    reduce_scatter x1 -> x0, waiting for transfers between devices: 39.7 us -> none  [on_device(): lax.psum_scatter(partial_logits(gathered, unembed), 'head', scatter_dimen...]
    ppermute x0 -> x9, starting transfers between devices: none -> 37.4 us  [the longest x3 12.9 us: on_device(): lax.ppermute(coded(partial_logits(z - distance + NZ) + down), 'head', DOWN)]
    gather x1 -> x0, local copies, waits for them, and re-layouts: 7.58 us -> none  [on_device(): picked = jnp.take(unembed, safe_ids, axis=2)]
    ppermute x0 -> x9, waiting for transfers between devices: none -> 6.41 us  [the longest x3 4.43 us: on_device(): lax.ppermute(coded(partial_logits(z - distance + NZ) + down), 'head', DOWN)]
  transfers between devices with their start and end apart: 2 -> 9, of which waited for: 2 -> 3; matrix products, arithmetic and copies ran while one was open for 3% -> 17% of each run, Pallas kernels for 0% -> 0%
where the time goes in v1:
time: 142 us; the launch traced here: 141 us
  blocking collectives  63.9 us (45%)
  starting transfers between devices  37.4 us (26%)
  local copies, waits for them, and re-layouts  16.3 us (11%)
  matrix products  9.22 us (6%)
  other arithmetic  6.49 us (5%)
  waiting for transfers between devices  6.41 us (5%)
    all_to_all x3, blocking collectives, share(): lax.all_to_all(copies, 'vocab', 0, 0, axis_index_groups=groups, tiled=True)  47.5 us
    all_to_all x1, blocking collectives, on_device(): lax.all_to_all(terms, 'vocab', 0, 0, tiled=True)  16.3 us
    ppermute x3, starting transfers between devices, on_device(): lax.ppermute(coded(partial_logits(z - distance + NZ) + down), 'head', DOWN)  12.9 us
    ppermute x1, starting transfers between devices, on_device(): down = lax.ppermute(far[:, half:], 'head', DOWN)  8.59 us
    ppermute x3, starting transfers between devices, on_device(): up = lax.ppermute(coded(partial_logits(z + distance) + up), 'head', UP)  6.02 us
    ppermute x1, starting transfers between devices, on_device(): other = lax.ppermute(own, 'vocab', CORE_SWAP)  5.85 us
    convert_element_type x1, local copies, waits for them, and re-layouts, on_device(): rows.reshape(-1, heads, hd).astype(jnp.float32)  5.41 us
    dot_general x1, matrix products, on_device(): lax.dot_general(chosen, weights, (((1,), (1,)), ((), ())), preferred_elem...  5.35 us
  transfers between devices with their start and end apart: 9, of which 3 were waited for; matrix products, arithmetic and copies ran while one was open for 17% of the time, Pallas kernels for 0%

profile of v1, /device:TPU:1, one launch (start us, length us, event | category | flops | bytes accessed | tf_op | source)
XLA Modules:
  0.0 140.8 jit_solution(1299404610491025259)
XLA Ops:
  0.6 0.9 copy.27
  1.6 16.7 %all_to_all.24 = bf16[8,16,1024]{2,1,0:T(8,128)(2,1)S(1)} all-to-all(bf16[8,16,1024]{2,1,0:T(8,128)(2,1)S(1)} %broadcast_in_dim.9), channel_id=1, replica_groups={{0,2,4,6,8,10,12,14},{1,3,5,7,9,11,13,15},{16,18,20,22,24,26,28,30},{17..., dimensions={0} | all-to-all | bytes 524288 | tf_op jit(solution)/shard_map/all_to_all | solution.py:23
  18.5 17.0 %all_to_all.25 = bf16[4,8,16,1024]{3,2,1,0:T(8,128)(2,1)S(1)} all-to-all(bf16[4,8,16,1024]{3,2,1,0:T(8,128)(2,1)S(1)} %broadcast_in_dim.10), channel_id=1, replica_groups={{0,16,32,48},{1,17,33,49},{2,18,34,50},{3,19,35,51},{4,20,36,52},{5,21,..., dimensions={0} | all-to-all | bytes 2097152 | tf_op jit(solution)/shard_map/all_to_all | solution.py:23
  35.5 5.9 %collective-permute-start = (bf16[4,8,16,1024]{3,2,1,0:T(8,128)(2,1)S(1)}, bf16[4,8,16,1024]{3,2,1,0:T(8,128)(2,1)}, u32[]{:S(2)}, u32[]{:S(2)}) collective-permute-start(bf16[4,8,16,1024]{3,2,1,0:T(8,128)(2,1)S(1)} %all_to_all.25), channel_id=1, source_target_pairs={{0,1},{1,0},{2,3},{3,2},{4,5},{5,4},{6,7},{7,6},{8,9},{9,8},{10,11... | collective-permute-start | bytes 3145736 | tf_op jit(solution)/shard_map/ppermute | solution.py:51
  41.7 2.0 %collective-permute-done = bf16[4,8,16,1024]{3,2,1,0:T(8,128)(2,1)} collective-permute-done((bf16[4,8,16,1024]{3,2,1,0:T(8,128)(2,1)S(1)}, bf16[4,8,16,1024]{3,2,1,0:T(8,128)(2,1)}, u32[]{:S(2)}, u32[]{:S(2)}) %collective-permute-start) | collective-permute-done | bytes 1048608 | tf_op jit(solution)/shard_map/ppermute | solution.py:51
  43.7 2.2 %fusion.11 = (bf16[2,1,64,1024]{3,2,1,0:T(8,128)(2,1)}, bf16[2,1,64,1024]{3,2,1,0:T(8,128)(2,1)S(1)}, bf16[2,1,64,1024]{3,2,1,0:T(8,128)(2,1)}, bf16[2,1,64,1024...) fusion(s32[]{:T(128)S(6)} %select_n.108, ...), kind=kLoop, calls=%fused_computation.38 | loop fusion | flops 786432 | bytes 3670040 | tf_op jit(solution)/shard_map/stack | solution.py:52
  46.4 0.8 fusion.17
  47.2 4.0 %collective-permute-start.1 = (f16[128,512]{1,0:T(8,128)(2,1)}, f16[128,512]{1,0:T(8,128)(2,1)S(1)}, u32[]{:S(2)}, u32[]{:S(2)}) collective-permute-start(f16[128,512]{1,0:T(8,128)(2,1)} %get-tuple-element.18), channel_id=1, source_target_pairs={{0,64},{64,128},{128,192},{192,256},{256,320},{320,384},{384,448},... | collective-permute-start | bytes 393224 | tf_op jit(solution)/shard_map/ppermute | solution.py:62
  51.2 8.6 %collective-permute-start.5 = (f16[128,512]{1,0:T(8,128)(2,1)}, f16[128,512]{1,0:T(8,128)(2,1)}, u32[]{:S(2)}, u32[]{:S(2)}) collective-permute-start(f16[128,512]{1,0:T(8,128)(2,1)} %get-tuple-element.19), channel_id=1, source_target_pairs={{0,448},{64,0},{128,64},{192,128},{256,192},{320,256},{384,320},{4... | collective-permute-start | bytes 393224 | tf_op jit(solution)/shard_map/ppermute | solution.py:63
  59.8 1.5 %maximum_convert_fusion = f32[2,4,8,16,1024]{4,3,2,1,0:T(8,128)S(1)} fusion(bf16[1,4,8,16,1024]{4,3,2,1,0:T(8,128)(2,1)} %bitcast.12, bf16[1,4,8,16,1024]{4,3,2,1,0:T(8,128)(2,1)S(1)} %bitcast.70), kind=kLoop, calls=%fused_computation.20 | loop fusion | flops 2097152 | bytes 6291456 | tf_op jit(solution)/shard_map/convert_element_type | solution.py:78
  61.3 2.9 %copy.25 = f32[128,8,8,128]{3,2,1,0:T(8,128)} copy(f32[128,8,8,128]{3,1,2,0:T(8,128)S(1)} %bitcast.68) | data formatting | bytes 8388608
  64.2 5.4 %copy.18 = f32[1024,8,128]{0,2,1:T(8,128)} copy(f32[1024,8,128]{2,1,0:T(8,128)} %bitcast.67) | data formatting | bytes 8388608 | tf_op jit(solution)/shard_map/convert_element_type | solution.py:78
  69.6 5.4 %multiply_reduce_fusion = f32[1024,8]{0,1:T(8,128)} fusion(f32[1024,8,128]{0,2,1:T(8,128)} %copy.18, bf16[8,128,1024]{2,1,0:T(8,128)(2,1)S(1)} %copy-done, s32[1024]{0:T(1024)S(1)} %sub.50), kind=kOutput, calls=%fused_computation | convolution fusion | flops 2150621184 | bytes 6328320 | tf_op jit(solution)/shard_map/dot_general | solution.py:77
  75.0 1.7 %copy.19 = f32[1024,8]{1,0:T(8,128)} copy(f32[1024,8]{0,1:T(8,128)} %multiply_reduce_fusion) | data formatting | bytes 65536 | tf_op jit(solution)/shard_map/reduce_sum | solution.py:79
  76.7 1.9 %reshape.59 = f32[2,4,8,128]{3,2,1,0:T(8,128)} reshape(f32[1024,8]{1,0:T(8,128)} %copy.19) | data formatting | bytes 65536 | tf_op jit(solution)/shard_map/reshape | solution.py:79
  78.6 1.0 fusion.7
  79.6 1.0 convert_multiply_fusion
  81.1 3.4 %collective-permute-start.6 = (f16[128,1024]{1,0:T(8,128)(2,1)S(1)}, f16[128,1024]{1,0:T(8,128)(2,1)S(1)}, u32[]{:S(2)}, u32[]{:S(2)}) collective-permute-start(f16[128,1024]{1,0:T(8,128)(2,1)S(1)} %multiply_convert_fusion.2), channel_id=1, source_target_pairs={{0,448},{64,0},{128,64},{192,128},{256,192},{320,256},{384,320},{4... | collective-permute-start | bytes 786440 | tf_op jit(solution)/shard_map/ppermute | solution.py:69
  85.0 2.1 %collective-permute-start.2 = (f16[128,1024]{1,0:T(8,128)(2,1)S(1)}, f16[128,1024]{1,0:T(8,128)(2,1)S(1)}, u32[]{:S(2)}, u32[]{:S(2)}) collective-permute-start(f16[128,1024]{1,0:T(8,128)(2,1)S(1)} %multiply_convert_fusion.5), channel_id=1, source_target_pairs={{0,64},{64,128},{128,192},{192,256},{256,320},{320,384},{384,448},... | collective-permute-start | bytes 786440 | tf_op jit(solution)/shard_map/ppermute | solution.py:68
  87.0 3.1 %collective-permute-done.6 = f16[128,1024]{1,0:T(8,128)(2,1)S(1)} collective-permute-done((f16[128,1024]{1,0:T(8,128)(2,1)S(1)}, f16[128,1024]{1,0:T(8,128)(2,1)S(1)}, u32[]{:S(2)}, u32[]{:S(2)}) %collective-permute-start.6) | collective-permute-done | bytes 262176 | tf_op jit(solution)/shard_map/ppermute | solution.py:69
  90.6 4.4 %collective-permute-start.7 = (f16[128,1024]{1,0:T(8,128)(2,1)S(1)}, f16[128,1024]{1,0:T(8,128)(2,1)S(1)}, u32[]{:S(2)}, u32[]{:S(2)}) collective-permute-start(f16[128,1024]{1,0:T(8,128)(2,1)S(1)} %multiply_convert_fusion.1), channel_id=1, source_target_pairs={{0,448},{64,0},{128,64},{192,128},{256,192},{320,256},{384,320},{4... | collective-permute-start | bytes 786440 | tf_op jit(solution)/shard_map/ppermute | solution.py:69
  95.1 0.5 multiply_convert_fusion.4
  95.6 2.1 %collective-permute-start.3 = (f16[128,1024]{1,0:T(8,128)(2,1)S(1)}, f16[128,1024]{1,0:T(8,128)(2,1)S(1)}, u32[]{:S(2)}, u32[]{:S(2)}) collective-permute-start(f16[128,1024]{1,0:T(8,128)(2,1)S(1)} %multiply_convert_fusion.4), channel_id=1, source_target_pairs={{0,64},{64,128},{128,192},{192,256},{256,320},{320,384},{384,448},... | collective-permute-start | bytes 786440 | tf_op jit(solution)/shard_map/ppermute | solution.py:68
  97.6 1.3 collective-permute-done.7
  98.9 0.5 multiply_convert_fusion
  99.4 5.2 %collective-permute-start.8 = (f16[128,1024]{1,0:T(8,128)(2,1)S(1)}, f16[128,1024]{1,0:T(8,128)(2,1)S(1)}, u32[]{:S(2)}, u32[]{:S(2)}) collective-permute-start(f16[128,1024]{1,0:T(8,128)(2,1)S(1)} %multiply_convert_fusion), channel_id=1, source_target_pairs={{0,448},{64,0},{128,64},{192,128},{256,192},{320,256},{384,320},{4... | collective-permute-start | bytes 786440 | tf_op jit(solution)/shard_map/ppermute | solution.py:69
  105.1 1.9 %collective-permute-start.4 = (f16[128,1024]{1,0:T(8,128)(2,1)S(1)}, f16[128,1024]{1,0:T(8,128)(2,1)S(1)}, u32[]{:S(2)}, u32[]{:S(2)}) collective-permute-start(f16[128,1024]{1,0:T(8,128)(2,1)S(1)} %multiply_convert_fusion.3), channel_id=1, source_target_pairs={{0,64},{64,128},{128,192},{192,256},{256,320},{320,384},{384,448},... | collective-permute-start | bytes 786440 | tf_op jit(solution)/shard_map/ppermute | solution.py:68
  107.1 16.3 %all_to_all.26 = f32[64,1,128]{2,1,0:T(1,128)S(1)} all-to-all(f32[64,1,128]{2,1,0:T(1,128)S(1)} %bitcast.84), channel_id=1, replica_groups=mesh['head'=8,'vocab'=64] {'vocab'}, dimensions={0} | all-to-all | bytes 65536 | tf_op jit(solution)/shard_map/all_to_all | solution.py:82
  123.5 0.6 fusion.16
  124.6 13.8 %all_to_all.27 = f32[64,2,128]{2,1,0:T(2,128)S(1)} all-to-all(f32[64,2,128]{2,1,0:T(2,128)S(1)} %broadcast_in_dim.11), channel_id=1, replica_groups=mesh['head'=8,'vocab'=64] {'vocab'}, dimensions={0} | all-to-all | bytes 131072 | tf_op jit(solution)/shard_map/all_to_all | solution.py:23
  139.0 0.7 copy.22
  140.0 0.8 copy.23
  (54 shorter events, 4.3 us)
Async XLA Ops:
  0.6 45.3 %copy-start = (bf16[8,128,1024]{2,1,0:T(8,128)(2,1)S(1)}, bf16[8,128,1024]{2,1,0:T(8,128)(2,1)}, u32[]{:S(2)}) copy-start(bf16[8,128,1024]{2,1,0:T(8,128)(2,1)} %param.4) | copy-start | bytes 6291460
  1.6 39.8 %copy-start.6 = (s32[1024]{0:T(1024)S(1)}, s32[1024]{0:T(1024)}, u32[]{:S(2)}) copy-start(s32[1024]{0:T(1024)} %param.5) | copy-start | bytes 12292
  35.5 8.3 %collective-permute-start = (bf16[4,8,16,1024]{3,2,1,0:T(8,128)(2,1)S(1)}, bf16[4,8,16,1024]{3,2,1,0:T(8,128)(2,1)}, u32[]{:S(2)}, u32[]{:S(2)}) collective-permute-start(bf16[4,8,16,1024]{3,2,1,0:T(8,128)(2,1)S(1)} %all_to_all.25), channel_id=1, source_target_pairs={{0,1},{1,0},{2,3},{3,2},{4,5},{5,4},{6,7},{7,6},{8,9},{9,8},{10,11... | collective-permute-start | bytes 3145736 | tf_op jit(solution)/shard_map/ppermute | solution.py:51
  47.2 37.3 %collective-permute-start.1 = (f16[128,512]{1,0:T(8,128)(2,1)}, f16[128,512]{1,0:T(8,128)(2,1)S(1)}, u32[]{:S(2)}, u32[]{:S(2)}) collective-permute-start(f16[128,512]{1,0:T(8,128)(2,1)} %get-tuple-element.18), channel_id=1, source_target_pairs={{0,64},{64,128},{128,192},{192,256},{256,320},{320,384},{384,448},... | collective-permute-start | bytes 393224 | tf_op jit(solution)/shard_map/ppermute | solution.py:62
  51.2 28.5 %collective-permute-start.5 = (f16[128,512]{1,0:T(8,128)(2,1)}, f16[128,512]{1,0:T(8,128)(2,1)}, u32[]{:S(2)}, u32[]{:S(2)}) collective-permute-start(f16[128,512]{1,0:T(8,128)(2,1)} %get-tuple-element.19), channel_id=1, source_target_pairs={{0,448},{64,0},{128,64},{192,128},{256,192},{320,256},{384,320},{4... | collective-permute-start | bytes 393224 | tf_op jit(solution)/shard_map/ppermute | solution.py:63
  79.6 4.9 %copy-start.4 = (bf16[2,1,64,1024]{3,2,1,0:T(8,128)(2,1)S(1)}, bf16[2,1,64,1024]{3,2,1,0:T(8,128)(2,1)}, u32[]{:S(2)}) copy-start(bf16[2,1,64,1024]{3,2,1,0:T(8,128)(2,1)} %get-tuple-element.10) | copy-start | bytes 786436
  81.1 9.1 %collective-permute-start.6 = (f16[128,1024]{1,0:T(8,128)(2,1)S(1)}, f16[128,1024]{1,0:T(8,128)(2,1)S(1)}, u32[]{:S(2)}, u32[]{:S(2)}) collective-permute-start(f16[128,1024]{1,0:T(8,128)(2,1)S(1)} %multiply_convert_fusion.2), channel_id=1, source_target_pairs={{0,448},{64,0},{128,64},{192,128},{256,192},{320,256},{384,320},{4... | collective-permute-start | bytes 786440 | tf_op jit(solution)/shard_map/ppermute | solution.py:69
  84.9 10.1 %copy-start.3 = (bf16[2,1,64,1024]{3,2,1,0:T(8,128)(2,1)S(1)}, bf16[2,1,64,1024]{3,2,1,0:T(8,128)(2,1)}, u32[]{:S(2)}) copy-start(bf16[2,1,64,1024]{3,2,1,0:T(8,128)(2,1)} %get-tuple-element.13) | copy-start | bytes 786436
  85.0 10.1 %collective-permute-start.2 = (f16[128,1024]{1,0:T(8,128)(2,1)S(1)}, f16[128,1024]{1,0:T(8,128)(2,1)S(1)}, u32[]{:S(2)}, u32[]{:S(2)}) collective-permute-start(f16[128,1024]{1,0:T(8,128)(2,1)S(1)} %multiply_convert_fusion.5), channel_id=1, source_target_pairs={{0,64},{64,128},{128,192},{192,256},{256,320},{320,384},{384,448},... | collective-permute-start | bytes 786440 | tf_op jit(solution)/shard_map/ppermute | solution.py:68
  90.6 8.3 %copy-start.2 = (bf16[2,1,64,1024]{3,2,1,0:T(8,128)(2,1)S(1)}, bf16[2,1,64,1024]{3,2,1,0:T(8,128)(2,1)}, u32[]{:S(2)}) copy-start(bf16[2,1,64,1024]{3,2,1,0:T(8,128)(2,1)} %get-tuple-element.15) | copy-start | bytes 786436
  90.6 8.3 %collective-permute-start.7 = (f16[128,1024]{1,0:T(8,128)(2,1)S(1)}, f16[128,1024]{1,0:T(8,128)(2,1)S(1)}, u32[]{:S(2)}, u32[]{:S(2)}) collective-permute-start(f16[128,1024]{1,0:T(8,128)(2,1)S(1)} %multiply_convert_fusion.1), channel_id=1, source_target_pairs={{0,448},{64,0},{128,64},{192,128},{256,192},{320,256},{384,320},{4... | collective-permute-start | bytes 786440 | tf_op jit(solution)/shard_map/ppermute | solution.py:69
  95.6 9.1 %copy-start.1 = (bf16[2,1,64,1024]{3,2,1,0:T(8,128)(2,1)S(1)}, bf16[2,1,64,1024]{3,2,1,0:T(8,128)(2,1)}, u32[]{:S(2)}) copy-start(bf16[2,1,64,1024]{3,2,1,0:T(8,128)(2,1)} %get-tuple-element.12) | copy-start | bytes 786436
  95.6 9.0 %collective-permute-start.3 = (f16[128,1024]{1,0:T(8,128)(2,1)S(1)}, f16[128,1024]{1,0:T(8,128)(2,1)S(1)}, u32[]{:S(2)}, u32[]{:S(2)}) collective-permute-start(f16[128,1024]{1,0:T(8,128)(2,1)S(1)} %multiply_convert_fusion.4), channel_id=1, source_target_pairs={{0,64},{64,128},{128,192},{192,256},{256,320},{320,384},{384,448},... | collective-permute-start | bytes 786440 | tf_op jit(solution)/shard_map/ppermute | solution.py:68
  99.4 7.6 %copy-start.5 = (f32[2,4,8,128]{3,2,1,0:T(8,128)S(1)}, f32[2,4,8,128]{3,2,1,0:T(8,128)}, u32[]{:S(2)}) copy-start(f32[2,4,8,128]{3,2,1,0:T(8,128)} %reshape.59) | copy-start | bytes 98308
  99.4 24.1 %collective-permute-start.8 = (f16[128,1024]{1,0:T(8,128)(2,1)S(1)}, f16[128,1024]{1,0:T(8,128)(2,1)S(1)}, u32[]{:S(2)}, u32[]{:S(2)}) collective-permute-start(f16[128,1024]{1,0:T(8,128)(2,1)S(1)} %multiply_convert_fusion), channel_id=1, source_target_pairs={{0,448},{64,0},{128,64},{192,128},{256,192},{320,256},{384,320},{4... | collective-permute-start | bytes 786440 | tf_op jit(solution)/shard_map/ppermute | solution.py:69
  105.1 18.4 %collective-permute-start.4 = (f16[128,1024]{1,0:T(8,128)(2,1)S(1)}, f16[128,1024]{1,0:T(8,128)(2,1)S(1)}, u32[]{:S(2)}, u32[]{:S(2)}) collective-permute-start(f16[128,1024]{1,0:T(8,128)(2,1)S(1)} %multiply_convert_fusion.3), channel_id=1, source_target_pairs={{0,64},{64,128},{128,192},{192,256},{256,320},{320,384},{384,448},... | collective-permute-start | bytes 786440 | tf_op jit(solution)/shard_map/ppermute | solution.py:68

commit v2 on v0

v2 whole, which is shorter than its diff:
```python
import functools

import jax
import jax.numpy as jnp
from jax import lax
from jax.experimental import pallas as pl
from jax.experimental.pallas import tpu as pltpu
from jax.sharding import PartitionSpec as P

NX, NY, NC, NZ = 4, 8, 2, 8
NV = NX * NY * NC
SCALE = 0.125
MIB = 2**20
SLOT_OF = {5: 0, 4: 1, 2: 2, 3: 3, 7: 4, 6: 5, 1: 6, 0: 7}


def vocab_index(x, y, c):
    return (x * NY + y) * NC + c


Y_GROUPS = [[vocab_index(x, y, c) for y in range(NY)] for x in range(NX) for c in range(NC)]
X_GROUPS = [[vocab_index(x, y, c) for x in range(NX)] for y in range(NY) for c in range(NC)]
CORE_MAJOR = [[vocab_index(x, y, c) for c in range(NC) for x in range(NX) for y in range(NY)]]
CORE_SWAP = [(v, v ^ 1) for v in range(NV)]


def matching(sign):
    pairs = []
    for z in range(NZ):
        for v in range(NV):
            step = sign if (z + v) % 2 == 0 else -sign
            pairs.append((z * NV + v, (z + step) % NZ * NV + v))
    return pairs


FIRST, SECOND = matching(1), matching(-1)


def share(block, groups, count):
    copies = jnp.broadcast_to(block[None], (count,) + block.shape)
    return lax.all_to_all(copies, "vocab", 0, 0, axis_index_groups=groups, tiled=True)


def coded(values):
    return (values * SCALE).astype(jnp.float16)


def decoded(values):
    return values.astype(jnp.float32) * (1.0 / SCALE)


def ring(values, pairs):
    return lax.ppermute(values, ("head", "vocab"), pairs)


def tied(value, earlier):
    return lax.optimization_barrier((value, earlier))[0]


def cost(flops, mib):
    return pl.CostEstimate(flops=flops, bytes_accessed=mib * MIB, transcendentals=0)


def params():
    return pltpu.CompilerParams(vmem_limit_bytes=32 * MIB)


SMEM = pl.BlockSpec(memory_space=pltpu.SMEM)
VMEM = pl.BlockSpec(memory_space=pltpu.VMEM)


def pick_kernel(per_device, place_ref, ids_ref, weights_ref, own_ref, other_ref):
    tokens, slab = ids_ref.shape[0], weights_ref.shape[1]
    core = place_ref[1]
    lanes = lax.broadcasted_iota(jnp.int32, (tokens, slab), 1)
    chosen = (ids_ref[...] == lanes).astype(jnp.float32).astype(jnp.bfloat16)
    picked = lax.dot_general(
        chosen, weights_ref[...], (((1,), (1,)), ((), ())), preferred_element_type=jnp.float32
    ).astype(jnp.bfloat16)
    for place in range(tokens // per_device // NC):
        first = picked[2 * place * per_device : (2 * place + 1) * per_device]
        second = picked[(2 * place + 1) * per_device : (2 * place + 2) * per_device]
        rows = slice(place * per_device, (place + 1) * per_device)
        own_ref[rows] = jnp.where(core == 0, first, second)
        other_ref[rows] = jnp.where(core == 0, second, first)


def pick_columns(place, ids, weights, per_device):
    depth, slab = weights.shape
    tokens = ids.shape[0]
    block = 256
    half = jax.ShapeDtypeStruct((tokens // NC, depth), jnp.bfloat16)
    return pl.pallas_call(
        functools.partial(pick_kernel, per_device),
        grid=(tokens // block,),
        in_specs=[
            SMEM,
            pl.BlockSpec((block, 1), lambda i: (i, 0)),
            pl.BlockSpec((depth, slab), lambda i: (0, 0)),
        ],
        out_specs=[pl.BlockSpec((block // NC, depth), lambda i: (i, 0))] * 2,
        out_shape=[half, half],
        cost_estimate=cost(2 * tokens * depth * slab, 8),
        compiler_params=params(),
    )(place, ids, weights)


def products_kernel(heads, per_device, kind, place_ref, rows_ref, picked_ref, weights_ref, *rest):
    earlier_ref = rest[0] if kind else None
    sums_ref, terms_ref = rest[kind:]
    z, core, way = place_ref[0], place_ref[1], place_ref[2]
    depth = rows_ref.shape[1]
    lanes = heads * per_device
    head_of = lax.broadcasted_iota(jnp.int32, (depth, lanes), 0) // (depth // heads)
    lane_head = lax.broadcasted_iota(jnp.int32, (depth, lanes), 1) % heads
    spread = (head_of == lane_head).astype(jnp.float32).astype(jnp.bfloat16)
    block = rows_ref.shape[0] // NZ
    step = 2 * block
    places = step // per_device
    token = lax.broadcasted_iota(jnp.int32, (places, per_device, lanes), 1)
    lane_token = lax.broadcasted_iota(jnp.int32, (places, per_device, lanes), 2) // heads

    def slot(target):
        distance = jnp.bitwise_and((target - z) * way, NZ - 1)
        found = jnp.int32(0)
        for key, value in SLOT_OF.items():
            found = jnp.where(distance == key, value, found)
        return found

    def body(i, carry):
        rows = rows_ref[pl.ds(i * step, step)]
        sums = jnp.dot(rows, weights_ref[...], preferred_element_type=jnp.float32)
        for part in range(2):
            sums_ref[slot(2 * i + part)] = sums[part * block : (part + 1) * block]
        products = rows.astype(jnp.float32) * picked_ref[pl.ds(i * step, step)].astype(jnp.float32)
        high = products.astype(jnp.bfloat16)
        low = (products - high.astype(jnp.float32)).astype(jnp.bfloat16)
        terms = jnp.dot(high, spread, preferred_element_type=jnp.float32)
        terms += jnp.dot(low, spread, preferred_element_type=jnp.float32)
        terms = jnp.where(token == lane_token, terms.reshape(places, per_device, lanes), 0.0)
        terms = jnp.sum(terms, axis=1)
        if kind == 0:
            terms_ref[pl.ds(i * places, places)] = terms
        else:
            terms_ref[1 - core, pl.ds(i * places, places), 0] = terms
        return carry

    lax.fori_loop(0, rows_ref.shape[0] // step, body, 0)
    if kind == 1:
        terms_ref[core, :, 0] = earlier_ref[...]


def products(place, rows, picked, weights, heads, per_device, earlier=None):
    tokens, depth = rows.shape
    slab = weights.shape[1]
    lanes = heads * per_device
    places = tokens // per_device
    kind = 0 if earlier is None else 1
    shape = (places, lanes) if kind == 0 else (NC, places, 1, lanes)
    return pl.pallas_call(
        functools.partial(products_kernel, heads, per_device, kind),
        in_specs=[SMEM, VMEM, VMEM, VMEM] + [VMEM] * kind,
        out_specs=[VMEM, VMEM],
        out_shape=[
            jax.ShapeDtypeStruct((NZ, tokens // NZ, slab), jnp.float32),
            jax.ShapeDtypeStruct(shape, jnp.float32),
        ],
        cost_estimate=cost(2 * tokens * depth * (slab + 4 * lanes), 6),
        compiler_params=params(),
    )(place, rows, picked, weights, *([] if earlier is None else [earlier]))


def eye(size):
    rows = lax.broadcasted_iota(jnp.int32, (size, size), 0)
    return rows == lax.broadcasted_iota(jnp.int32, (size, size), 1)


def stats_kernel(place_ref, own_ref, other_ref, terms_ref, message_ref):
    core = place_ref[1]
    found = []
    for ref in (own_ref, other_ref):
        logits = ref[...]
        top = jnp.max(logits, axis=1, keepdims=True)
        found.append(top + jnp.log(jnp.sum(jnp.exp(logits - top), axis=1, keepdims=True)))
    own, other = found
    lse = jnp.concatenate([jnp.where(core == 0, own, other), jnp.where(core == 0, other, own)], axis=0)
    size = lse.shape[0]
    lse = jnp.sum(jnp.where(eye(size), lse, 0.0), axis=0, keepdims=True)
    terms = jnp.sum(terms_ref[...], axis=0)
    message = jnp.concatenate([lse, terms], axis=0)
    message_ref[...] = jnp.broadcast_to(message[None], message_ref.shape)


def stats(place, own, other, terms):
    size = own.shape[0] + other.shape[0]
    return pl.pallas_call(
        stats_kernel,
        in_specs=[SMEM, VMEM, VMEM, VMEM],
        out_specs=VMEM,
        out_shape=jax.ShapeDtypeStruct((NV, 2, size), jnp.float32),
        cost_estimate=cost(0, 1),
        compiler_params=params(),
    )(place, own, other, terms)


def finish_kernel(heads, per_device, place_ref, own_ref, other_ref, messages_ref, out_ref, attribution_ref):
    core = place_ref[1]
    every = messages_ref[:, 0, :]
    size = every.shape[1]
    top = jnp.max(every, axis=0, keepdims=True)
    lse = top + jnp.log(jnp.sum(jnp.exp(every - top), axis=0, keepdims=True))
    lse = jnp.sum(jnp.where(eye(size), lse, 0.0), axis=1, keepdims=True)
    half = size // NC
    for c in range(NC):
        logits = jnp.where(core == c, own_ref[...], other_ref[...])
        values = (logits - lse[c * half : (c + 1) * half]).astype(out_ref.dtype)
        for place in range(half // per_device):
            start = (place * NC + c) * per_device
            out_ref[start : start + per_device] = values[place * per_device : (place + 1) * per_device]
    terms = messages_ref[:, 1, :]
    shape = (NV, per_device, size)
    token = lax.broadcasted_iota(jnp.int32, shape, 1)
    lane_token = lax.broadcasted_iota(jnp.int32, shape, 2) // heads
    terms = jnp.where(token == lane_token, jnp.broadcast_to(terms[:, None, :], shape), 0.0)
    head = lax.broadcasted_iota(jnp.int32, (heads, size), 0)
    lane_head = lax.broadcasted_iota(jnp.int32, (heads, size), 1) % heads
    attribution_ref[...] = lax.dot_general(
        (head == lane_head).astype(jnp.float32),
        terms.reshape(NV * per_device, size),
        (((1,), (1,)), ((), ())),
        preferred_element_type=jnp.float32,
        precision=lax.Precision.HIGHEST,
    )


def finish(place, own, other, messages, heads, per_device):
    tokens, slab = own.shape[0] + other.shape[0], own.shape[1]
    return pl.pallas_call(
        functools.partial(finish_kernel, heads, per_device),
        in_specs=[SMEM, VMEM, VMEM, VMEM],
        out_specs=[VMEM, VMEM],
        out_shape=[
            jax.ShapeDtypeStruct((tokens, slab), jnp.bfloat16),
            jax.ShapeDtypeStruct((heads, NV * per_device), jnp.float32),
        ],
        cost_estimate=cost(0, 1),
        compiler_params=params(),
    )(place, own, other, messages)


def on_device(heads_out, unembed, targets):
    per_device, heads, hd = heads_out.shape
    depth = heads * hd
    slab = unembed.shape[2]
    weights = unembed.reshape(depth, slab)
    vocab_id = lax.axis_index("vocab")
    z = lax.axis_index("head")
    core = vocab_id & 1
    way = 1 - 2 * ((z + core) & 1)
    place = jnp.stack([z, core, way])
    ids = (targets - vocab_id * slab).reshape(-1, 1)
    picked_own, picked_other = pick_columns(place, ids, weights, per_device)

    column = share(heads_out.reshape(per_device, depth), Y_GROUPS, NY)
    own = share(column, X_GROUPS, NX)
    other = lax.ppermute(own, "vocab", CORE_SWAP).reshape(-1, depth)
    sums_a, terms = products(place, own.reshape(-1, depth), picked_own, weights, heads, per_device)
    a = coded(sums_a[0:2])
    got_a = ring(a, SECOND)
    sums_b, terms = products(place, tied(other, a), picked_other, weights, heads, per_device, terms)
    b = coded(sums_b[0:2])
    got_b = ring(b, SECOND)

    a = coded(sums_a[2:4] + decoded(tied(got_a, b)))
    got_a = ring(a, FIRST)
    b = coded(sums_b[2:4] + decoded(tied(got_b, a)))
    got_b = ring(b, FIRST)
    terms = tied(terms, b).reshape(NV, 1, per_device * heads)
    terms = lax.all_to_all(terms, "vocab", 0, 0, axis_index_groups=CORE_MAJOR, tiled=True)
    a = coded(sums_a[4:6] + decoded(tied(got_a, b)))
    got_a = ring(a, SECOND)
    b = coded(sums_b[4:6] + decoded(tied(got_b, a)))
    got_b = ring(b, SECOND)
    got_a = decoded(tied(got_a, b))
    a = coded(sums_a[6] + got_a[1])
    last_a = ring(a, FIRST)
    got_b = decoded(tied(got_b, a))
    b = coded(sums_b[6] + got_b[1])
    last_b = ring(b, FIRST)
    own_logits = sums_a[7] + got_a[0] + decoded(tied(last_a, b))
    other_logits = sums_b[7] + got_b[0] + decoded(last_b)

    message = stats(place, own_logits, other_logits, terms)
    messages = lax.all_to_all(message, "vocab", 0, 0, tiled=True)
    log_probs, attribution = finish(place, own_logits, other_logits, messages, heads, per_device)
    return (log_probs, attribution.T)


def solution(mesh):
    in_specs = (P("vocab", "head", None), P("head", None, "vocab"), P())
    out_specs = (P("head", "vocab"), P(None, "head"))
    return jax.shard_map(
        on_device, mesh=mesh, in_specs=in_specs, out_specs=out_specs, check_vma=False
    )
```

time: 542 us -> 130 us (0.24)
  blocking collectives: 370 us -> 56 us
  waiting for transfers between devices: 126 us -> 5.45 us
  starting transfers between devices: 0.08 us -> 46 us
  Pallas kernels: 0 us -> 14.2 us
  between operations: 14.1 us -> 0.91 us
  local copies, waits for them, and re-layouts: 12.4 us -> 2.72 us
  other arithmetic: 11.5 us -> 3.85 us
  matrix products: 6.48 us -> 0 us
    psum x1 -> x0, blocking collectives: 246 us -> none  [on_device(): lax.psum(jnp.sum(jnp.exp(logits - top), axis=1, keepdims=True), 'vocab')]
    pmax x1 -> x0, blocking collectives: 124 us -> none  [on_device(): top = lax.pmax(local_top, 'vocab')]
    all_gather x1 -> x0, waiting for transfers between devices: 86.6 us -> none  [on_device(): gathered = lax.all_gather(heads_out, 'vocab', axis=0, tiled=True)]
    all_to_all x0 -> x3, blocking collectives: none -> 56 us  [the longest x2 33.7 us: share(): lax.all_to_all(copies, 'vocab', 0, 0, axis_index_groups=groups, tiled=True)]
    reduce_scatter x1 -> x0, waiting for transfers between devices: 39.7 us -> none  [on_device(): lax.psum_scatter(partial_logits(gathered, unembed), 'head', scatter_dimen...]
    ppermute x0 -> x9, starting transfers between devices: none -> 39.2 us  [the longest x8 33.4 us: ring(): return lax.ppermute(values, ('head', 'vocab'), pairs)]
    pallas_call x0 -> x5, Pallas kernels: none -> 14.2 us  [the longest x2 7.65 us: products(): pl.pallas_call(functools.partial(products_kernel, heads, per_device, kind...]
    gather x1 -> x0, local copies, waits for them, and re-layouts: 7.58 us -> none  [on_device(): picked = jnp.take(unembed, safe_ids, axis=2)]
  transfers between devices with their start and end apart: 2 -> 10, of which waited for: 2 -> 3; matrix products, arithmetic and copies ran while one was open for 3% -> 3% of each run, Pallas kernels for 0% -> 9%
where the time goes in v2:
time: 130 us; the launch traced here: 129 us
  blocking collectives  56 us (43%)
  starting transfers between devices  46 us (35%)
  Pallas kernels  14.2 us (11%)
  waiting for transfers between devices  5.45 us (4%)
  other arithmetic  3.85 us (3%)
  local copies, waits for them, and re-layouts  2.72 us (2%)
    all_to_all x2, blocking collectives, share(): lax.all_to_all(copies, 'vocab', 0, 0, axis_index_groups=groups, tiled=True)  33.7 us
    ppermute x8, starting transfers between devices, ring(): return lax.ppermute(values, ('head', 'vocab'), pairs)  33.4 us
    all_to_all x1, blocking collectives, on_device(): messages = lax.all_to_all(message, 'vocab', 0, 0, tiled=True)  22.3 us
    pallas_call x2, Pallas kernels, products(): pl.pallas_call(functools.partial(products_kernel, heads, per_device, kind...  7.65 us
    all_to_all x1, starting transfers between devices, on_device(): lax.all_to_all(terms, 'vocab', 0, 0, axis_index_groups=CORE_MAJOR, tiled=...  6.76 us
    ppermute x1, starting transfers between devices, on_device(): other = lax.ppermute(own, 'vocab', CORE_SWAP).reshape(-1, depth)  5.85 us
    ppermute x8, waiting for transfers between devices, ring(): return lax.ppermute(values, ('head', 'vocab'), pairs)  5.44 us
    pallas_call x1, Pallas kernels, pick_columns(): pl.pallas_call(functools.partial(pick_kernel, per_device), grid=(tokens /...  3.83 us
  transfers between devices with their start and end apart: 10, of which 3 were waited for; matrix products, arithmetic and copies ran while one was open for 3% of the time, Pallas kernels for 9%

profile of v2, /device:TPU:1, one launch (start us, length us, event | category | flops | bytes accessed | tf_op | source)
XLA Modules:
  0.0 129.1 jit_solution(3970161366203938376)
XLA Ops:
  0.6 0.8 copy.8
  1.4 16.7 %all_to_all.20 = bf16[8,16,1024]{2,1,0:T(8,128)(2,1)S(1)} all-to-all(bf16[8,16,1024]{2,1,0:T(8,128)(2,1)S(1)} %broadcast_in_dim.14), channel_id=1, replica_groups={{0,2,4,6,8,10,12,14},{1,3,5,7,9,11,13,15},{16,18,20,22,24,26,28,30},{17..., dimensions={0} | all-to-all | bytes 524288 | tf_op jit(solution)/shard_map/all_to_all | solution.py:41
  18.2 0.1 broadcast_in_dim.15
  18.3 17.0 %all_to_all.21 = bf16[4,8,16,1024]{3,2,1,0:T(8,128)(2,1)S(1)} all-to-all(bf16[4,8,16,1024]{3,2,1,0:T(8,128)(2,1)S(1)} %broadcast_in_dim.15), channel_id=1, replica_groups={{0,16,32,48},{1,17,33,49},{2,18,34,50},{3,19,35,51},{4,20,36,52},{5,21,..., dimensions={0} | all-to-all | bytes 2097152 | tf_op jit(solution)/shard_map/all_to_all | solution.py:41
  35.3 5.9 %collective-permute-start.1 = (bf16[4,8,16,1024]{3,2,1,0:T(8,128)(2,1)S(1)}, bf16[4,8,16,1024]{3,2,1,0:T(8,128)(2,1)}, u32[]{:S(2)}, u32[]{:S(2)}) collective-permute-start(bf16[4,8,16,1024]{3,2,1,0:T(8,128)(2,1)S(1)} %all_to_all.21), channel_id=1, source_target_pairs={{0,1},{1,0},{2,3},{3,2},{4,5},{5,4},{6,7},{7,6},{8,9},{9,8},{10,11... | collective-permute-start | bytes 3145736 | tf_op jit(solution)/shard_map/ppermute | solution.py:266
  41.2 0.2 copy.5.ids_ref
  41.4 0.1 pad_add_fusion.place_ref
  41.5 1.6 %copy-done.1 = bf16[8,128,1024]{2,1,0:T(8,128)(2,1)S(1)} copy-done((bf16[8,128,1024]{2,1,0:T(8,128)(2,1)S(1)}, bf16[8,128,1024]{2,1,0:T(8,128)(2,1)}, u32[]{:S(2)}) %copy-start.1) | copy-done | bytes 2097176
  43.1 3.8 %shard_map.50 = (bf16[512,1024]{1,0:T(8,128)(2,1)S(1)}, bf16[512,1024]{1,0:T(8,128)(2,1)S(1)}) custom-call(s32[3]{0:T(128)S(1)} %pad_add_fusion.place_ref, s32[1024,1]{1,0:T(8,128)S(1)} %copy.5.ids_ref, bf16[1024,1024]{1,0:T(8,128)(2,1)S(1)} %bitcast.26), custom_call_target="tpu_custom_call" | custom-call | flops 2147483648 | bytes 8388608 | tf_op jit(solution)/shard_map/pallas_call | solution.py:93
  46.9 3.2 %shard_map.51 = (f32[8,64,1024]{2,1,0:T(8,128)S(1)}, f32[32,128]{1,0:T(8,128)S(1)}) custom-call(s32[3]{0:T(128)S(1)} %pad_add_fusion.place_ref, bf16[512,1024]{1,0:T(8,128)(2,1)S(1)} %bitcast.25, bf16[512,1024]{1,0:T(8,128)(2,1)S(1)} %get-tuple-element.19.picked_ref, bf16[1024,1024]{1,0:T(8,128)(2,1)S(1)} %bitcast.27), custom_call_target="tpu_custom_call" | custom-call | flops 1610612736 | bytes 6291456 | tf_op jit(solution)/shard_map/pallas_call | solution.py:160
  50.1 4.0 %collective-permute-start = (f16[2,64,1024]{2,1,0:T(8,128)(2,1)S(1)}, f16[2,64,1024]{2,1,0:T(8,128)(2,1)S(1)}, u32[]{:S(2)}, u32[]{:S(2)}) collective-permute-start(f16[2,64,1024]{2,1,0:T(8,128)(2,1)S(1)} %multiply_convert_fusion.5), channel_id=1, source_target_pairs={{0,448},{1,65},{2,450},{3,67},{4,452},{5,69},{6,454},{7,71},{8,456... | collective-permute-start | bytes 786440 | tf_op jit(solution)/shard_map/ppermute | solution.py:53
  54.2 4.5 %shard_map.52 = (f32[8,64,1024]{2,1,0:T(8,128)S(1)}, f32[2,32,1,128]{3,2,1,0:T(1,128)}) custom-call(s32[3]{0:T(128)S(1)} %pad_add_fusion.place_ref, bf16[512,1024]{1,0:T(8,128)(2,1)} %bitcast.6.rows_ref, bf16[512,1024]{1,0:T(8,128)(2,1)S(1)} %get-tuple-element.22.picked_ref, bf16[1024,1024]{1,0:T(8,128)(2,1)S(1)} %bitcast.28, ...), custom_call_target="tpu_custom_call" | custom-call | flops 1610612736 | bytes 6291456 | tf_op jit(solution)/shard_map/pallas_call | solution.py:160
  58.7 1.9 %collective-permute-start.3 = (f16[2,64,1024]{2,1,0:T(8,128)(2,1)S(1)}, f16[2,64,1024]{2,1,0:T(8,128)(2,1)S(1)}, u32[]{:S(2)}, u32[]{:S(2)}) collective-permute-start(f16[2,64,1024]{2,1,0:T(8,128)(2,1)S(1)} %multiply_convert_fusion.4), channel_id=1, source_target_pairs={{0,448},{1,65},{2,450},{3,67},{4,452},{5,69},{6,454},{7,71},{8,456... | collective-permute-start | bytes 786440 | tf_op jit(solution)/shard_map/ppermute | solution.py:53
  60.6 0.1 multiply_convert_fusion.3
  60.8 10.0 %collective-permute-start.2 = (f16[2,64,1024]{2,1,0:T(8,128)(2,1)S(1)}, f16[2,64,1024]{2,1,0:T(8,128)(2,1)S(1)}, u32[]{:S(2)}, u32[]{:S(2)}) collective-permute-start(f16[2,64,1024]{2,1,0:T(8,128)(2,1)S(1)} %multiply_convert_fusion.3), channel_id=1, source_target_pairs={{0,64},{1,449},{2,66},{3,451},{4,68},{5,453},{6,70},{7,455},{8,72}... | collective-permute-start | bytes 786440 | tf_op jit(solution)/shard_map/ppermute | solution.py:53
  70.8 0.1 multiply_convert_fusion.2
  70.9 4.1 %collective-permute-start.5 = (f16[2,64,1024]{2,1,0:T(8,128)(2,1)S(1)}, f16[2,64,1024]{2,1,0:T(8,128)(2,1)S(1)}, u32[]{:S(2)}, u32[]{:S(2)}) collective-permute-start(f16[2,64,1024]{2,1,0:T(8,128)(2,1)S(1)} %multiply_convert_fusion.2), channel_id=1, source_target_pairs={{0,64},{1,449},{2,66},{3,451},{4,68},{5,453},{6,70},{7,455},{8,72}... | collective-permute-start | bytes 786440 | tf_op jit(solution)/shard_map/ppermute | solution.py:53
  75.1 2.4 %collective-permute-done.2 = f16[2,64,1024]{2,1,0:T(8,128)(2,1)S(1)} collective-permute-done((f16[2,64,1024]{2,1,0:T(8,128)(2,1)S(1)}, f16[2,64,1024]{2,1,0:T(8,128)(2,1)S(1)}, u32[]{:S(2)}, u32[]{:S(2)}) %collective-permute-start.2) | collective-permute-done | bytes 262176 | tf_op jit(solution)/shard_map/ppermute | solution.py:53
  77.5 0.1 multiply_convert_fusion.1
  77.6 1.9 %collective-permute-start.4 = (f16[2,64,1024]{2,1,0:T(8,128)(2,1)S(1)}, f16[2,64,1024]{2,1,0:T(8,128)(2,1)S(1)}, u32[]{:S(2)}, u32[]{:S(2)}) collective-permute-start(f16[2,64,1024]{2,1,0:T(8,128)(2,1)S(1)} %multiply_convert_fusion.1), channel_id=1, source_target_pairs={{0,448},{1,65},{2,450},{3,67},{4,452},{5,69},{6,454},{7,71},{8,456... | collective-permute-start | bytes 786440 | tf_op jit(solution)/shard_map/ppermute | solution.py:53
  79.5 6.8 %all-to-all-start.2 = ((f32[64,1,128]{2,1,0:T(1,128)}), f32[64,1,128]{2,1,0:T(1,128)S(1)}, u32[]{:S(2)}, u32[]{:S(2)}) async-start(f32[64,1,128]{2,1,0:T(1,128)} %bitcast.11), calls=%async_computation.2 | async-start | bytes 65536 | tf_op jit(solution)/shard_map/all_to_all | solution.py:279
  86.3 1.1 multiply_convert_fusion
  87.4 3.6 %collective-permute-start.7 = (f16[2,64,1024]{2,1,0:T(8,128)(2,1)S(1)}, f16[2,64,1024]{2,1,0:T(8,128)(2,1)S(1)}, u32[]{:S(2)}, u32[]{:S(2)}) collective-permute-start(f16[2,64,1024]{2,1,0:T(8,128)(2,1)S(1)} %multiply_convert_fusion), channel_id=1, source_target_pairs={{0,448},{1,65},{2,450},{3,67},{4,452},{5,69},{6,454},{7,71},{8,456... | collective-permute-start | bytes 786440 | tf_op jit(solution)/shard_map/ppermute | solution.py:53
  91.2 3.1 %collective-permute-start.6 = (f16[64,1024]{1,0:T(8,128)(2,1)S(1)}, f16[64,1024]{1,0:T(8,128)(2,1)S(1)}, u32[]{:S(2)}, u32[]{:S(2)}) collective-permute-start(f16[64,1024]{1,0:T(8,128)(2,1)S(1)} %fusion.8), channel_id=1, source_target_pairs={{0,64},{1,449},{2,66},{3,451},{4,68},{5,453},{6,70},{7,455},{8,72}... | collective-permute-start | bytes 393224 | tf_op jit(solution)/shard_map/ppermute | solution.py:53
  94.3 0.8 collective-permute-done.7
  95.2 1.0 fusion.9
  96.2 4.6 %collective-permute-start.8 = (f16[64,1024]{1,0:T(8,128)(2,1)S(1)}, f16[64,1024]{1,0:T(8,128)(2,1)S(1)}, u32[]{:S(2)}, u32[]{:S(2)}) collective-permute-start(f16[64,1024]{1,0:T(8,128)(2,1)S(1)} %fusion.9), channel_id=1, source_target_pairs={{0,64},{1,449},{2,66},{3,451},{4,68},{5,453},{6,70},{7,455},{8,72}... | collective-permute-start | bytes 393224 | tf_op jit(solution)/shard_map/ppermute | solution.py:53
  100.8 2.3 %collective-permute-done.8 = f16[64,1024]{1,0:T(8,128)(2,1)S(1)} collective-permute-done((f16[64,1024]{1,0:T(8,128)(2,1)S(1)}, f16[64,1024]{1,0:T(8,128)(2,1)S(1)}, u32[]{:S(2)}, u32[]{:S(2)}) %collective-permute-start.8) | collective-permute-done | bytes 131104 | tf_op jit(solution)/shard_map/ppermute | solution.py:53
  103.1 1.0 fusion.1.other_ref
  104.1 0.9 shard_map.53
  105.0 22.3 %all_to_all.22.messages_ref = f32[64,2,128]{2,1,0:T(2,128)S(1)} all-to-all(f32[64,2,128]{2,1,0:T(2,128)S(1)} %shard_map.53), channel_id=1, replica_groups=mesh['head'=8,'vocab'=64] {'vocab'}, dimensions={0} | all-to-all | bytes 131072 | tf_op jit(solution)/shard_map/all_to_all | solution.py:294
  127.3 1.8 %shard_map.54 = (bf16[128,1024]{1,0:T(8,128)(2,1)}, f32[8,1024]{1,0:T(8,128)}) custom-call(s32[3]{0:T(128)S(1)} %pad_add_fusion.place_ref, f32[64,1024]{1,0:T(8,128)S(1)} %fusion.7.own_ref, f32[64,1024]{1,0:T(8,128)S(1)} %fusion.1.other_ref, f32[64,2,128]{2,1,0:T(2,128)S(1)} %all_to_all.22.messages_ref), custom_call_target="tpu_custom_call" | custom-call | bytes 1048576 | tf_op jit(solution)/shard_map/pallas_call | solution.py:238
  (20 shorter events, 0.4 us)
Async XLA Ops:
  1.4 39.8 %copy-start.2 = (s32[1024]{0:T(1024)S(1)}, s32[1024]{0:T(1024)}, u32[]{:S(2)}) copy-start(s32[1024]{0:T(1024)} %param.5) | copy-start | bytes 12292
  35.3 18.9 %collective-permute-start.1 = (bf16[4,8,16,1024]{3,2,1,0:T(8,128)(2,1)S(1)}, bf16[4,8,16,1024]{3,2,1,0:T(8,128)(2,1)}, u32[]{:S(2)}, u32[]{:S(2)}) collective-permute-start(bf16[4,8,16,1024]{3,2,1,0:T(8,128)(2,1)S(1)} %all_to_all.21), channel_id=1, source_target_pairs={{0,1},{1,0},{2,3},{3,2},{4,5},{5,4},{6,7},{7,6},{8,9},{9,8},{10,11... | collective-permute-start | bytes 3145736 | tf_op jit(solution)/shard_map/ppermute | solution.py:266
  41.5 1.6 %copy-start.1 = (bf16[8,128,1024]{2,1,0:T(8,128)(2,1)S(1)}, bf16[8,128,1024]{2,1,0:T(8,128)(2,1)}, u32[]{:S(2)}) copy-start(bf16[8,128,1024]{2,1,0:T(8,128)(2,1)} %param.4) | copy-start | bytes 6291460
  50.1 10.5 %collective-permute-start = (f16[2,64,1024]{2,1,0:T(8,128)(2,1)S(1)}, f16[2,64,1024]{2,1,0:T(8,128)(2,1)S(1)}, u32[]{:S(2)}, u32[]{:S(2)}) collective-permute-start(f16[2,64,1024]{2,1,0:T(8,128)(2,1)S(1)} %multiply_convert_fusion.5), channel_id=1, source_target_pairs={{0,448},{1,65},{2,450},{3,67},{4,452},{5,69},{6,454},{7,71},{8,456... | collective-permute-start | bytes 786440 | tf_op jit(solution)/shard_map/ppermute | solution.py:53
  58.6 12.2 %copy-start = (f32[8,64,1024]{2,1,0:T(8,128)}, f32[8,64,1024]{2,1,0:T(8,128)S(1)}, u32[]{:S(2)}) copy-start(f32[8,64,1024]{2,1,0:T(8,128)S(1)} %get-tuple-element.24) | copy-start | bytes 6291460
  58.7 12.1 %collective-permute-start.3 = (f16[2,64,1024]{2,1,0:T(8,128)(2,1)S(1)}, f16[2,64,1024]{2,1,0:T(8,128)(2,1)S(1)}, u32[]{:S(2)}, u32[]{:S(2)}) collective-permute-start(f16[2,64,1024]{2,1,0:T(8,128)(2,1)S(1)} %multiply_convert_fusion.4), channel_id=1, source_target_pairs={{0,448},{1,65},{2,450},{3,67},{4,452},{5,69},{6,454},{7,71},{8,456... | collective-permute-start | bytes 786440 | tf_op jit(solution)/shard_map/ppermute | solution.py:53
  60.8 16.7 %collective-permute-start.2 = (f16[2,64,1024]{2,1,0:T(8,128)(2,1)S(1)}, f16[2,64,1024]{2,1,0:T(8,128)(2,1)S(1)}, u32[]{:S(2)}, u32[]{:S(2)}) collective-permute-start(f16[2,64,1024]{2,1,0:T(8,128)(2,1)S(1)} %multiply_convert_fusion.3), channel_id=1, source_target_pairs={{0,64},{1,449},{2,66},{3,451},{4,68},{5,453},{6,70},{7,455},{8,72}... | collective-permute-start | bytes 786440 | tf_op jit(solution)/shard_map/ppermute | solution.py:53
  70.9 15.4 %collective-permute-start.5 = (f16[2,64,1024]{2,1,0:T(8,128)(2,1)S(1)}, f16[2,64,1024]{2,1,0:T(8,128)(2,1)S(1)}, u32[]{:S(2)}, u32[]{:S(2)}) collective-permute-start(f16[2,64,1024]{2,1,0:T(8,128)(2,1)S(1)} %multiply_convert_fusion.2), channel_id=1, source_target_pairs={{0,64},{1,449},{2,66},{3,451},{4,68},{5,453},{6,70},{7,455},{8,72}... | collective-permute-start | bytes 786440 | tf_op jit(solution)/shard_map/ppermute | solution.py:53
  77.6 13.5 %collective-permute-start.4 = (f16[2,64,1024]{2,1,0:T(8,128)(2,1)S(1)}, f16[2,64,1024]{2,1,0:T(8,128)(2,1)S(1)}, u32[]{:S(2)}, u32[]{:S(2)}) collective-permute-start(f16[2,64,1024]{2,1,0:T(8,128)(2,1)S(1)} %multiply_convert_fusion.1), channel_id=1, source_target_pairs={{0,448},{1,65},{2,450},{3,67},{4,452},{5,69},{6,454},{7,71},{8,456... | collective-permute-start | bytes 786440 | tf_op jit(solution)/shard_map/ppermute | solution.py:53
  79.5 24.6 %all-to-all-start.2 = ((f32[64,1,128]{2,1,0:T(1,128)}), f32[64,1,128]{2,1,0:T(1,128)S(1)}, u32[]{:S(2)}, u32[]{:S(2)}) async-start(f32[64,1,128]{2,1,0:T(1,128)} %bitcast.11), calls=%async_computation.2 | async-start | bytes 65536 | tf_op jit(solution)/shard_map/all_to_all | solution.py:279
  87.4 7.7 %collective-permute-start.7 = (f16[2,64,1024]{2,1,0:T(8,128)(2,1)S(1)}, f16[2,64,1024]{2,1,0:T(8,128)(2,1)S(1)}, u32[]{:S(2)}, u32[]{:S(2)}) collective-permute-start(f16[2,64,1024]{2,1,0:T(8,128)(2,1)S(1)} %multiply_convert_fusion), channel_id=1, source_target_pairs={{0,448},{1,65},{2,450},{3,67},{4,452},{5,69},{6,454},{7,71},{8,456... | collective-permute-start | bytes 786440 | tf_op jit(solution)/shard_map/ppermute | solution.py:53
  91.2 9.6 %collective-permute-start.6 = (f16[64,1024]{1,0:T(8,128)(2,1)S(1)}, f16[64,1024]{1,0:T(8,128)(2,1)S(1)}, u32[]{:S(2)}, u32[]{:S(2)}) collective-permute-start(f16[64,1024]{1,0:T(8,128)(2,1)S(1)} %fusion.8), channel_id=1, source_target_pairs={{0,64},{1,449},{2,66},{3,451},{4,68},{5,453},{6,70},{7,455},{8,72}... | collective-permute-start | bytes 393224 | tf_op jit(solution)/shard_map/ppermute | solution.py:53
  96.2 6.9 %collective-permute-start.8 = (f16[64,1024]{1,0:T(8,128)(2,1)S(1)}, f16[64,1024]{1,0:T(8,128)(2,1)S(1)}, u32[]{:S(2)}, u32[]{:S(2)}) collective-permute-start(f16[64,1024]{1,0:T(8,128)(2,1)S(1)} %fusion.9), channel_id=1, source_target_pairs={{0,64},{1,449},{2,66},{3,451},{4,68},{5,453},{6,70},{7,455},{8,72}... | collective-permute-start | bytes 393224 | tf_op jit(solution)/shard_map/ppermute | solution.py:53

commit v3 on v2

v3 whole, which is shorter than its diff:
```python
import functools

import jax
import jax.numpy as jnp
from jax import lax
from jax.experimental import pallas as pl
from jax.experimental.pallas import tpu as pltpu
from jax.sharding import PartitionSpec as P

NX, NY, NC, NZ = 4, 8, 2, 8
NV = NX * NY * NC
SCALE = 0.125
MIB = 2**20
SLOT_OF = {4: 0, 5: 1, 3: 2, 6: 3, 2: 4, 7: 5, 1: 6, 0: 7}


def vocab_index(x, y, c):
    return (x * NY + y) * NC + c


Y_GROUPS = [[vocab_index(x, y, c) for y in range(NY)] for x in range(NX) for c in range(NC)]
X_GROUPS = [[vocab_index(x, y, c) for x in range(NX)] for y in range(NY) for c in range(NC)]
CORE_MAJOR = [[vocab_index(x, y, c) for c in range(NC) for x in range(NX) for y in range(NY)]]
CORE_SWAP = [(v, v ^ 1) for v in range(NV)]


def hop(sign):
    pairs = []
    for z in range(NZ):
        for v in range(NV):
            step = sign if v % NC == 0 else -sign
            pairs.append((z * NV + v, (z + step) % NZ * NV + v))
    return pairs


AHEAD, BACK, AHEAD_TWO, BACK_TWO = hop(1), hop(-1), hop(2), hop(-2)


def share(block, groups, count):
    copies = jnp.broadcast_to(block[None], (count,) + block.shape)
    return lax.all_to_all(copies, "vocab", 0, 0, axis_index_groups=groups, tiled=True)


def coded(values):
    return (values * SCALE).astype(jnp.float16)


def decoded(values):
    return values.astype(jnp.float32) * (1.0 / SCALE)


def ring(values, pairs):
    return lax.ppermute(values, ("head", "vocab"), pairs)


def tied(value, earlier):
    return lax.optimization_barrier((value, earlier))[0]


def cost(flops, mib):
    return pl.CostEstimate(flops=flops, bytes_accessed=mib * MIB, transcendentals=0)


def params():
    return pltpu.CompilerParams(vmem_limit_bytes=20 * MIB)


SMEM = pl.BlockSpec(memory_space=pltpu.SMEM)
VMEM = pl.BlockSpec(memory_space=pltpu.VMEM)


def pick_kernel(per_device, place_ref, ids_ref, weights_ref, own_ref, other_ref):
    tokens, slab = ids_ref.shape[0], weights_ref.shape[1]
    core = place_ref[1]
    lanes = lax.broadcasted_iota(jnp.int32, (tokens, slab), 1)
    chosen = (ids_ref[...] == lanes).astype(jnp.float32).astype(jnp.bfloat16)
    picked = lax.dot_general(
        chosen, weights_ref[...], (((1,), (1,)), ((), ())), preferred_element_type=jnp.float32
    ).astype(jnp.bfloat16)
    for place in range(tokens // per_device // NC):
        first = picked[2 * place * per_device : (2 * place + 1) * per_device]
        second = picked[(2 * place + 1) * per_device : (2 * place + 2) * per_device]
        rows = slice(place * per_device, (place + 1) * per_device)
        own_ref[rows] = jnp.where(core == 0, first, second)
        other_ref[rows] = jnp.where(core == 0, second, first)


def pick_columns(place, ids, weights, per_device):
    depth, slab = weights.shape
    tokens = ids.shape[0]
    block = 256
    half = jax.ShapeDtypeStruct((tokens // NC, depth), jnp.bfloat16)
    return pl.pallas_call(
        functools.partial(pick_kernel, per_device),
        grid=(tokens // block,),
        in_specs=[
            SMEM,
            pl.BlockSpec((block, 1), lambda i: (i, 0)),
            pl.BlockSpec((depth, slab), lambda i: (0, 0)),
        ],
        out_specs=[pl.BlockSpec((block // NC, depth), lambda i: (i, 0))] * 2,
        out_shape=[half, half],
        cost_estimate=cost(2 * tokens * depth * slab, 8),
        compiler_params=params(),
    )(place, ids, weights)


def sums_kernel(kind, place_ref, rows_ref, weights_ref, *rest):
    sums_ref = rest[-1]
    z, way = place_ref[0], place_ref[2]
    block = sums_ref.shape[2]
    parts = rows_ref.shape[0] // block
    sums = jnp.dot(rows_ref[...], weights_ref[...], preferred_element_type=jnp.float32)
    for part in range(parts):
        target = pl.program_id(0) * parts + part
        distance = jnp.bitwise_and((target - z) * way, NZ - 1)
        slot = jnp.int32(0)
        for key, value in SLOT_OF.items():
            slot = jnp.where(distance == key, value, slot)
        sums_ref[slot, kind] = sums[part * block : (part + 1) * block]


def partial_sums(place, rows, weights, earlier=None):
    tokens, depth = rows.shape
    slab = weights.shape[1]
    steps = 2
    kind = 0 if earlier is None else 1
    return pl.pallas_call(
        functools.partial(sums_kernel, kind),
        grid=(steps,),
        in_specs=[SMEM, pl.BlockSpec((tokens // steps, depth), lambda i: (i, 0)), VMEM] + [VMEM] * kind,
        out_specs=VMEM,
        out_shape=jax.ShapeDtypeStruct((NZ, NC, tokens // NZ, slab), jnp.float32),
        input_output_aliases={3: 0} if kind else {},
        cost_estimate=cost(2 * tokens * depth * slab, 6),
        compiler_params=params(),
    )(place, rows, weights, *([earlier] if kind else []))


def terms_kernel(heads, per_device, place_ref, own_ref, other_ref, picked_own_ref, picked_other_ref, terms_ref):
    core = place_ref[1]
    tokens, depth = own_ref.shape
    lanes = heads * per_device
    places = tokens // per_device
    head_of = lax.broadcasted_iota(jnp.int32, (depth, lanes), 0) // (depth // heads)
    lane_head = lax.broadcasted_iota(jnp.int32, (depth, lanes), 1) % heads
    spread = (head_of == lane_head).astype(jnp.float32).astype(jnp.bfloat16)
    token = lax.broadcasted_iota(jnp.int32, (places, per_device, lanes), 1)
    lane_token = lax.broadcasted_iota(jnp.int32, (places, per_device, lanes), 2) // heads
    parts = []
    for rows_ref, picked_ref in ((own_ref, picked_own_ref), (other_ref, picked_other_ref)):
        products = rows_ref[...].astype(jnp.float32) * picked_ref[...].astype(jnp.float32)
        high = products.astype(jnp.bfloat16)
        parts += [high, (products - high.astype(jnp.float32)).astype(jnp.bfloat16)]
    sums = jnp.dot(jnp.concatenate(parts, axis=0), spread, preferred_element_type=jnp.float32)
    for kind in range(NC):
        start = 2 * kind * tokens
        terms = sums[start : start + tokens] + sums[start + tokens : start + 2 * tokens]
        terms = jnp.where(token == lane_token, terms.reshape(places, per_device, lanes), 0.0)
        terms_ref[jnp.bitwise_xor(core, kind), :, 0] = jnp.sum(terms, axis=1)


def head_terms(place, own, other, picked_own, picked_other, heads, per_device):
    tokens, depth = own.shape
    lanes = heads * per_device
    steps = 2
    rows = pl.BlockSpec((tokens // steps, depth), lambda i: (i, 0))
    places = tokens // per_device
    return pl.pallas_call(
        functools.partial(terms_kernel, heads, per_device),
        grid=(steps,),
        in_specs=[SMEM, rows, rows, rows, rows],
        out_specs=pl.BlockSpec((NC, places // steps, 1, lanes), lambda i: (0, i, 0, 0)),
        out_shape=jax.ShapeDtypeStruct((NC, places, 1, lanes), jnp.float32),
        cost_estimate=cost(16 * tokens * depth * lanes, 4),
        compiler_params=params(),
    )(place, own, other, picked_own, picked_other)


def eye(size):
    rows = lax.broadcasted_iota(jnp.int32, (size, size), 0)
    return rows == lax.broadcasted_iota(jnp.int32, (size, size), 1)


def stats_kernel(place_ref, logits_ref, terms_ref, message_ref):
    core = place_ref[1]
    found = []
    for kind in range(NC):
        logits = logits_ref[kind]
        top = jnp.max(logits, axis=1, keepdims=True)
        found.append(top + jnp.log(jnp.sum(jnp.exp(logits - top), axis=1, keepdims=True)))
    own, other = found
    lse = jnp.concatenate([jnp.where(core == 0, own, other), jnp.where(core == 0, other, own)], axis=0)
    size = lse.shape[0]
    lse = jnp.sum(jnp.where(eye(size), lse, 0.0), axis=0, keepdims=True)
    terms = jnp.sum(terms_ref[...], axis=0)
    message = jnp.concatenate([lse, terms], axis=0)
    message_ref[...] = jnp.broadcast_to(message[None], message_ref.shape)


def stats(place, logits, terms):
    size = NC * logits.shape[1]
    return pl.pallas_call(
        stats_kernel,
        in_specs=[SMEM, VMEM, VMEM],
        out_specs=VMEM,
        out_shape=jax.ShapeDtypeStruct((NV, 2, size), jnp.float32),
        cost_estimate=cost(0, 1),
        compiler_params=params(),
    )(place, logits, terms)


def finish_kernel(heads, per_device, place_ref, logits_ref, messages_ref, out_ref, attribution_ref):
    core = place_ref[1]
    every = messages_ref[:, 0, :]
    size = every.shape[1]
    top = jnp.max(every, axis=0, keepdims=True)
    lse = top + jnp.log(jnp.sum(jnp.exp(every - top), axis=0, keepdims=True))
    lse = jnp.sum(jnp.where(eye(size), lse, 0.0), axis=1, keepdims=True)
    half = size // NC
    for c in range(NC):
        logits = logits_ref[jnp.bitwise_xor(core, c)]
        values = (logits - lse[c * half : (c + 1) * half]).astype(out_ref.dtype)
        for place in range(half // per_device):
            start = (place * NC + c) * per_device
            out_ref[start : start + per_device] = values[place * per_device : (place + 1) * per_device]
    terms = messages_ref[:, 1, :]
    shape = (NV, per_device, size)
    token = lax.broadcasted_iota(jnp.int32, shape, 1)
    lane_token = lax.broadcasted_iota(jnp.int32, shape, 2) // heads
    terms = jnp.where(token == lane_token, jnp.broadcast_to(terms[:, None, :], shape), 0.0)
    head = lax.broadcasted_iota(jnp.int32, (heads, size), 0)
    lane_head = lax.broadcasted_iota(jnp.int32, (heads, size), 1) % heads
    attribution_ref[...] = lax.dot_general(
        (head == lane_head).astype(jnp.float32),
        terms.reshape(NV * per_device, size),
        (((1,), (1,)), ((), ())),
        preferred_element_type=jnp.float32,
        precision=lax.Precision.HIGHEST,
    )


def finish(place, logits, messages, heads, per_device):
    tokens, slab = NC * logits.shape[1], logits.shape[2]
    return pl.pallas_call(
        functools.partial(finish_kernel, heads, per_device),
        in_specs=[SMEM, VMEM, VMEM],
        out_specs=[VMEM, VMEM],
        out_shape=[
            jax.ShapeDtypeStruct((tokens, slab), jnp.bfloat16),
            jax.ShapeDtypeStruct((heads, NV * per_device), jnp.float32),
        ],
        cost_estimate=cost(0, 1),
        compiler_params=params(),
    )(place, logits, messages)


def on_device(heads_out, unembed, targets):
    per_device, heads, hd = heads_out.shape
    depth = heads * hd
    slab = unembed.shape[2]
    weights = unembed.reshape(depth, slab)
    vocab_id = lax.axis_index("vocab")
    z = lax.axis_index("head")
    core = vocab_id & 1
    way = 1 - 2 * core
    place = jnp.stack([z, core, way])
    ids = (targets - vocab_id * slab).reshape(-1, 1)
    picked_own, picked_other = pick_columns(place, ids, weights, per_device)
    column = share(heads_out.reshape(per_device, depth), Y_GROUPS, NY)
    own = share(column, X_GROUPS, NX).reshape(-1, depth)
    own = tied(own, picked_own)
    other = lax.ppermute(own, "vocab", CORE_SWAP)
    sums = partial_sums(place, own, weights)
    sums = partial_sums(place, tied(other, sums), weights, sums)

    sent = coded(sums[0])
    four = ring(sent, AHEAD_TWO)
    sent = coded(tied(sums, sent)[1])
    five = ring(sent, BACK)
    sent = coded(tied(sums, sent)[2])
    three = ring(sent, AHEAD)
    terms = head_terms(place, own, tied(other, sent), picked_own, picked_other, heads, per_device)
    sent = coded(tied(sums, terms)[6])
    one = ring(sent, AHEAD)
    sent = coded(sums[4] + decoded(tied(four, sent)) + decoded(three))
    two = ring(sent, AHEAD_TWO)
    sent = coded(sums[3] + decoded(tied(five, sent)))
    six = ring(sent, BACK_TWO)
    sent = coded(tied(sums, sent)[5])
    seven = ring(sent, BACK)
    terms = tied(terms, sent).reshape(NV, 1, per_device * heads)
    terms = lax.all_to_all(terms, "vocab", 0, 0, axis_index_groups=CORE_MAJOR, tiled=True)
    logits = sums[7] + decoded(one) + decoded(two) + decoded(six) + decoded(seven)

    message = stats(place, logits, terms)
    messages = lax.all_to_all(message, "vocab", 0, 0, tiled=True)
    log_probs, attribution = finish(place, logits, messages, heads, per_device)
    return (log_probs, attribution.T)


def solution(mesh):
    in_specs = (P("vocab", "head", None), P("head", None, "vocab"), P())
    out_specs = (P("head", "vocab"), P(None, "head"))
    return jax.shard_map(
        on_device, mesh=mesh, in_specs=in_specs, out_specs=out_specs, check_vma=False
    )
```

time: 130 us -> 114 us (0.88)
  blocking collectives: 56 us -> 30.8 us
  waiting for transfers between devices: 5.45 us -> 14.3 us
  local copies, waits for them, and re-layouts: 2.72 us -> 6.11 us
  other arithmetic: 3.85 us -> 1.87 us
    all_to_all x2 -> x1, blocking collectives: 33.7 us -> 16.7 us  [share(): lax.all_to_all(copies, 'vocab', 0, 0, axis_index_groups=groups, tiled=True)]
    all_to_all x1, blocking collectives: 22.3 us -> 14 us  [on_device(): messages = lax.all_to_all(message, 'vocab', 0, 0, tiled=True)]
    ppermute x8 -> x7, starting transfers between devices: 33.4 us -> 28.2 us  [ring(): return lax.ppermute(values, ('head', 'vocab'), pairs)]
    all_to_all x0 -> x1, starting transfers between devices: none -> 5.09 us  [share(): lax.all_to_all(copies, 'vocab', 0, 0, axis_index_groups=groups, tiled=True)]
    all_to_all x0 -> x1, waiting for transfers between devices: none -> 4.09 us  [share(): lax.all_to_all(copies, 'vocab', 0, 0, axis_index_groups=groups, tiled=True)]
    all_to_all x1, waiting for transfers between devices: 0.01 us -> 3.76 us  [on_device(): lax.all_to_all(terms, 'vocab', 0, 0, axis_index_groups=CORE_MAJOR, tiled=...]
    convert_element_type x8 -> x7, other arithmetic: 2.59 us -> 0.49 us  [coded(): return (values * SCALE).astype(jnp.float16)]
    unnamed x7 -> x17, local copies, waits for them, and re-layouts: 2.37 us -> 3.93 us
  transfers between devices with their start and end apart: 10 -> 10, of which waited for: 3 -> 6; matrix products, arithmetic and copies ran while one was open for 3% -> 2% of each run, Pallas kernels for 9% -> 7%
where the time goes in v3:
time: 114 us
  starting transfers between devices  46.6 us (41%)
  blocking collectives  30.8 us (27%)
  waiting for transfers between devices  14.3 us (13%)
  Pallas kernels  13.1 us (11%)
  local copies, waits for them, and re-layouts  6.11 us (5%)
  other arithmetic  1.87 us (2%)
    ppermute x7, starting transfers between devices, ring(): return lax.ppermute(values, ('head', 'vocab'), pairs)  28.2 us
    all_to_all x1, blocking collectives, share(): lax.all_to_all(copies, 'vocab', 0, 0, axis_index_groups=groups, tiled=True)  16.7 us
    all_to_all x1, blocking collectives, on_device(): messages = lax.all_to_all(message, 'vocab', 0, 0, tiled=True)  14 us
    all_to_all x1, starting transfers between devices, on_device(): lax.all_to_all(terms, 'vocab', 0, 0, axis_index_groups=CORE_MAJOR, tiled=...  7.53 us
    ppermute x7, waiting for transfers between devices, ring(): return lax.ppermute(values, ('head', 'vocab'), pairs)  6.2 us
    ppermute x1, starting transfers between devices, on_device(): other = lax.ppermute(own, 'vocab', CORE_SWAP)  5.86 us
    all_to_all x1, starting transfers between devices, share(): lax.all_to_all(copies, 'vocab', 0, 0, axis_index_groups=groups, tiled=True)  5.09 us
    all_to_all x1, waiting for transfers between devices, share(): lax.all_to_all(copies, 'vocab', 0, 0, axis_index_groups=groups, tiled=True)  4.09 us
  transfers between devices with their start and end apart: 10, of which 6 were waited for; matrix products, arithmetic and copies ran while one was open for 2% of the time, Pallas kernels for 7%

profile of v3, /device:TPU:1, one launch (start us, length us, event | category | flops | bytes accessed | tf_op | source)
XLA Modules:
  0.0 113.7 jit_solution(10709175861831279104)
XLA Ops:
  0.6 0.9 copy.9
  1.6 16.7 %all_to_all.20 = bf16[8,16,1024]{2,1,0:T(8,128)(2,1)S(1)} all-to-all(bf16[8,16,1024]{2,1,0:T(8,128)(2,1)S(1)} %broadcast_in_dim.14), channel_id=1, replica_groups={{0,2,4,6,8,10,12,14},{1,3,5,7,9,11,13,15},{16,18,20,22,24,26,28,30},{17..., dimensions={0} | all-to-all | bytes 524288 | tf_op jit(solution)/shard_map/all_to_all | solution.py:41
  18.3 1.1 broadcast_in_dim.15
  19.4 5.1 %all-to-all-start.1 = ((bf16[4,8,16,1024]{3,2,1,0:T(8,128)(2,1)}), bf16[4,8,16,1024]{3,2,1,0:T(8,128)(2,1)S(1)}, u32[]{:S(2)}, u32[]{:S(2)}) async-start(bf16[4,8,16,1024]{3,2,1,0:T(8,128)(2,1)} %broadcast_in_dim.15), calls=%async_computation.1 | async-start | bytes 2097152 | tf_op jit(solution)/shard_map/all_to_all | solution.py:41
  24.5 1.0 copy.6.ids_ref
  25.7 1.0 copy-done.6
  26.7 3.9 %shard_map.50 = (bf16[512,1024]{1,0:T(8,128)(2,1)S(1)}, bf16[512,1024]{1,0:T(8,128)(2,1)S(1)}) custom-call(s32[3]{0:T(128)S(1)} %pad_add_fusion.place_ref, s32[1024,1]{1,0:T(8,128)S(1)} %copy-done.6, bf16[1024,1024]{1,0:T(8,128)(2,1)S(1)} %bitcast.53), custom_call_target="tpu_custom_call" | custom-call | flops 2147483648 | bytes 8388608 | tf_op jit(solution)/shard_map/pallas_call | solution.py:93
  30.6 1.0 copy-done.2
  31.6 1.0 copy-done.4
  32.5 4.1 %all-to-all-done.1 = bf16[4,8,16,1024]{3,2,1,0:T(8,128)(2,1)S(1)} async-done(((bf16[4,8,16,1024]{3,2,1,0:T(8,128)(2,1)}), bf16[4,8,16,1024]{3,2,1,0:T(8,128)(2,1)S(1)}, u32[]{:S(2)}, u32[]{:S(2)}) %all-to-all-start.1) | async-done | bytes 1048608 | tf_op jit(solution)/shard_map/all_to_all | solution.py:41
  36.6 5.9 %collective-permute-start = (bf16[512,1024]{1,0:T(8,128)(2,1)S(1)}, bf16[512,1024]{1,0:T(8,128)(2,1)S(1)}, u32[]{:S(2)}, u32[]{:S(2)}) collective-permute-start(bf16[512,1024]{1,0:T(8,128)(2,1)S(1)} %bitcast.50), channel_id=1, source_target_pairs={{0,1},{1,0},{2,3},{3,2},{4,5},{5,4},{6,7},{7,6},{8,9},{9,8},{10,11... | collective-permute-start | bytes 3145736 | tf_op jit(solution)/shard_map/ppermute | solution.py:273
  42.5 2.0 %shard_map.51.rest_0_ = f32[8,2,64,1024]{3,2,1,0:T(8,128)S(1)} custom-call(s32[3]{0:T(128)S(1)} %pad_add_fusion.place_ref, bf16[512,1024]{1,0:T(8,128)(2,1)S(1)} %bitcast.51, bf16[1024,1024]{1,0:T(8,128)(2,1)S(1)} %bitcast.54), custom_call_target="tpu_custom_call" | custom-call | flops 1073741824 | bytes 6291456 | tf_op jit(solution)/shard_map/pallas_call | solution.py:128
  44.5 0.2 collective-permute-done.rows_ref.other_ref
  44.8 2.0 %shard_map.52 = f32[8,2,64,1024]{3,2,1,0:T(8,128)S(1)} custom-call(s32[3]{0:T(128)S(1)} %pad_add_fusion.place_ref, bf16[512,1024]{1,0:T(8,128)(2,1)S(1)} %collective-permute-done.rows_ref.other_ref, bf16[1024,1024]{1,0:T(8,128)(2,1)S(1)} %bitcast.55, f32[8,2,64,1024]{3,2,1,0:T(8,128)S(1)} %shard_map.51.rest_0_), custom_call_target="tpu_custom_call", output_to_operand_aliasing={{}: (3, {})} | custom-call | flops 1073741824 | bytes 6291456 | tf_op jit(solution)/shard_map/pallas_call | solution.py:128
  46.9 4.0 %collective-permute-start.5 = (f16[2,64,1024]{2,1,0:T(8,128)(2,1)S(1)}, f16[2,64,1024]{2,1,0:T(8,128)(2,1)S(1)}, u32[]{:S(2)}, u32[]{:S(2)}) collective-permute-start(f16[2,64,1024]{2,1,0:T(8,128)(2,1)S(1)} %fusion.12), channel_id=1, source_target_pairs={{0,448},{1,65},{2,450},{3,67},{4,452},{5,69},{6,454},{7,71},{8,456... | collective-permute-start | bytes 786440 | tf_op jit(solution)/shard_map/ppermute | solution.py:53
  50.9 9.8 %collective-permute-start.2 = (f16[2,64,1024]{2,1,0:T(8,128)(2,1)S(1)}, f16[2,64,1024]{2,1,0:T(8,128)(2,1)S(1)}, u32[]{:S(2)}, u32[]{:S(2)}) collective-permute-start(f16[2,64,1024]{2,1,0:T(8,128)(2,1)S(1)} %fusion.16), channel_id=1, source_target_pairs={{0,128},{1,385},{2,130},{3,387},{4,132},{5,389},{6,134},{7,391},{8... | collective-permute-start | bytes 786440 | tf_op jit(solution)/shard_map/ppermute | solution.py:53
  60.7 2.2 %collective-permute-start.3 = (f16[2,64,1024]{2,1,0:T(8,128)(2,1)S(1)}, f16[2,64,1024]{2,1,0:T(8,128)(2,1)S(1)}, u32[]{:S(2)}, u32[]{:S(2)}) collective-permute-start(f16[2,64,1024]{2,1,0:T(8,128)(2,1)S(1)} %fusion.13), channel_id=1, source_target_pairs={{0,64},{1,449},{2,66},{3,451},{4,68},{5,453},{6,70},{7,455},{8,72}... | collective-permute-start | bytes 786440 | tf_op jit(solution)/shard_map/ppermute | solution.py:53
  62.9 2.6 %shard_map.53 = f32[2,32,1,128]{3,2,1,0:T(1,128)} custom-call(s32[3]{0:T(128)S(1)} %pad_add_fusion.place_ref, bf16[512,1024]{1,0:T(8,128)(2,1)S(1)} %bitcast.52, bf16[512,1024]{1,0:T(8,128)(2,1)S(1)} %collective-permute-done.rows_ref.other_ref, bf16[512,1024]{1,0:T(8,128)(2,1)S(1)} %copy-done.3, bf16[512,1024]{1,0:T(8,128)(2,1)S(1)} %copy-done.5), custom_call_target="tpu_custom_call" | custom-call | flops 1073741824 | bytes 4194304 | tf_op jit(solution)/shard_map/pallas_call | solution.py:169
  65.6 2.2 %collective-permute-start.1 = (f16[2,64,1024]{2,1,0:T(8,128)(2,1)S(1)}, f16[2,64,1024]{2,1,0:T(8,128)(2,1)S(1)}, u32[]{:S(2)}, u32[]{:S(2)}) collective-permute-start(f16[2,64,1024]{2,1,0:T(8,128)(2,1)S(1)} %fusion.14), channel_id=1, source_target_pairs={{0,64},{1,449},{2,66},{3,451},{4,68},{5,453},{6,70},{7,455},{8,72}... | collective-permute-start | bytes 786440 | tf_op jit(solution)/shard_map/ppermute | solution.py:53
  67.8 2.3 %collective-permute-done.3 = f16[2,64,1024]{2,1,0:T(8,128)(2,1)S(1)} collective-permute-done((f16[2,64,1024]{2,1,0:T(8,128)(2,1)S(1)}, f16[2,64,1024]{2,1,0:T(8,128)(2,1)S(1)}, u32[]{:S(2)}, u32[]{:S(2)}) %collective-permute-start.3) | collective-permute-done | bytes 262176 | tf_op jit(solution)/shard_map/ppermute | solution.py:53
  70.1 0.2 fusion.6
  70.4 1.9 %collective-permute-start.7 = (f16[2,64,1024]{2,1,0:T(8,128)(2,1)S(1)}, f16[2,64,1024]{2,1,0:T(8,128)(2,1)S(1)}, u32[]{:S(2)}, u32[]{:S(2)}) collective-permute-start(f16[2,64,1024]{2,1,0:T(8,128)(2,1)S(1)} %fusion.15), channel_id=1, source_target_pairs={{0,448},{1,65},{2,450},{3,67},{4,452},{5,69},{6,454},{7,71},{8,456... | collective-permute-start | bytes 786440 | tf_op jit(solution)/shard_map/ppermute | solution.py:53
  72.4 2.6 %collective-permute-start.6 = (f16[2,64,1024]{2,1,0:T(8,128)(2,1)S(1)}, f16[2,64,1024]{2,1,0:T(8,128)(2,1)S(1)}, u32[]{:S(2)}, u32[]{:S(2)}) collective-permute-start(f16[2,64,1024]{2,1,0:T(8,128)(2,1)S(1)} %fusion.2), channel_id=1, source_target_pairs={{0,384},{1,129},{2,386},{3,131},{4,388},{5,133},{6,390},{7,135},{8... | collective-permute-start | bytes 786440 | tf_op jit(solution)/shard_map/ppermute | solution.py:53
  75.0 5.5 %collective-permute-start.4 = (f16[2,64,1024]{2,1,0:T(8,128)(2,1)S(1)}, f16[2,64,1024]{2,1,0:T(8,128)(2,1)S(1)}, u32[]{:S(2)}, u32[]{:S(2)}) collective-permute-start(f16[2,64,1024]{2,1,0:T(8,128)(2,1)S(1)} %fusion.6), channel_id=1, source_target_pairs={{0,128},{1,385},{2,130},{3,387},{4,132},{5,389},{6,134},{7,391},{8... | collective-permute-start | bytes 786440 | tf_op jit(solution)/shard_map/ppermute | solution.py:53
  80.5 7.5 %all-to-all-start.2 = ((f32[64,1,128]{2,1,0:T(1,128)}), f32[64,1,128]{2,1,0:T(1,128)S(1)}, u32[]{:S(2)}, u32[]{:S(2)}) async-start(f32[64,1,128]{2,1,0:T(1,128)} %bitcast.14), calls=%async_computation.2 | async-start | bytes 65536 | tf_op jit(solution)/shard_map/all_to_all | solution.py:293
  88.1 1.3 %collective-permute-done.6 = f16[2,64,1024]{2,1,0:T(8,128)(2,1)S(1)} collective-permute-done((f16[2,64,1024]{2,1,0:T(8,128)(2,1)S(1)}, f16[2,64,1024]{2,1,0:T(8,128)(2,1)S(1)}, u32[]{:S(2)}, u32[]{:S(2)}) %collective-permute-start.6) | collective-permute-done | bytes 262176 | tf_op jit(solution)/shard_map/ppermute | solution.py:53
  89.4 2.6 %collective-permute-done.4 = f16[2,64,1024]{2,1,0:T(8,128)(2,1)S(1)} collective-permute-done((f16[2,64,1024]{2,1,0:T(8,128)(2,1)S(1)}, f16[2,64,1024]{2,1,0:T(8,128)(2,1)S(1)}, u32[]{:S(2)}, u32[]{:S(2)}) %collective-permute-start.4) | collective-permute-done | bytes 262176 | tf_op jit(solution)/shard_map/ppermute | solution.py:53
  92.0 1.3 %fusion.11.logits_ref = f32[2,64,1024]{2,1,0:T(8,128)S(1)} fusion(f32[8,2,64,1024]{3,2,1,0:T(8,128)} %copy-done, f16[2,64,1024]{2,1,0:T(8,128)(2,1)S(1)} %collective-permute-done.7, f16[2,64,1024]{2,1,0:T(8,128)(2,1)S(1)} %collective-permute-done.6, f16[2,64,1024]{2,1,0:T(8,128)(2,1)S(1)} %collective-permute-done.4, ...), kind=kLoop, calls=%fused_computation.15 | loop fusion | flops 1572864 | bytes 2097152 | tf_op jit(solution)/shard_map/add | solution.py:294
  93.3 3.8 %all-to-all-done.2.terms_ref = f32[64,1,128]{2,1,0:T(1,128)S(1)} async-done(((f32[64,1,128]{2,1,0:T(1,128)}), f32[64,1,128]{2,1,0:T(1,128)S(1)}, u32[]{:S(2)}, u32[]{:S(2)}) %all-to-all-start.2) | async-done | bytes 32800 | tf_op jit(solution)/shard_map/all_to_all | solution.py:293
  97.0 0.9 shard_map.54
  97.9 14.0 %all_to_all.21.messages_ref = f32[64,2,128]{2,1,0:T(2,128)S(1)} all-to-all(f32[64,2,128]{2,1,0:T(2,128)S(1)} %shard_map.54), channel_id=1, replica_groups=mesh['head'=8,'vocab'=64] {'vocab'}, dimensions={0} | all-to-all | bytes 131072 | tf_op jit(solution)/shard_map/all_to_all | solution.py:297
  112.0 1.7 %shard_map.55 = (bf16[128,1024]{1,0:T(8,128)(2,1)}, f32[8,1024]{1,0:T(8,128)}) custom-call(s32[3]{0:T(128)S(1)} %pad_add_fusion.place_ref, f32[2,64,1024]{2,1,0:T(8,128)S(1)} %fusion.11.logits_ref, f32[64,2,128]{2,1,0:T(2,128)S(1)} %all_to_all.21.messages_ref), custom_call_target="tpu_custom_call" | custom-call | bytes 1048576 | tf_op jit(solution)/shard_map/pallas_call | solution.py:245
  (26 shorter events, 0.5 us)
Async XLA Ops:
  0.6 23.9 %copy-start.7 = (s32[1024]{0:T(1024)S(1)}, s32[1024]{0:T(1024)}, u32[]{:S(2)}) copy-start(s32[1024]{0:T(1024)} %param.5) | copy-start | bytes 12292
  0.6 25.0 %copy-start.1 = (bf16[8,128,1024]{2,1,0:T(8,128)(2,1)S(1)}, bf16[8,128,1024]{2,1,0:T(8,128)(2,1)}, u32[]{:S(2)}) copy-start(bf16[8,128,1024]{2,1,0:T(8,128)(2,1)} %param.4) | copy-start | bytes 6291460
  19.4 17.2 %all-to-all-start.1 = ((bf16[4,8,16,1024]{3,2,1,0:T(8,128)(2,1)}), bf16[4,8,16,1024]{3,2,1,0:T(8,128)(2,1)S(1)}, u32[]{:S(2)}, u32[]{:S(2)}) async-start(bf16[4,8,16,1024]{3,2,1,0:T(8,128)(2,1)} %broadcast_in_dim.15), calls=%async_computation.1 | async-start | bytes 2097152 | tf_op jit(solution)/shard_map/all_to_all | solution.py:41
  25.7 1.0 copy-start.6
  30.6 1.0 copy-start.2
  31.6 1.0 copy-start.4
  36.6 8.1 %collective-permute-start = (bf16[512,1024]{1,0:T(8,128)(2,1)S(1)}, bf16[512,1024]{1,0:T(8,128)(2,1)S(1)}, u32[]{:S(2)}, u32[]{:S(2)}) collective-permute-start(bf16[512,1024]{1,0:T(8,128)(2,1)S(1)} %bitcast.50), channel_id=1, source_target_pairs={{0,1},{1,0},{2,3},{3,2},{4,5},{5,4},{6,7},{7,6},{8,9},{9,8},{10,11... | collective-permute-start | bytes 3145736 | tf_op jit(solution)/shard_map/ppermute | solution.py:273
  44.5 18.4 %copy-start.3 = (bf16[512,1024]{1,0:T(8,128)(2,1)S(1)}, bf16[512,1024]{1,0:T(8,128)(2,1)}, u32[]{:S(2)}) copy-start(bf16[512,1024]{1,0:T(8,128)(2,1)} %copy-done.2) | copy-start | bytes 3145732
  44.5 18.4 %copy-start.5 = (bf16[512,1024]{1,0:T(8,128)(2,1)S(1)}, bf16[512,1024]{1,0:T(8,128)(2,1)}, u32[]{:S(2)}) copy-start(bf16[512,1024]{1,0:T(8,128)(2,1)} %copy-done.4) | copy-start | bytes 3145732
  46.8 23.6 %copy-start = (f32[8,2,64,1024]{3,2,1,0:T(8,128)}, f32[8,2,64,1024]{3,2,1,0:T(8,128)S(1)}, u32[]{:S(2)}) copy-start(f32[8,2,64,1024]{3,2,1,0:T(8,128)S(1)} %shard_map.52) | copy-start | bytes 12582916
  46.9 23.4 %collective-permute-start.5 = (f16[2,64,1024]{2,1,0:T(8,128)(2,1)S(1)}, f16[2,64,1024]{2,1,0:T(8,128)(2,1)S(1)}, u32[]{:S(2)}, u32[]{:S(2)}) collective-permute-start(f16[2,64,1024]{2,1,0:T(8,128)(2,1)S(1)} %fusion.12), channel_id=1, source_target_pairs={{0,448},{1,65},{2,450},{3,67},{4,452},{5,69},{6,454},{7,71},{8,456... | collective-permute-start | bytes 786440 | tf_op jit(solution)/shard_map/ppermute | solution.py:53
  50.9 16.9 %collective-permute-start.2 = (f16[2,64,1024]{2,1,0:T(8,128)(2,1)S(1)}, f16[2,64,1024]{2,1,0:T(8,128)(2,1)S(1)}, u32[]{:S(2)}, u32[]{:S(2)}) collective-permute-start(f16[2,64,1024]{2,1,0:T(8,128)(2,1)S(1)} %fusion.16), channel_id=1, source_target_pairs={{0,128},{1,385},{2,130},{3,387},{4,132},{5,389},{6,134},{7,391},{8... | collective-permute-start | bytes 786440 | tf_op jit(solution)/shard_map/ppermute | solution.py:53
  60.7 9.4 %collective-permute-start.3 = (f16[2,64,1024]{2,1,0:T(8,128)(2,1)S(1)}, f16[2,64,1024]{2,1,0:T(8,128)(2,1)S(1)}, u32[]{:S(2)}, u32[]{:S(2)}) collective-permute-start(f16[2,64,1024]{2,1,0:T(8,128)(2,1)S(1)} %fusion.13), channel_id=1, source_target_pairs={{0,64},{1,449},{2,66},{3,451},{4,68},{5,453},{6,70},{7,455},{8,72}... | collective-permute-start | bytes 786440 | tf_op jit(solution)/shard_map/ppermute | solution.py:53
  65.6 22.4 %collective-permute-start.1 = (f16[2,64,1024]{2,1,0:T(8,128)(2,1)S(1)}, f16[2,64,1024]{2,1,0:T(8,128)(2,1)S(1)}, u32[]{:S(2)}, u32[]{:S(2)}) collective-permute-start(f16[2,64,1024]{2,1,0:T(8,128)(2,1)S(1)} %fusion.14), channel_id=1, source_target_pairs={{0,64},{1,449},{2,66},{3,451},{4,68},{5,453},{6,70},{7,455},{8,72}... | collective-permute-start | bytes 786440 | tf_op jit(solution)/shard_map/ppermute | solution.py:53
  70.4 17.6 %collective-permute-start.7 = (f16[2,64,1024]{2,1,0:T(8,128)(2,1)S(1)}, f16[2,64,1024]{2,1,0:T(8,128)(2,1)S(1)}, u32[]{:S(2)}, u32[]{:S(2)}) collective-permute-start(f16[2,64,1024]{2,1,0:T(8,128)(2,1)S(1)} %fusion.15), channel_id=1, source_target_pairs={{0,448},{1,65},{2,450},{3,67},{4,452},{5,69},{6,454},{7,71},{8,456... | collective-permute-start | bytes 786440 | tf_op jit(solution)/shard_map/ppermute | solution.py:53
  72.4 17.0 %collective-permute-start.6 = (f16[2,64,1024]{2,1,0:T(8,128)(2,1)S(1)}, f16[2,64,1024]{2,1,0:T(8,128)(2,1)S(1)}, u32[]{:S(2)}, u32[]{:S(2)}) collective-permute-start(f16[2,64,1024]{2,1,0:T(8,128)(2,1)S(1)} %fusion.2), channel_id=1, source_target_pairs={{0,384},{1,129},{2,386},{3,131},{4,388},{5,133},{6,390},{7,135},{8... | collective-permute-start | bytes 786440 | tf_op jit(solution)/shard_map/ppermute | solution.py:53
  75.0 17.0 %collective-permute-start.4 = (f16[2,64,1024]{2,1,0:T(8,128)(2,1)S(1)}, f16[2,64,1024]{2,1,0:T(8,128)(2,1)S(1)}, u32[]{:S(2)}, u32[]{:S(2)}) collective-permute-start(f16[2,64,1024]{2,1,0:T(8,128)(2,1)S(1)} %fusion.6), channel_id=1, source_target_pairs={{0,128},{1,385},{2,130},{3,387},{4,132},{5,389},{6,134},{7,391},{8... | collective-permute-start | bytes 786440 | tf_op jit(solution)/shard_map/ppermute | solution.py:53
  80.5 16.5 %all-to-all-start.2 = ((f32[64,1,128]{2,1,0:T(1,128)}), f32[64,1,128]{2,1,0:T(1,128)S(1)}, u32[]{:S(2)}, u32[]{:S(2)}) async-start(f32[64,1,128]{2,1,0:T(1,128)} %bitcast.14), calls=%async_computation.2 | async-start | bytes 65536 | tf_op jit(solution)/shard_map/all_to_all | solution.py:293

commit v4 on v3

--- a/solution.py
+++ b/solution.py
@@ -276,22 +276,25 @@
 
     sent = coded(sums[0])
     four = ring(sent, AHEAD_TWO)
+    sent = coded(tied(sums, sent)[2])
+    three = ring(sent, AHEAD)
     sent = coded(tied(sums, sent)[1])
     five = ring(sent, BACK)
-    sent = coded(tied(sums, sent)[2])
-    three = ring(sent, AHEAD)
+    sent = coded(tied(sums, sent)[6])
+    one = ring(sent, AHEAD)
     terms = head_terms(place, own, tied(other, sent), picked_own, picked_other, heads, per_device)
-    sent = coded(tied(sums, terms)[6])
-    one = ring(sent, AHEAD)
+    sums = tied(sums, terms)
+    sent = coded(tied(sums, sent)[5])
+    seven = ring(sent, BACK)
     sent = coded(sums[4] + decoded(tied(four, sent)) + decoded(three))
     two = ring(sent, AHEAD_TWO)
     sent = coded(sums[3] + decoded(tied(five, sent)))
     six = ring(sent, BACK_TWO)
-    sent = coded(tied(sums, sent)[5])
-    seven = ring(sent, BACK)
     terms = tied(terms, sent).reshape(NV, 1, per_device * heads)
     terms = lax.all_to_all(terms, "vocab", 0, 0, axis_index_groups=CORE_MAJOR, tiled=True)
-    logits = sums[7] + decoded(one) + decoded(two) + decoded(six) + decoded(seven)
+    part = tied(sums, sent)[7] + decoded(one) + decoded(seven)
+    sent = tied(sent, part)
+    logits = part + decoded(two) + decoded(six)
 
     message = stats(place, logits, terms)
     messages = lax.all_to_all(message, "vocab", 0, 0, tiled=True)

time: 114 us -> 110 us (0.965)
  starting transfers between devices: 46.6 us -> 44.2 us
  waiting for transfers between devices: 14.3 us -> 12 us
    all_to_all x1, starting transfers between devices: 7.53 us -> 4.66 us  [on_device(): lax.all_to_all(terms, 'vocab', 0, 0, axis_index_groups=CORE_MAJOR, tiled=...]
    all_to_all x1, waiting for transfers between devices: 3.76 us -> 2.03 us  [on_device(): lax.all_to_all(terms, 'vocab', 0, 0, axis_index_groups=CORE_MAJOR, tiled=...]
  transfers between devices with their start and end apart: 10 -> 10, of which waited for: 6 -> 4; matrix products, arithmetic and copies ran while one was open for 2% -> 3% of each run, Pallas kernels for 7% -> 8%
where the time goes in v4:
time: 110 us; the launch traced here: 109 us
  starting transfers between devices  44.2 us (40%)
  blocking collectives  30.8 us (28%)
  Pallas kernels  13.1 us (12%)
  waiting for transfers between devices  12 us (11%)
  local copies, waits for them, and re-layouts  6.1 us (6%)
  other arithmetic  1.88 us (2%)
    ppermute x7, starting transfers between devices, ring(): return lax.ppermute(values, ('head', 'vocab'), pairs)  28.6 us
    all_to_all x1, blocking collectives, share(): lax.all_to_all(copies, 'vocab', 0, 0, axis_index_groups=groups, tiled=True)  16.7 us
    all_to_all x1, blocking collectives, on_device(): messages = lax.all_to_all(message, 'vocab', 0, 0, tiled=True)  14 us
    ppermute x1, starting transfers between devices, on_device(): other = lax.ppermute(own, 'vocab', CORE_SWAP)  5.86 us
    ppermute x7, waiting for transfers between devices, ring(): return lax.ppermute(values, ('head', 'vocab'), pairs)  5.63 us
    all_to_all x1, starting transfers between devices, share(): lax.all_to_all(copies, 'vocab', 0, 0, axis_index_groups=groups, tiled=True)  5.09 us
    all_to_all x1, starting transfers between devices, on_device(): lax.all_to_all(terms, 'vocab', 0, 0, axis_index_groups=CORE_MAJOR, tiled=...  4.66 us
    all_to_all x1, waiting for transfers between devices, share(): lax.all_to_all(copies, 'vocab', 0, 0, axis_index_groups=groups, tiled=True)  4.09 us
  transfers between devices with their start and end apart: 10, of which 4 were waited for; matrix products, arithmetic and copies ran while one was open for 3% of the time, Pallas kernels for 8%

profile of v4, /device:TPU:1, one launch (start us, length us, event | category | flops | bytes accessed | tf_op | source)
XLA Modules:
  0.0 109.0 jit_solution(9272490765106220769)
XLA Ops:
  0.6 0.9 copy.9
  1.6 16.7 %all_to_all.20 = bf16[8,16,1024]{2,1,0:T(8,128)(2,1)S(1)} all-to-all(bf16[8,16,1024]{2,1,0:T(8,128)(2,1)S(1)} %broadcast_in_dim.14), channel_id=1, replica_groups={{0,2,4,6,8,10,12,14},{1,3,5,7,9,11,13,15},{16,18,20,22,24,26,28,30},{17..., dimensions={0} | all-to-all | bytes 524288 | tf_op jit(solution)/shard_map/all_to_all | solution.py:41
  18.3 1.1 %broadcast_in_dim.15 = bf16[4,8,16,1024]{3,2,1,0:T(8,128)(2,1)} broadcast(bf16[8,16,1024]{2,1,0:T(8,128)(2,1)S(1)} %all_to_all.20), dimensions={1,2,3} | broadcast | bytes 1310720 | tf_op jit(solution)/shard_map/broadcast_in_dim | solution.py:40
  19.4 5.1 %all-to-all-start.1 = ((bf16[4,8,16,1024]{3,2,1,0:T(8,128)(2,1)}), bf16[4,8,16,1024]{3,2,1,0:T(8,128)(2,1)S(1)}, u32[]{:S(2)}, u32[]{:S(2)}) async-start(bf16[4,8,16,1024]{3,2,1,0:T(8,128)(2,1)} %broadcast_in_dim.15), calls=%async_computation.1 | async-start | bytes 2097152 | tf_op jit(solution)/shard_map/all_to_all | solution.py:41
  24.5 1.0 copy.6.ids_ref
  25.6 0.1 pad_add_fusion.place_ref
  25.7 1.0 copy-done.6
  26.7 3.9 %shard_map.50 = (bf16[512,1024]{1,0:T(8,128)(2,1)S(1)}, bf16[512,1024]{1,0:T(8,128)(2,1)S(1)}) custom-call(s32[3]{0:T(128)S(1)} %pad_add_fusion.place_ref, s32[1024,1]{1,0:T(8,128)S(1)} %copy-done.6, bf16[1024,1024]{1,0:T(8,128)(2,1)S(1)} %bitcast.47), custom_call_target="tpu_custom_call" | custom-call | flops 2147483648 | bytes 8388608 | tf_op jit(solution)/shard_map/pallas_call | solution.py:93
  30.6 1.0 copy-done.2
  31.6 1.0 copy-done.4
  32.5 4.1 %all-to-all-done.1 = bf16[4,8,16,1024]{3,2,1,0:T(8,128)(2,1)S(1)} async-done(((bf16[4,8,16,1024]{3,2,1,0:T(8,128)(2,1)}), bf16[4,8,16,1024]{3,2,1,0:T(8,128)(2,1)S(1)}, u32[]{:S(2)}, u32[]{:S(2)}) %all-to-all-start.1) | async-done | bytes 1048608 | tf_op jit(solution)/shard_map/all_to_all | solution.py:41
  36.6 5.9 %collective-permute-start = (bf16[512,1024]{1,0:T(8,128)(2,1)S(1)}, bf16[512,1024]{1,0:T(8,128)(2,1)S(1)}, u32[]{:S(2)}, u32[]{:S(2)}) collective-permute-start(bf16[512,1024]{1,0:T(8,128)(2,1)S(1)} %bitcast.44), channel_id=1, source_target_pairs={{0,1},{1,0},{2,3},{3,2},{4,5},{5,4},{6,7},{7,6},{8,9},{9,8},{10,11... | collective-permute-start | bytes 3145736 | tf_op jit(solution)/shard_map/ppermute | solution.py:273
  42.5 2.0 %shard_map.51.rest_0_ = f32[8,2,64,1024]{3,2,1,0:T(8,128)S(1)} custom-call(s32[3]{0:T(128)S(1)} %pad_add_fusion.place_ref, bf16[512,1024]{1,0:T(8,128)(2,1)S(1)} %bitcast.45, bf16[1024,1024]{1,0:T(8,128)(2,1)S(1)} %bitcast.48), custom_call_target="tpu_custom_call" | custom-call | flops 1073741824 | bytes 6291456 | tf_op jit(solution)/shard_map/pallas_call | solution.py:128
  44.5 0.2 collective-permute-done.rows_ref.other_ref
  44.8 2.0 %shard_map.52 = f32[8,2,64,1024]{3,2,1,0:T(8,128)S(1)} custom-call(s32[3]{0:T(128)S(1)} %pad_add_fusion.place_ref, bf16[512,1024]{1,0:T(8,128)(2,1)S(1)} %collective-permute-done.rows_ref.other_ref, bf16[1024,1024]{1,0:T(8,128)(2,1)S(1)} %bitcast.49, f32[8,2,64,1024]{3,2,1,0:T(8,128)S(1)} %shard_map.51.rest_0_), custom_call_target="tpu_custom_call", output_to_operand_aliasing={{}: (3, {})} | custom-call | flops 1073741824 | bytes 6291456 | tf_op jit(solution)/shard_map/pallas_call | solution.py:128
  46.9 4.0 %collective-permute-start.1 = (f16[2,64,1024]{2,1,0:T(8,128)(2,1)S(1)}, f16[2,64,1024]{2,1,0:T(8,128)(2,1)S(1)}, u32[]{:S(2)}, u32[]{:S(2)}) collective-permute-start(f16[2,64,1024]{2,1,0:T(8,128)(2,1)S(1)} %fusion.10), channel_id=1, source_target_pairs={{0,448},{1,65},{2,450},{3,67},{4,452},{5,69},{6,454},{7,71},{8,456... | collective-permute-start | bytes 786440 | tf_op jit(solution)/shard_map/ppermute | solution.py:53
  50.9 8.6 %collective-permute-start.3 = (f16[2,64,1024]{2,1,0:T(8,128)(2,1)S(1)}, f16[2,64,1024]{2,1,0:T(8,128)(2,1)S(1)}, u32[]{:S(2)}, u32[]{:S(2)}) collective-permute-start(f16[2,64,1024]{2,1,0:T(8,128)(2,1)S(1)} %fusion.9), channel_id=1, source_target_pairs={{0,64},{1,449},{2,66},{3,451},{4,68},{5,453},{6,70},{7,455},{8,72}... | collective-permute-start | bytes 786440 | tf_op jit(solution)/shard_map/ppermute | solution.py:53
  59.5 3.4 %collective-permute-start.2 = (f16[2,64,1024]{2,1,0:T(8,128)(2,1)S(1)}, f16[2,64,1024]{2,1,0:T(8,128)(2,1)S(1)}, u32[]{:S(2)}, u32[]{:S(2)}) collective-permute-start(f16[2,64,1024]{2,1,0:T(8,128)(2,1)S(1)} %fusion.13), channel_id=1, source_target_pairs={{0,128},{1,385},{2,130},{3,387},{4,132},{5,389},{6,134},{7,391},{8... | collective-permute-start | bytes 786440 | tf_op jit(solution)/shard_map/ppermute | solution.py:53
  62.9 2.2 %collective-permute-start.4 = (f16[2,64,1024]{2,1,0:T(8,128)(2,1)S(1)}, f16[2,64,1024]{2,1,0:T(8,128)(2,1)S(1)}, u32[]{:S(2)}, u32[]{:S(2)}) collective-permute-start(f16[2,64,1024]{2,1,0:T(8,128)(2,1)S(1)} %fusion.11), channel_id=1, source_target_pairs={{0,64},{1,449},{2,66},{3,451},{4,68},{5,453},{6,70},{7,455},{8,72}... | collective-permute-start | bytes 786440 | tf_op jit(solution)/shard_map/ppermute | solution.py:53
  65.2 2.6 %shard_map.53 = f32[2,32,1,128]{3,2,1,0:T(1,128)} custom-call(s32[3]{0:T(128)S(1)} %pad_add_fusion.place_ref, bf16[512,1024]{1,0:T(8,128)(2,1)S(1)} %bitcast.46, bf16[512,1024]{1,0:T(8,128)(2,1)S(1)} %collective-permute-done.rows_ref.other_ref, bf16[512,1024]{1,0:T(8,128)(2,1)S(1)} %copy-done.3, bf16[512,1024]{1,0:T(8,128)(2,1)S(1)} %copy-done.5), custom_call_target="tpu_custom_call" | custom-call | flops 1073741824 | bytes 4194304 | tf_op jit(solution)/shard_map/pallas_call | solution.py:169
  67.9 3.1 %collective-permute-start.5 = (f16[2,64,1024]{2,1,0:T(8,128)(2,1)S(1)}, f16[2,64,1024]{2,1,0:T(8,128)(2,1)S(1)}, u32[]{:S(2)}, u32[]{:S(2)}) collective-permute-start(f16[2,64,1024]{2,1,0:T(8,128)(2,1)S(1)} %fusion.12), channel_id=1, source_target_pairs={{0,448},{1,65},{2,450},{3,67},{4,452},{5,69},{6,454},{7,71},{8,456... | collective-permute-start | bytes 786440 | tf_op jit(solution)/shard_map/ppermute | solution.py:53
  71.0 0.2 fusion.6
  71.2 0.1 fusion.8
  71.3 2.8 %collective-permute-start.7 = (f16[2,64,1024]{2,1,0:T(8,128)(2,1)S(1)}, f16[2,64,1024]{2,1,0:T(8,128)(2,1)S(1)}, u32[]{:S(2)}, u32[]{:S(2)}) collective-permute-start(f16[2,64,1024]{2,1,0:T(8,128)(2,1)S(1)} %fusion.8), channel_id=1, source_target_pairs={{0,384},{1,129},{2,386},{3,131},{4,388},{5,133},{6,390},{7,135},{8... | collective-permute-start | bytes 786440 | tf_op jit(solution)/shard_map/ppermute | solution.py:53
  74.1 4.6 %collective-permute-start.6 = (f16[2,64,1024]{2,1,0:T(8,128)(2,1)S(1)}, f16[2,64,1024]{2,1,0:T(8,128)(2,1)S(1)}, u32[]{:S(2)}, u32[]{:S(2)}) collective-permute-start(f16[2,64,1024]{2,1,0:T(8,128)(2,1)S(1)} %fusion.6), channel_id=1, source_target_pairs={{0,128},{1,385},{2,130},{3,387},{4,132},{5,389},{6,134},{7,391},{8... | collective-permute-start | bytes 786440 | tf_op jit(solution)/shard_map/ppermute | solution.py:53
  78.7 4.7 %all-to-all-start.2 = ((f32[64,1,128]{2,1,0:T(1,128)}), f32[64,1,128]{2,1,0:T(1,128)S(1)}, u32[]{:S(2)}, u32[]{:S(2)}) async-start(f32[64,1,128]{2,1,0:T(1,128)} %bitcast.14), calls=%async_computation.2 | async-start | bytes 65536 | tf_op jit(solution)/shard_map/all_to_all | solution.py:294
  83.4 5.6 %collective-permute-done.6 = f16[2,64,1024]{2,1,0:T(8,128)(2,1)S(1)} collective-permute-done((f16[2,64,1024]{2,1,0:T(8,128)(2,1)S(1)}, f16[2,64,1024]{2,1,0:T(8,128)(2,1)S(1)}, u32[]{:S(2)}, u32[]{:S(2)}) %collective-permute-start.6) | collective-permute-done | bytes 262176 | tf_op jit(solution)/shard_map/ppermute | solution.py:53
  89.0 1.3 %fusion.3.logits_ref = f32[2,64,1024]{2,1,0:T(8,128)S(1)} fusion(f16[2,64,1024]{2,1,0:T(8,128)(2,1)S(1)} %collective-permute-done.7, f16[2,64,1024]{2,1,0:T(8,128)(2,1)S(1)} %collective-permute-done.6, f16[2,64,1024]{2,1,0:T(8,128)(2,1)S(1)} %collective-permute-done.5, f16[2,64,1024]{2,1,0:T(8,128)(2,1)S(1)} %collective-permute-done.4, ...), kind=kLoop, calls=%fused_computation.5 | loop fusion | flops 1572864 | bytes 2097152 | tf_op jit(solution)/shard_map/add | solution.py:297
  90.3 2.0 %all-to-all-done.2.terms_ref = f32[64,1,128]{2,1,0:T(1,128)S(1)} async-done(((f32[64,1,128]{2,1,0:T(1,128)}), f32[64,1,128]{2,1,0:T(1,128)S(1)}, u32[]{:S(2)}, u32[]{:S(2)}) %all-to-all-start.2) | async-done | bytes 32800 | tf_op jit(solution)/shard_map/all_to_all | solution.py:294
  92.3 0.9 shard_map.54
  93.3 14.0 %all_to_all.21.messages_ref = f32[64,2,128]{2,1,0:T(2,128)S(1)} all-to-all(f32[64,2,128]{2,1,0:T(2,128)S(1)} %shard_map.54), channel_id=1, replica_groups=mesh['head'=8,'vocab'=64] {'vocab'}, dimensions={0} | all-to-all | bytes 131072 | tf_op jit(solution)/shard_map/all_to_all | solution.py:300
  107.3 1.7 %shard_map.55 = (bf16[128,1024]{1,0:T(8,128)(2,1)}, f32[8,1024]{1,0:T(8,128)}) custom-call(s32[3]{0:T(128)S(1)} %pad_add_fusion.place_ref, f32[2,64,1024]{2,1,0:T(8,128)S(1)} %fusion.3.logits_ref, f32[64,2,128]{2,1,0:T(2,128)S(1)} %all_to_all.21.messages_ref), custom_call_target="tpu_custom_call" | custom-call | bytes 1048576 | tf_op jit(solution)/shard_map/pallas_call | solution.py:245
  (26 shorter events, 0.3 us)
Async XLA Ops:
  0.6 23.9 %copy-start.7 = (s32[1024]{0:T(1024)S(1)}, s32[1024]{0:T(1024)}, u32[]{:S(2)}) copy-start(s32[1024]{0:T(1024)} %param.5) | copy-start | bytes 12292
  0.6 25.0 %copy-start.1 = (bf16[8,128,1024]{2,1,0:T(8,128)(2,1)S(1)}, bf16[8,128,1024]{2,1,0:T(8,128)(2,1)}, u32[]{:S(2)}) copy-start(bf16[8,128,1024]{2,1,0:T(8,128)(2,1)} %param.4) | copy-start | bytes 6291460
  19.4 17.2 %all-to-all-start.1 = ((bf16[4,8,16,1024]{3,2,1,0:T(8,128)(2,1)}), bf16[4,8,16,1024]{3,2,1,0:T(8,128)(2,1)S(1)}, u32[]{:S(2)}, u32[]{:S(2)}) async-start(bf16[4,8,16,1024]{3,2,1,0:T(8,128)(2,1)} %broadcast_in_dim.15), calls=%async_computation.1 | async-start | bytes 2097152 | tf_op jit(solution)/shard_map/all_to_all | solution.py:41
  25.7 1.0 copy-start.6
  30.6 1.0 copy-start.2
  31.5 1.0 copy-start.4
  36.6 8.1 %collective-permute-start = (bf16[512,1024]{1,0:T(8,128)(2,1)S(1)}, bf16[512,1024]{1,0:T(8,128)(2,1)S(1)}, u32[]{:S(2)}, u32[]{:S(2)}) collective-permute-start(bf16[512,1024]{1,0:T(8,128)(2,1)S(1)} %bitcast.44), channel_id=1, source_target_pairs={{0,1},{1,0},{2,3},{3,2},{4,5},{5,4},{6,7},{7,6},{8,9},{9,8},{10,11... | collective-permute-start | bytes 3145736 | tf_op jit(solution)/shard_map/ppermute | solution.py:273
  44.5 20.6 %copy-start.3 = (bf16[512,1024]{1,0:T(8,128)(2,1)S(1)}, bf16[512,1024]{1,0:T(8,128)(2,1)}, u32[]{:S(2)}) copy-start(bf16[512,1024]{1,0:T(8,128)(2,1)} %copy-done.2) | copy-start | bytes 3145732
  44.5 20.6 %copy-start.5 = (bf16[512,1024]{1,0:T(8,128)(2,1)S(1)}, bf16[512,1024]{1,0:T(8,128)(2,1)}, u32[]{:S(2)}) copy-start(bf16[512,1024]{1,0:T(8,128)(2,1)} %copy-done.4) | copy-start | bytes 3145732
  46.7 24.4 %copy-start = (f32[8,2,64,1024]{3,2,1,0:T(8,128)}, f32[8,2,64,1024]{3,2,1,0:T(8,128)S(1)}, u32[]{:S(2)}) copy-start(f32[8,2,64,1024]{3,2,1,0:T(8,128)S(1)} %shard_map.52) | copy-start | bytes 12582916
  46.9 24.2 %collective-permute-start.1 = (f16[2,64,1024]{2,1,0:T(8,128)(2,1)S(1)}, f16[2,64,1024]{2,1,0:T(8,128)(2,1)S(1)}, u32[]{:S(2)}, u32[]{:S(2)}) collective-permute-start(f16[2,64,1024]{2,1,0:T(8,128)(2,1)S(1)} %fusion.10), channel_id=1, source_target_pairs={{0,448},{1,65},{2,450},{3,67},{4,452},{5,69},{6,454},{7,71},{8,456... | collective-permute-start | bytes 786440 | tf_op jit(solution)/shard_map/ppermute | solution.py:53
  50.9 20.1 %collective-permute-start.3 = (f16[2,64,1024]{2,1,0:T(8,128)(2,1)S(1)}, f16[2,64,1024]{2,1,0:T(8,128)(2,1)S(1)}, u32[]{:S(2)}, u32[]{:S(2)}) collective-permute-start(f16[2,64,1024]{2,1,0:T(8,128)(2,1)S(1)} %fusion.9), channel_id=1, source_target_pairs={{0,64},{1,449},{2,66},{3,451},{4,68},{5,453},{6,70},{7,455},{8,72}... | collective-permute-start | bytes 786440 | tf_op jit(solution)/shard_map/ppermute | solution.py:53
  59.5 11.4 %collective-permute-start.2 = (f16[2,64,1024]{2,1,0:T(8,128)(2,1)S(1)}, f16[2,64,1024]{2,1,0:T(8,128)(2,1)S(1)}, u32[]{:S(2)}, u32[]{:S(2)}) collective-permute-start(f16[2,64,1024]{2,1,0:T(8,128)(2,1)S(1)} %fusion.13), channel_id=1, source_target_pairs={{0,128},{1,385},{2,130},{3,387},{4,132},{5,389},{6,134},{7,391},{8... | collective-permute-start | bytes 786440 | tf_op jit(solution)/shard_map/ppermute | solution.py:53
  62.9 20.4 %collective-permute-start.4 = (f16[2,64,1024]{2,1,0:T(8,128)(2,1)S(1)}, f16[2,64,1024]{2,1,0:T(8,128)(2,1)S(1)}, u32[]{:S(2)}, u32[]{:S(2)}) collective-permute-start(f16[2,64,1024]{2,1,0:T(8,128)(2,1)S(1)} %fusion.11), channel_id=1, source_target_pairs={{0,64},{1,449},{2,66},{3,451},{4,68},{5,453},{6,70},{7,455},{8,72}... | collective-permute-start | bytes 786440 | tf_op jit(solution)/shard_map/ppermute | solution.py:53
  67.9 15.5 %collective-permute-start.5 = (f16[2,64,1024]{2,1,0:T(8,128)(2,1)S(1)}, f16[2,64,1024]{2,1,0:T(8,128)(2,1)S(1)}, u32[]{:S(2)}, u32[]{:S(2)}) collective-permute-start(f16[2,64,1024]{2,1,0:T(8,128)(2,1)S(1)} %fusion.12), channel_id=1, source_target_pairs={{0,448},{1,65},{2,450},{3,67},{4,452},{5,69},{6,454},{7,71},{8,456... | collective-permute-start | bytes 786440 | tf_op jit(solution)/shard_map/ppermute | solution.py:53
  71.3 12.1 %collective-permute-start.7 = (f16[2,64,1024]{2,1,0:T(8,128)(2,1)S(1)}, f16[2,64,1024]{2,1,0:T(8,128)(2,1)S(1)}, u32[]{:S(2)}, u32[]{:S(2)}) collective-permute-start(f16[2,64,1024]{2,1,0:T(8,128)(2,1)S(1)} %fusion.8), channel_id=1, source_target_pairs={{0,384},{1,129},{2,386},{3,131},{4,388},{5,133},{6,390},{7,135},{8... | collective-permute-start | bytes 786440 | tf_op jit(solution)/shard_map/ppermute | solution.py:53
  74.1 14.9 %collective-permute-start.6 = (f16[2,64,1024]{2,1,0:T(8,128)(2,1)S(1)}, f16[2,64,1024]{2,1,0:T(8,128)(2,1)S(1)}, u32[]{:S(2)}, u32[]{:S(2)}) collective-permute-start(f16[2,64,1024]{2,1,0:T(8,128)(2,1)S(1)} %fusion.6), channel_id=1, source_target_pairs={{0,128},{1,385},{2,130},{3,387},{4,132},{5,389},{6,134},{7,391},{8... | collective-permute-start | bytes 786440 | tf_op jit(solution)/shard_map/ppermute | solution.py:53
  78.7 13.6 %all-to-all-start.2 = ((f32[64,1,128]{2,1,0:T(1,128)}), f32[64,1,128]{2,1,0:T(1,128)S(1)}, u32[]{:S(2)}, u32[]{:S(2)}) async-start(f32[64,1,128]{2,1,0:T(1,128)} %bitcast.14), calls=%async_computation.2 | async-start | bytes 65536 | tf_op jit(solution)/shard_map/all_to_all | solution.py:294

commit v5 on v4

--- a/solution.py
+++ b/solution.py
@@ -224,20 +224,21 @@
         for place in range(half // per_device):
             start = (place * NC + c) * per_device
             out_ref[start : start + per_device] = values[place * per_device : (place + 1) * per_device]
-    terms = messages_ref[:, 1, :]
     shape = (NV, per_device, size)
     token = lax.broadcasted_iota(jnp.int32, shape, 1)
-    lane_token = lax.broadcasted_iota(jnp.int32, shape, 2) // heads
-    terms = jnp.where(token == lane_token, jnp.broadcast_to(terms[:, None, :], shape), 0.0)
+    here = token == lax.broadcasted_iota(jnp.int32, shape, 2) // heads
     head = lax.broadcasted_iota(jnp.int32, (heads, size), 0)
     lane_head = lax.broadcasted_iota(jnp.int32, (heads, size), 1) % heads
-    attribution_ref[...] = lax.dot_general(
-        (head == lane_head).astype(jnp.float32),
-        terms.reshape(NV * per_device, size),
-        (((1,), (1,)), ((), ())),
-        preferred_element_type=jnp.float32,
-        precision=lax.Precision.HIGHEST,
-    )
+    same = (head == lane_head).astype(jnp.float32).astype(jnp.bfloat16)
+    left = messages_ref[:, 1, :]
+    total = jnp.zeros((heads, NV * per_device), jnp.float32)
+    for _ in range(3):
+        part = left.astype(jnp.bfloat16).astype(jnp.float32)
+        left = left - part
+        spread = jnp.where(here, jnp.broadcast_to(part[:, None, :], shape), 0.0)
+        spread = spread.reshape(NV * per_device, size).astype(jnp.bfloat16)
+        total += lax.dot_general(same, spread, (((1,), (1,)), ((), ())), preferred_element_type=jnp.float32)
+    attribution_ref[...] = total
 
 
 def finish(place, logits, messages, heads, per_device):
@@ -286,15 +287,14 @@
     sums = tied(sums, terms)
     sent = coded(tied(sums, sent)[5])
     seven = ring(sent, BACK)
+    sent = coded(sums[3] + decoded(tied(five, sent)))
+    six = ring(sent, BACK_TWO)
     sent = coded(sums[4] + decoded(tied(four, sent)) + decoded(three))
     two = ring(sent, AHEAD_TWO)
-    sent = coded(sums[3] + decoded(tied(five, sent)))
-    six = ring(sent, BACK_TWO)
     terms = tied(terms, sent).reshape(NV, 1, per_device * heads)
     terms = lax.all_to_all(terms, "vocab", 0, 0, axis_index_groups=CORE_MAJOR, tiled=True)
     part = tied(sums, sent)[7] + decoded(one) + decoded(seven)
-    sent = tied(sent, part)
-    logits = part + decoded(two) + decoded(six)
+    logits = tied(part, sent) + decoded(two) + decoded(six)
 
     message = stats(place, logits, terms)
     messages = lax.all_to_all(message, "vocab", 0, 0, tiled=True)

time: 110 us -> 110 us (level)
  waiting for transfers between devices: 12 us -> 13.2 us
    unnamed x17 -> x15, local copies, waits for them, and re-layouts: 3.93 us -> 3.93 us
  transfers between devices with their start and end apart: 10 -> 10, of which waited for: 4 -> 4; matrix products, arithmetic and copies ran while one was open for 3% -> 2% of each run, Pallas kernels for 8% -> 8%
where the time goes in v5:
time: 110 us; the launch traced here: 109 us
  starting transfers between devices  44.2 us (40%)
  blocking collectives  30.8 us (28%)
  waiting for transfers between devices  13.2 us (12%)
  Pallas kernels  12.9 us (12%)
  local copies, waits for them, and re-layouts  6.12 us (6%)
    ppermute x7, starting transfers between devices, ring(): return lax.ppermute(values, ('head', 'vocab'), pairs)  28.6 us
    all_to_all x1, blocking collectives, share(): lax.all_to_all(copies, 'vocab', 0, 0, axis_index_groups=groups, tiled=True)  16.7 us
    all_to_all x1, blocking collectives, on_device(): messages = lax.all_to_all(message, 'vocab', 0, 0, tiled=True)  14 us
    ppermute x1, starting transfers between devices, on_device(): other = lax.ppermute(own, 'vocab', CORE_SWAP)  5.86 us
    ppermute x7, waiting for transfers between devices, ring(): return lax.ppermute(values, ('head', 'vocab'), pairs)  5.81 us
    all_to_all x1, starting transfers between devices, share(): lax.all_to_all(copies, 'vocab', 0, 0, axis_index_groups=groups, tiled=True)  5.09 us
    all_to_all x1, starting transfers between devices, on_device(): lax.all_to_all(terms, 'vocab', 0, 0, axis_index_groups=CORE_MAJOR, tiled=...  4.67 us
    all_to_all x1, waiting for transfers between devices, share(): lax.all_to_all(copies, 'vocab', 0, 0, axis_index_groups=groups, tiled=True)  4.08 us
  transfers between devices with their start and end apart: 10, of which 4 were waited for; matrix products, arithmetic and copies ran while one was open for 2% of the time, Pallas kernels for 8%

profile of v5, /device:TPU:1, one launch (start us, length us, event | category | flops | bytes accessed | tf_op | source)
XLA Modules:
  0.0 109.0 jit_solution(13002742866521429002)
XLA Ops:
  0.6 0.9 copy.9
  1.6 16.7 %all_to_all.20 = bf16[8,16,1024]{2,1,0:T(8,128)(2,1)S(1)} all-to-all(bf16[8,16,1024]{2,1,0:T(8,128)(2,1)S(1)} %broadcast_in_dim.14), channel_id=1, replica_groups={{0,2,4,6,8,10,12,14},{1,3,5,7,9,11,13,15},{16,18,20,22,24,26,28,30},{17..., dimensions={0} | all-to-all | bytes 524288 | tf_op jit(solution)/shard_map/all_to_all | solution.py:41
  18.3 1.1 %broadcast_in_dim.15 = bf16[4,8,16,1024]{3,2,1,0:T(8,128)(2,1)} broadcast(bf16[8,16,1024]{2,1,0:T(8,128)(2,1)S(1)} %all_to_all.20), dimensions={1,2,3} | broadcast | bytes 1310720 | tf_op jit(solution)/shard_map/broadcast_in_dim | solution.py:40
  19.5 5.1 %all-to-all-start.1 = ((bf16[4,8,16,1024]{3,2,1,0:T(8,128)(2,1)}), bf16[4,8,16,1024]{3,2,1,0:T(8,128)(2,1)S(1)}, u32[]{:S(2)}, u32[]{:S(2)}) async-start(bf16[4,8,16,1024]{3,2,1,0:T(8,128)(2,1)} %broadcast_in_dim.15), calls=%async_computation.1 | async-start | bytes 2097152 | tf_op jit(solution)/shard_map/all_to_all | solution.py:41
  24.6 1.1 copy.6.ids_ref
  25.7 1.0 copy-done.5
  26.7 3.9 %shard_map.50 = (bf16[512,1024]{1,0:T(8,128)(2,1)S(1)}, bf16[512,1024]{1,0:T(8,128)(2,1)S(1)}) custom-call(s32[3]{0:T(128)S(1)} %pad_add_fusion.place_ref, s32[1024,1]{1,0:T(8,128)S(1)} %copy-done.5, bf16[1024,1024]{1,0:T(8,128)(2,1)S(1)} %bitcast.43), custom_call_target="tpu_custom_call" | custom-call | flops 2147483648 | bytes 8388608 | tf_op jit(solution)/shard_map/pallas_call | solution.py:93
  30.6 1.0 copy-done.1
  31.6 1.0 copy-done.3
  32.6 4.1 %all-to-all-done.1 = bf16[4,8,16,1024]{3,2,1,0:T(8,128)(2,1)S(1)} async-done(((bf16[4,8,16,1024]{3,2,1,0:T(8,128)(2,1)}), bf16[4,8,16,1024]{3,2,1,0:T(8,128)(2,1)S(1)}, u32[]{:S(2)}, u32[]{:S(2)}) %all-to-all-start.1) | async-done | bytes 1048608 | tf_op jit(solution)/shard_map/all_to_all | solution.py:41
  36.6 5.9 %collective-permute-start = (bf16[512,1024]{1,0:T(8,128)(2,1)S(1)}, bf16[512,1024]{1,0:T(8,128)(2,1)S(1)}, u32[]{:S(2)}, u32[]{:S(2)}) collective-permute-start(bf16[512,1024]{1,0:T(8,128)(2,1)S(1)} %bitcast.40), channel_id=1, source_target_pairs={{0,1},{1,0},{2,3},{3,2},{4,5},{5,4},{6,7},{7,6},{8,9},{9,8},{10,11... | collective-permute-start | bytes 3145736 | tf_op jit(solution)/shard_map/ppermute | solution.py:274
  42.5 2.0 %shard_map.51.rest_0_ = f32[8,2,64,1024]{3,2,1,0:T(8,128)S(1)} custom-call(s32[3]{0:T(128)S(1)} %pad_add_fusion.place_ref, bf16[512,1024]{1,0:T(8,128)(2,1)S(1)} %bitcast.41, bf16[1024,1024]{1,0:T(8,128)(2,1)S(1)} %bitcast.44), custom_call_target="tpu_custom_call" | custom-call | flops 1073741824 | bytes 6291456 | tf_op jit(solution)/shard_map/pallas_call | solution.py:128
  44.5 0.2 collective-permute-done.rows_ref.other_ref
  44.8 2.0 %shard_map.52 = f32[8,2,64,1024]{3,2,1,0:T(8,128)S(1)} custom-call(s32[3]{0:T(128)S(1)} %pad_add_fusion.place_ref, bf16[512,1024]{1,0:T(8,128)(2,1)S(1)} %collective-permute-done.rows_ref.other_ref, bf16[1024,1024]{1,0:T(8,128)(2,1)S(1)} %bitcast.45, f32[8,2,64,1024]{3,2,1,0:T(8,128)S(1)} %shard_map.51.rest_0_), custom_call_target="tpu_custom_call", output_to_operand_aliasing={{}: (3, {})} | custom-call | flops 1073741824 | bytes 6291456 | tf_op jit(solution)/shard_map/pallas_call | solution.py:128
  46.9 4.0 %collective-permute-start.2 = (f16[2,64,1024]{2,1,0:T(8,128)(2,1)S(1)}, f16[2,64,1024]{2,1,0:T(8,128)(2,1)S(1)}, u32[]{:S(2)}, u32[]{:S(2)}) collective-permute-start(f16[2,64,1024]{2,1,0:T(8,128)(2,1)S(1)} %fusion.8), channel_id=1, source_target_pairs={{0,448},{1,65},{2,450},{3,67},{4,452},{5,69},{6,454},{7,71},{8,456... | collective-permute-start | bytes 786440 | tf_op jit(solution)/shard_map/ppermute | solution.py:53
  50.9 8.6 %collective-permute-start.3 = (f16[2,64,1024]{2,1,0:T(8,128)(2,1)S(1)}, f16[2,64,1024]{2,1,0:T(8,128)(2,1)S(1)}, u32[]{:S(2)}, u32[]{:S(2)}) collective-permute-start(f16[2,64,1024]{2,1,0:T(8,128)(2,1)S(1)} %fusion.7), channel_id=1, source_target_pairs={{0,64},{1,449},{2,66},{3,451},{4,68},{5,453},{6,70},{7,455},{8,72}... | collective-permute-start | bytes 786440 | tf_op jit(solution)/shard_map/ppermute | solution.py:53
  59.5 3.4 %collective-permute-start.1 = (f16[2,64,1024]{2,1,0:T(8,128)(2,1)S(1)}, f16[2,64,1024]{2,1,0:T(8,128)(2,1)S(1)}, u32[]{:S(2)}, u32[]{:S(2)}) collective-permute-start(f16[2,64,1024]{2,1,0:T(8,128)(2,1)S(1)} %fusion.11), channel_id=1, source_target_pairs={{0,128},{1,385},{2,130},{3,387},{4,132},{5,389},{6,134},{7,391},{8... | collective-permute-start | bytes 786440 | tf_op jit(solution)/shard_map/ppermute | solution.py:53
  62.9 2.2 %collective-permute-start.4 = (f16[2,64,1024]{2,1,0:T(8,128)(2,1)S(1)}, f16[2,64,1024]{2,1,0:T(8,128)(2,1)S(1)}, u32[]{:S(2)}, u32[]{:S(2)}) collective-permute-start(f16[2,64,1024]{2,1,0:T(8,128)(2,1)S(1)} %fusion.9), channel_id=1, source_target_pairs={{0,64},{1,449},{2,66},{3,451},{4,68},{5,453},{6,70},{7,455},{8,72}... | collective-permute-start | bytes 786440 | tf_op jit(solution)/shard_map/ppermute | solution.py:53
  65.2 2.6 %shard_map.53 = f32[2,32,1,128]{3,2,1,0:T(1,128)} custom-call(s32[3]{0:T(128)S(1)} %pad_add_fusion.place_ref, bf16[512,1024]{1,0:T(8,128)(2,1)S(1)} %bitcast.42, bf16[512,1024]{1,0:T(8,128)(2,1)S(1)} %collective-permute-done.rows_ref.other_ref, bf16[512,1024]{1,0:T(8,128)(2,1)S(1)} %copy-done.2, bf16[512,1024]{1,0:T(8,128)(2,1)S(1)} %copy-done.4), custom_call_target="tpu_custom_call" | custom-call | flops 1073741824 | bytes 4194304 | tf_op jit(solution)/shard_map/pallas_call | solution.py:169
  67.9 3.1 %collective-permute-start.5 = (f16[2,64,1024]{2,1,0:T(8,128)(2,1)S(1)}, f16[2,64,1024]{2,1,0:T(8,128)(2,1)S(1)}, u32[]{:S(2)}, u32[]{:S(2)}) collective-permute-start(f16[2,64,1024]{2,1,0:T(8,128)(2,1)S(1)} %fusion.10), channel_id=1, source_target_pairs={{0,448},{1,65},{2,450},{3,67},{4,452},{5,69},{6,454},{7,71},{8,456... | collective-permute-start | bytes 786440 | tf_op jit(solution)/shard_map/ppermute | solution.py:53
  71.0 0.1 fusion.3
  71.1 2.8 %collective-permute-start.7 = (f16[2,64,1024]{2,1,0:T(8,128)(2,1)S(1)}, f16[2,64,1024]{2,1,0:T(8,128)(2,1)S(1)}, u32[]{:S(2)}, u32[]{:S(2)}) collective-permute-start(f16[2,64,1024]{2,1,0:T(8,128)(2,1)S(1)} %fusion.3), channel_id=1, source_target_pairs={{0,384},{1,129},{2,386},{3,131},{4,388},{5,133},{6,390},{7,135},{8... | collective-permute-start | bytes 786440 | tf_op jit(solution)/shard_map/ppermute | solution.py:53
  73.9 0.2 fusion.6
  74.1 4.6 %collective-permute-start.6 = (f16[2,64,1024]{2,1,0:T(8,128)(2,1)S(1)}, f16[2,64,1024]{2,1,0:T(8,128)(2,1)S(1)}, u32[]{:S(2)}, u32[]{:S(2)}) collective-permute-start(f16[2,64,1024]{2,1,0:T(8,128)(2,1)S(1)} %fusion.6), channel_id=1, source_target_pairs={{0,128},{1,385},{2,130},{3,387},{4,132},{5,389},{6,134},{7,391},{8... | collective-permute-start | bytes 786440 | tf_op jit(solution)/shard_map/ppermute | solution.py:53
  78.7 0.1 fusion.1
  78.8 4.7 %all-to-all-start.2 = ((f32[64,1,128]{2,1,0:T(1,128)}), f32[64,1,128]{2,1,0:T(1,128)S(1)}, u32[]{:S(2)}, u32[]{:S(2)}) async-start(f32[64,1,128]{2,1,0:T(1,128)} %bitcast.14), calls=%async_computation.2 | async-start | bytes 65536 | tf_op jit(solution)/shard_map/all_to_all | solution.py:295
  83.5 5.8 %collective-permute-done.6 = f16[2,64,1024]{2,1,0:T(8,128)(2,1)S(1)} collective-permute-done((f16[2,64,1024]{2,1,0:T(8,128)(2,1)S(1)}, f16[2,64,1024]{2,1,0:T(8,128)(2,1)S(1)}, u32[]{:S(2)}, u32[]{:S(2)}) %collective-permute-start.6) | collective-permute-done | bytes 262176 | tf_op jit(solution)/shard_map/ppermute | solution.py:53
  89.3 0.1 multiply_add_fusion.logits_ref
  89.4 3.0 %all-to-all-done.2.terms_ref = f32[64,1,128]{2,1,0:T(1,128)S(1)} async-done(((f32[64,1,128]{2,1,0:T(1,128)}), f32[64,1,128]{2,1,0:T(1,128)S(1)}, u32[]{:S(2)}, u32[]{:S(2)}) %all-to-all-start.2) | async-done | bytes 32800 | tf_op jit(solution)/shard_map/all_to_all | solution.py:295
  92.5 0.9 shard_map.54
  93.4 14.0 %all_to_all.21.messages_ref = f32[64,2,128]{2,1,0:T(2,128)S(1)} all-to-all(f32[64,2,128]{2,1,0:T(2,128)S(1)} %shard_map.54), channel_id=1, replica_groups=mesh['head'=8,'vocab'=64] {'vocab'}, dimensions={0} | all-to-all | bytes 131072 | tf_op jit(solution)/shard_map/all_to_all | solution.py:300
  107.4 1.5 %shard_map.55 = (bf16[128,1024]{1,0:T(8,128)(2,1)}, f32[8,1024]{1,0:T(8,128)}) custom-call(s32[3]{0:T(128)S(1)} %pad_add_fusion.place_ref, f32[2,64,1024]{2,1,0:T(8,128)S(1)} %multiply_add_fusion.logits_ref, f32[64,2,128]{2,1,0:T(2,128)S(1)} %all_to_all.21.messages_ref), custom_call_target="tpu_custom_call" | custom-call | bytes 1048576 | tf_op jit(solution)/shard_map/pallas_call | solution.py:246
  (25 shorter events, 0.4 us)
Async XLA Ops:
  0.6 23.9 %copy-start.6 = (s32[1024]{0:T(1024)S(1)}, s32[1024]{0:T(1024)}, u32[]{:S(2)}) copy-start(s32[1024]{0:T(1024)} %param.5) | copy-start | bytes 12292
  0.6 25.0 %copy-start = (bf16[8,128,1024]{2,1,0:T(8,128)(2,1)S(1)}, bf16[8,128,1024]{2,1,0:T(8,128)(2,1)}, u32[]{:S(2)}) copy-start(bf16[8,128,1024]{2,1,0:T(8,128)(2,1)} %param.4) | copy-start | bytes 6291460
  19.5 17.2 %all-to-all-start.1 = ((bf16[4,8,16,1024]{3,2,1,0:T(8,128)(2,1)}), bf16[4,8,16,1024]{3,2,1,0:T(8,128)(2,1)S(1)}, u32[]{:S(2)}, u32[]{:S(2)}) async-start(bf16[4,8,16,1024]{3,2,1,0:T(8,128)(2,1)} %broadcast_in_dim.15), calls=%async_computation.1 | async-start | bytes 2097152 | tf_op jit(solution)/shard_map/all_to_all | solution.py:41
  25.7 1.0 copy-start.5
  30.6 1.0 copy-start.1
  31.6 1.0 copy-start.3
  36.6 8.1 %collective-permute-start = (bf16[512,1024]{1,0:T(8,128)(2,1)S(1)}, bf16[512,1024]{1,0:T(8,128)(2,1)S(1)}, u32[]{:S(2)}, u32[]{:S(2)}) collective-permute-start(bf16[512,1024]{1,0:T(8,128)(2,1)S(1)} %bitcast.40), channel_id=1, source_target_pairs={{0,1},{1,0},{2,3},{3,2},{4,5},{5,4},{6,7},{7,6},{8,9},{9,8},{10,11... | collective-permute-start | bytes 3145736 | tf_op jit(solution)/shard_map/ppermute | solution.py:274
  44.5 20.6 %copy-start.2 = (bf16[512,1024]{1,0:T(8,128)(2,1)S(1)}, bf16[512,1024]{1,0:T(8,128)(2,1)}, u32[]{:S(2)}) copy-start(bf16[512,1024]{1,0:T(8,128)(2,1)} %copy-done.1) | copy-start | bytes 3145732
  44.5 20.6 %copy-start.4 = (bf16[512,1024]{1,0:T(8,128)(2,1)S(1)}, bf16[512,1024]{1,0:T(8,128)(2,1)}, u32[]{:S(2)}) copy-start(bf16[512,1024]{1,0:T(8,128)(2,1)} %copy-done.3) | copy-start | bytes 3145732
  46.9 24.0 %collective-permute-start.2 = (f16[2,64,1024]{2,1,0:T(8,128)(2,1)S(1)}, f16[2,64,1024]{2,1,0:T(8,128)(2,1)S(1)}, u32[]{:S(2)}, u32[]{:S(2)}) collective-permute-start(f16[2,64,1024]{2,1,0:T(8,128)(2,1)S(1)} %fusion.8), channel_id=1, source_target_pairs={{0,448},{1,65},{2,450},{3,67},{4,452},{5,69},{6,454},{7,71},{8,456... | collective-permute-start | bytes 786440 | tf_op jit(solution)/shard_map/ppermute | solution.py:53
  50.9 23.0 %collective-permute-start.3 = (f16[2,64,1024]{2,1,0:T(8,128)(2,1)S(1)}, f16[2,64,1024]{2,1,0:T(8,128)(2,1)S(1)}, u32[]{:S(2)}, u32[]{:S(2)}) collective-permute-start(f16[2,64,1024]{2,1,0:T(8,128)(2,1)S(1)} %fusion.7), channel_id=1, source_target_pairs={{0,64},{1,449},{2,66},{3,451},{4,68},{5,453},{6,70},{7,455},{8,72}... | collective-permute-start | bytes 786440 | tf_op jit(solution)/shard_map/ppermute | solution.py:53
  59.5 14.4 %collective-permute-start.1 = (f16[2,64,1024]{2,1,0:T(8,128)(2,1)S(1)}, f16[2,64,1024]{2,1,0:T(8,128)(2,1)S(1)}, u32[]{:S(2)}, u32[]{:S(2)}) collective-permute-start(f16[2,64,1024]{2,1,0:T(8,128)(2,1)S(1)} %fusion.11), channel_id=1, source_target_pairs={{0,128},{1,385},{2,130},{3,387},{4,132},{5,389},{6,134},{7,391},{8... | collective-permute-start | bytes 786440 | tf_op jit(solution)/shard_map/ppermute | solution.py:53
  62.9 15.8 %collective-permute-start.4 = (f16[2,64,1024]{2,1,0:T(8,128)(2,1)S(1)}, f16[2,64,1024]{2,1,0:T(8,128)(2,1)S(1)}, u32[]{:S(2)}, u32[]{:S(2)}) collective-permute-start(f16[2,64,1024]{2,1,0:T(8,128)(2,1)S(1)} %fusion.9), channel_id=1, source_target_pairs={{0,64},{1,449},{2,66},{3,451},{4,68},{5,453},{6,70},{7,455},{8,72}... | collective-permute-start | bytes 786440 | tf_op jit(solution)/shard_map/ppermute | solution.py:53
  67.9 10.8 %collective-permute-start.5 = (f16[2,64,1024]{2,1,0:T(8,128)(2,1)S(1)}, f16[2,64,1024]{2,1,0:T(8,128)(2,1)S(1)}, u32[]{:S(2)}, u32[]{:S(2)}) collective-permute-start(f16[2,64,1024]{2,1,0:T(8,128)(2,1)S(1)} %fusion.10), channel_id=1, source_target_pairs={{0,448},{1,65},{2,450},{3,67},{4,452},{5,69},{6,454},{7,71},{8,456... | collective-permute-start | bytes 786440 | tf_op jit(solution)/shard_map/ppermute | solution.py:53
  71.1 12.4 %collective-permute-start.7 = (f16[2,64,1024]{2,1,0:T(8,128)(2,1)S(1)}, f16[2,64,1024]{2,1,0:T(8,128)(2,1)S(1)}, u32[]{:S(2)}, u32[]{:S(2)}) collective-permute-start(f16[2,64,1024]{2,1,0:T(8,128)(2,1)S(1)} %fusion.3), channel_id=1, source_target_pairs={{0,384},{1,129},{2,386},{3,131},{4,388},{5,133},{6,390},{7,135},{8... | collective-permute-start | bytes 786440 | tf_op jit(solution)/shard_map/ppermute | solution.py:53
  74.1 15.2 %collective-permute-start.6 = (f16[2,64,1024]{2,1,0:T(8,128)(2,1)S(1)}, f16[2,64,1024]{2,1,0:T(8,128)(2,1)S(1)}, u32[]{:S(2)}, u32[]{:S(2)}) collective-permute-start(f16[2,64,1024]{2,1,0:T(8,128)(2,1)S(1)} %fusion.6), channel_id=1, source_target_pairs={{0,128},{1,385},{2,130},{3,387},{4,132},{5,389},{6,134},{7,391},{8... | collective-permute-start | bytes 786440 | tf_op jit(solution)/shard_map/ppermute | solution.py:53
  78.8 13.7 %all-to-all-start.2 = ((f32[64,1,128]{2,1,0:T(1,128)}), f32[64,1,128]{2,1,0:T(1,128)S(1)}, u32[]{:S(2)}, u32[]{:S(2)}) async-start(f32[64,1,128]{2,1,0:T(1,128)} %bitcast.14), calls=%async_computation.2 | async-start | bytes 65536 | tf_op jit(solution)/shard_map/all_to_all | solution.py:295

commit v6 on v5

--- a/solution.py
+++ b/solution.py
@@ -62,7 +62,7 @@
 
 
 def params():
-    return pltpu.CompilerParams(vmem_limit_bytes=20 * MIB)
+    return pltpu.CompilerParams(vmem_limit_bytes=14 * MIB)
 
 
 SMEM = pl.BlockSpec(memory_space=pltpu.SMEM)
@@ -112,8 +112,7 @@
     parts = rows_ref.shape[0] // block
     sums = jnp.dot(rows_ref[...], weights_ref[...], preferred_element_type=jnp.float32)
     for part in range(parts):
-        target = pl.program_id(0) * parts + part
-        distance = jnp.bitwise_and((target - z) * way, NZ - 1)
+        distance = jnp.bitwise_and((part - z) * way, NZ - 1)
         slot = jnp.int32(0)
         for key, value in SLOT_OF.items():
             slot = jnp.where(distance == key, value, slot)
@@ -123,12 +122,10 @@
 def partial_sums(place, rows, weights, earlier=None):
     tokens, depth = rows.shape
     slab = weights.shape[1]
-    steps = 2
     kind = 0 if earlier is None else 1
     return pl.pallas_call(
         functools.partial(sums_kernel, kind),
-        grid=(steps,),
-        in_specs=[SMEM, pl.BlockSpec((tokens // steps, depth), lambda i: (i, 0)), VMEM] + [VMEM] * kind,
+        in_specs=[SMEM, VMEM, VMEM] + [VMEM] * kind,
         out_specs=VMEM,
         out_shape=jax.ShapeDtypeStruct((NZ, NC, tokens // NZ, slab), jnp.float32),
         input_output_aliases={3: 0} if kind else {},

time: 110 us -> 109 us (level)
  no operation moved by 1% of the time
where the time goes in v6:
time: 109 us
  starting transfers between devices  44.2 us (41%)
  blocking collectives  30.8 us (28%)
  waiting for transfers between devices  13.4 us (12%)
  Pallas kernels  12.5 us (11%)
  local copies, waits for them, and re-layouts  6.12 us (6%)
    ppermute x7, starting transfers between devices, ring(): return lax.ppermute(values, ('head', 'vocab'), pairs)  28.6 us
    all_to_all x1, blocking collectives, share(): lax.all_to_all(copies, 'vocab', 0, 0, axis_index_groups=groups, tiled=True)  16.7 us
    all_to_all x1, blocking collectives, on_device(): messages = lax.all_to_all(message, 'vocab', 0, 0, tiled=True)  14 us
    ppermute x1, starting transfers between devices, on_device(): other = lax.ppermute(own, 'vocab', CORE_SWAP)  5.86 us
    ppermute x7, waiting for transfers between devices, ring(): return lax.ppermute(values, ('head', 'vocab'), pairs)  5.81 us
    all_to_all x1, starting transfers between devices, share(): lax.all_to_all(copies, 'vocab', 0, 0, axis_index_groups=groups, tiled=True)  5.09 us
    all_to_all x1, starting transfers between devices, on_device(): lax.all_to_all(terms, 'vocab', 0, 0, axis_index_groups=CORE_MAJOR, tiled=...  4.66 us
    all_to_all x1, waiting for transfers between devices, share(): lax.all_to_all(copies, 'vocab', 0, 0, axis_index_groups=groups, tiled=True)  4.08 us
  transfers between devices with their start and end apart: 10, of which 4 were waited for; matrix products, arithmetic and copies ran while one was open for 2% of the time, Pallas kernels for 8%

profile of v6, /device:TPU:1, one launch (start us, length us, event | category | flops | bytes accessed | tf_op | source)
XLA Modules:
  0.0 108.8 jit_solution(13517927151903936658)
XLA Ops:
  0.6 0.9 copy.9
  1.6 16.7 %all_to_all.20 = bf16[8,16,1024]{2,1,0:T(8,128)(2,1)S(1)} all-to-all(bf16[8,16,1024]{2,1,0:T(8,128)(2,1)S(1)} %broadcast_in_dim.14), channel_id=1, replica_groups={{0,2,4,6,8,10,12,14},{1,3,5,7,9,11,13,15},{16,18,20,22,24,26,28,30},{17..., dimensions={0} | all-to-all | bytes 524288 | tf_op jit(solution)/shard_map/all_to_all | solution.py:41
  18.3 1.1 %broadcast_in_dim.15 = bf16[4,8,16,1024]{3,2,1,0:T(8,128)(2,1)} broadcast(bf16[8,16,1024]{2,1,0:T(8,128)(2,1)S(1)} %all_to_all.20), dimensions={1,2,3} | broadcast | bytes 1310720 | tf_op jit(solution)/shard_map/broadcast_in_dim | solution.py:40
  19.5 5.1 %all-to-all-start.1 = ((bf16[4,8,16,1024]{3,2,1,0:T(8,128)(2,1)}), bf16[4,8,16,1024]{3,2,1,0:T(8,128)(2,1)S(1)}, u32[]{:S(2)}, u32[]{:S(2)}) async-start(bf16[4,8,16,1024]{3,2,1,0:T(8,128)(2,1)} %broadcast_in_dim.15), calls=%async_computation.1 | async-start | bytes 2097152 | tf_op jit(solution)/shard_map/all_to_all | solution.py:41
  24.6 1.1 copy.6.ids_ref
  25.7 1.0 copy-done.5
  26.7 3.9 %shard_map.50 = (bf16[512,1024]{1,0:T(8,128)(2,1)S(1)}, bf16[512,1024]{1,0:T(8,128)(2,1)S(1)}) custom-call(s32[3]{0:T(128)S(1)} %pad_add_fusion.place_ref, s32[1024,1]{1,0:T(8,128)S(1)} %copy-done.5, bf16[1024,1024]{1,0:T(8,128)(2,1)S(1)} %bitcast.43), custom_call_target="tpu_custom_call" | custom-call | flops 2147483648 | bytes 8388608 | tf_op jit(solution)/shard_map/pallas_call | solution.py:93
  30.6 1.0 copy-done.1
  31.6 1.0 copy-done.3
  32.6 4.1 %all-to-all-done.1 = bf16[4,8,16,1024]{3,2,1,0:T(8,128)(2,1)S(1)} async-done(((bf16[4,8,16,1024]{3,2,1,0:T(8,128)(2,1)}), bf16[4,8,16,1024]{3,2,1,0:T(8,128)(2,1)S(1)}, u32[]{:S(2)}, u32[]{:S(2)}) %all-to-all-start.1) | async-done | bytes 1048608 | tf_op jit(solution)/shard_map/all_to_all | solution.py:41
  36.6 5.9 %collective-permute-start = (bf16[512,1024]{1,0:T(8,128)(2,1)S(1)}, bf16[512,1024]{1,0:T(8,128)(2,1)S(1)}, u32[]{:S(2)}, u32[]{:S(2)}) collective-permute-start(bf16[512,1024]{1,0:T(8,128)(2,1)S(1)} %bitcast.40), channel_id=1, source_target_pairs={{0,1},{1,0},{2,3},{3,2},{4,5},{5,4},{6,7},{7,6},{8,9},{9,8},{10,11... | collective-permute-start | bytes 3145736 | tf_op jit(solution)/shard_map/ppermute | solution.py:271
  42.5 1.8 %shard_map.51.rest_0_ = f32[8,2,64,1024]{3,2,1,0:T(8,128)S(1)} custom-call(s32[3]{0:T(128)S(1)} %pad_add_fusion.place_ref, bf16[512,1024]{1,0:T(8,128)(2,1)S(1)} %bitcast.41, bf16[1024,1024]{1,0:T(8,128)(2,1)S(1)} %bitcast.44), custom_call_target="tpu_custom_call" | custom-call | flops 1073741824 | bytes 6291456 | tf_op jit(solution)/shard_map/pallas_call | solution.py:126
  44.3 0.4 collective-permute-done.rows_ref.other_ref
  44.8 1.8 %shard_map.52 = f32[8,2,64,1024]{3,2,1,0:T(8,128)S(1)} custom-call(s32[3]{0:T(128)S(1)} %pad_add_fusion.place_ref, bf16[512,1024]{1,0:T(8,128)(2,1)S(1)} %collective-permute-done.rows_ref.other_ref, bf16[1024,1024]{1,0:T(8,128)(2,1)S(1)} %bitcast.45, f32[8,2,64,1024]{3,2,1,0:T(8,128)S(1)} %shard_map.51.rest_0_), custom_call_target="tpu_custom_call", output_to_operand_aliasing={{}: (3, {})} | custom-call | flops 1073741824 | bytes 6291456 | tf_op jit(solution)/shard_map/pallas_call | solution.py:126
  46.7 4.0 %collective-permute-start.2 = (f16[2,64,1024]{2,1,0:T(8,128)(2,1)S(1)}, f16[2,64,1024]{2,1,0:T(8,128)(2,1)S(1)}, u32[]{:S(2)}, u32[]{:S(2)}) collective-permute-start(f16[2,64,1024]{2,1,0:T(8,128)(2,1)S(1)} %fusion.8), channel_id=1, source_target_pairs={{0,448},{1,65},{2,450},{3,67},{4,452},{5,69},{6,454},{7,71},{8,456... | collective-permute-start | bytes 786440 | tf_op jit(solution)/shard_map/ppermute | solution.py:53
  50.7 8.6 %collective-permute-start.3 = (f16[2,64,1024]{2,1,0:T(8,128)(2,1)S(1)}, f16[2,64,1024]{2,1,0:T(8,128)(2,1)S(1)}, u32[]{:S(2)}, u32[]{:S(2)}) collective-permute-start(f16[2,64,1024]{2,1,0:T(8,128)(2,1)S(1)} %fusion.7), channel_id=1, source_target_pairs={{0,64},{1,449},{2,66},{3,451},{4,68},{5,453},{6,70},{7,455},{8,72}... | collective-permute-start | bytes 786440 | tf_op jit(solution)/shard_map/ppermute | solution.py:53
  59.3 3.4 %collective-permute-start.1 = (f16[2,64,1024]{2,1,0:T(8,128)(2,1)S(1)}, f16[2,64,1024]{2,1,0:T(8,128)(2,1)S(1)}, u32[]{:S(2)}, u32[]{:S(2)}) collective-permute-start(f16[2,64,1024]{2,1,0:T(8,128)(2,1)S(1)} %fusion.11), channel_id=1, source_target_pairs={{0,128},{1,385},{2,130},{3,387},{4,132},{5,389},{6,134},{7,391},{8... | collective-permute-start | bytes 786440 | tf_op jit(solution)/shard_map/ppermute | solution.py:53
  62.8 2.2 %collective-permute-start.4 = (f16[2,64,1024]{2,1,0:T(8,128)(2,1)S(1)}, f16[2,64,1024]{2,1,0:T(8,128)(2,1)S(1)}, u32[]{:S(2)}, u32[]{:S(2)}) collective-permute-start(f16[2,64,1024]{2,1,0:T(8,128)(2,1)S(1)} %fusion.9), channel_id=1, source_target_pairs={{0,64},{1,449},{2,66},{3,451},{4,68},{5,453},{6,70},{7,455},{8,72}... | collective-permute-start | bytes 786440 | tf_op jit(solution)/shard_map/ppermute | solution.py:53
  65.0 2.6 %shard_map.53 = f32[2,32,1,128]{3,2,1,0:T(1,128)} custom-call(s32[3]{0:T(128)S(1)} %pad_add_fusion.place_ref, bf16[512,1024]{1,0:T(8,128)(2,1)S(1)} %bitcast.42, bf16[512,1024]{1,0:T(8,128)(2,1)S(1)} %collective-permute-done.rows_ref.other_ref, bf16[512,1024]{1,0:T(8,128)(2,1)S(1)} %copy-done.2, bf16[512,1024]{1,0:T(8,128)(2,1)S(1)} %copy-done.4), custom_call_target="tpu_custom_call" | custom-call | flops 1073741824 | bytes 4194304 | tf_op jit(solution)/shard_map/pallas_call | solution.py:166
  67.7 3.1 %collective-permute-start.5 = (f16[2,64,1024]{2,1,0:T(8,128)(2,1)S(1)}, f16[2,64,1024]{2,1,0:T(8,128)(2,1)S(1)}, u32[]{:S(2)}, u32[]{:S(2)}) collective-permute-start(f16[2,64,1024]{2,1,0:T(8,128)(2,1)S(1)} %fusion.10), channel_id=1, source_target_pairs={{0,448},{1,65},{2,450},{3,67},{4,452},{5,69},{6,454},{7,71},{8,456... | collective-permute-start | bytes 786440 | tf_op jit(solution)/shard_map/ppermute | solution.py:53
  70.8 0.1 fusion.3
  70.9 2.8 %collective-permute-start.7 = (f16[2,64,1024]{2,1,0:T(8,128)(2,1)S(1)}, f16[2,64,1024]{2,1,0:T(8,128)(2,1)S(1)}, u32[]{:S(2)}, u32[]{:S(2)}) collective-permute-start(f16[2,64,1024]{2,1,0:T(8,128)(2,1)S(1)} %fusion.3), channel_id=1, source_target_pairs={{0,384},{1,129},{2,386},{3,131},{4,388},{5,133},{6,390},{7,135},{8... | collective-permute-start | bytes 786440 | tf_op jit(solution)/shard_map/ppermute | solution.py:53
  73.8 0.2 fusion.6
  73.9 4.6 %collective-permute-start.6 = (f16[2,64,1024]{2,1,0:T(8,128)(2,1)S(1)}, f16[2,64,1024]{2,1,0:T(8,128)(2,1)S(1)}, u32[]{:S(2)}, u32[]{:S(2)}) collective-permute-start(f16[2,64,1024]{2,1,0:T(8,128)(2,1)S(1)} %fusion.6), channel_id=1, source_target_pairs={{0,128},{1,385},{2,130},{3,387},{4,132},{5,389},{6,134},{7,391},{8... | collective-permute-start | bytes 786440 | tf_op jit(solution)/shard_map/ppermute | solution.py:53
  78.5 0.1 fusion.1
  78.6 4.7 %all-to-all-start.2 = ((f32[64,1,128]{2,1,0:T(1,128)}), f32[64,1,128]{2,1,0:T(1,128)S(1)}, u32[]{:S(2)}, u32[]{:S(2)}) async-start(f32[64,1,128]{2,1,0:T(1,128)} %bitcast.14), calls=%async_computation.2 | async-start | bytes 65536 | tf_op jit(solution)/shard_map/all_to_all | solution.py:292
  83.3 5.8 %collective-permute-done.6 = f16[2,64,1024]{2,1,0:T(8,128)(2,1)S(1)} collective-permute-done((f16[2,64,1024]{2,1,0:T(8,128)(2,1)S(1)}, f16[2,64,1024]{2,1,0:T(8,128)(2,1)S(1)}, u32[]{:S(2)}, u32[]{:S(2)}) %collective-permute-start.6) | collective-permute-done | bytes 262176 | tf_op jit(solution)/shard_map/ppermute | solution.py:53
  89.1 0.1 multiply_add_fusion.logits_ref
  89.2 3.0 %all-to-all-done.2.terms_ref = f32[64,1,128]{2,1,0:T(1,128)S(1)} async-done(((f32[64,1,128]{2,1,0:T(1,128)}), f32[64,1,128]{2,1,0:T(1,128)S(1)}, u32[]{:S(2)}, u32[]{:S(2)}) %all-to-all-start.2) | async-done | bytes 32800 | tf_op jit(solution)/shard_map/all_to_all | solution.py:292
  92.3 0.9 shard_map.54
  93.2 14.0 %all_to_all.21.messages_ref = f32[64,2,128]{2,1,0:T(2,128)S(1)} all-to-all(f32[64,2,128]{2,1,0:T(2,128)S(1)} %shard_map.54), channel_id=1, replica_groups=mesh['head'=8,'vocab'=64] {'vocab'}, dimensions={0} | all-to-all | bytes 131072 | tf_op jit(solution)/shard_map/all_to_all | solution.py:297
  107.2 1.5 %shard_map.55 = (bf16[128,1024]{1,0:T(8,128)(2,1)}, f32[8,1024]{1,0:T(8,128)}) custom-call(s32[3]{0:T(128)S(1)} %pad_add_fusion.place_ref, f32[2,64,1024]{2,1,0:T(8,128)S(1)} %multiply_add_fusion.logits_ref, f32[64,2,128]{2,1,0:T(2,128)S(1)} %all_to_all.21.messages_ref), custom_call_target="tpu_custom_call" | custom-call | bytes 1048576 | tf_op jit(solution)/shard_map/pallas_call | solution.py:243
  (25 shorter events, 0.4 us)
Async XLA Ops:
  0.6 23.9 %copy-start.6 = (s32[1024]{0:T(1024)S(1)}, s32[1024]{0:T(1024)}, u32[]{:S(2)}) copy-start(s32[1024]{0:T(1024)} %param.5) | copy-start | bytes 12292
  0.6 25.0 %copy-start = (bf16[8,128,1024]{2,1,0:T(8,128)(2,1)S(1)}, bf16[8,128,1024]{2,1,0:T(8,128)(2,1)}, u32[]{:S(2)}) copy-start(bf16[8,128,1024]{2,1,0:T(8,128)(2,1)} %param.4) | copy-start | bytes 6291460
  19.5 17.2 %all-to-all-start.1 = ((bf16[4,8,16,1024]{3,2,1,0:T(8,128)(2,1)}), bf16[4,8,16,1024]{3,2,1,0:T(8,128)(2,1)S(1)}, u32[]{:S(2)}, u32[]{:S(2)}) async-start(bf16[4,8,16,1024]{3,2,1,0:T(8,128)(2,1)} %broadcast_in_dim.15), calls=%async_computation.1 | async-start | bytes 2097152 | tf_op jit(solution)/shard_map/all_to_all | solution.py:41
  25.7 1.0 copy-start.5
  30.6 1.0 copy-start.1
  31.6 1.0 copy-start.3
  36.6 8.1 %collective-permute-start = (bf16[512,1024]{1,0:T(8,128)(2,1)S(1)}, bf16[512,1024]{1,0:T(8,128)(2,1)S(1)}, u32[]{:S(2)}, u32[]{:S(2)}) collective-permute-start(bf16[512,1024]{1,0:T(8,128)(2,1)S(1)} %bitcast.40), channel_id=1, source_target_pairs={{0,1},{1,0},{2,3},{3,2},{4,5},{5,4},{6,7},{7,6},{8,9},{9,8},{10,11... | collective-permute-start | bytes 3145736 | tf_op jit(solution)/shard_map/ppermute | solution.py:271
  44.3 20.6 %copy-start.2 = (bf16[512,1024]{1,0:T(8,128)(2,1)S(1)}, bf16[512,1024]{1,0:T(8,128)(2,1)}, u32[]{:S(2)}) copy-start(bf16[512,1024]{1,0:T(8,128)(2,1)} %copy-done.1) | copy-start | bytes 3145732
  44.3 20.6 %copy-start.4 = (bf16[512,1024]{1,0:T(8,128)(2,1)S(1)}, bf16[512,1024]{1,0:T(8,128)(2,1)}, u32[]{:S(2)}) copy-start(bf16[512,1024]{1,0:T(8,128)(2,1)} %copy-done.3) | copy-start | bytes 3145732
  46.7 24.0 %collective-permute-start.2 = (f16[2,64,1024]{2,1,0:T(8,128)(2,1)S(1)}, f16[2,64,1024]{2,1,0:T(8,128)(2,1)S(1)}, u32[]{:S(2)}, u32[]{:S(2)}) collective-permute-start(f16[2,64,1024]{2,1,0:T(8,128)(2,1)S(1)} %fusion.8), channel_id=1, source_target_pairs={{0,448},{1,65},{2,450},{3,67},{4,452},{5,69},{6,454},{7,71},{8,456... | collective-permute-start | bytes 786440 | tf_op jit(solution)/shard_map/ppermute | solution.py:53
  50.7 23.0 %collective-permute-start.3 = (f16[2,64,1024]{2,1,0:T(8,128)(2,1)S(1)}, f16[2,64,1024]{2,1,0:T(8,128)(2,1)S(1)}, u32[]{:S(2)}, u32[]{:S(2)}) collective-permute-start(f16[2,64,1024]{2,1,0:T(8,128)(2,1)S(1)} %fusion.7), channel_id=1, source_target_pairs={{0,64},{1,449},{2,66},{3,451},{4,68},{5,453},{6,70},{7,455},{8,72}... | collective-permute-start | bytes 786440 | tf_op jit(solution)/shard_map/ppermute | solution.py:53
  59.3 14.4 %collective-permute-start.1 = (f16[2,64,1024]{2,1,0:T(8,128)(2,1)S(1)}, f16[2,64,1024]{2,1,0:T(8,128)(2,1)S(1)}, u32[]{:S(2)}, u32[]{:S(2)}) collective-permute-start(f16[2,64,1024]{2,1,0:T(8,128)(2,1)S(1)} %fusion.11), channel_id=1, source_target_pairs={{0,128},{1,385},{2,130},{3,387},{4,132},{5,389},{6,134},{7,391},{8... | collective-permute-start | bytes 786440 | tf_op jit(solution)/shard_map/ppermute | solution.py:53
  62.8 15.7 %collective-permute-start.4 = (f16[2,64,1024]{2,1,0:T(8,128)(2,1)S(1)}, f16[2,64,1024]{2,1,0:T(8,128)(2,1)S(1)}, u32[]{:S(2)}, u32[]{:S(2)}) collective-permute-start(f16[2,64,1024]{2,1,0:T(8,128)(2,1)S(1)} %fusion.9), channel_id=1, source_target_pairs={{0,64},{1,449},{2,66},{3,451},{4,68},{5,453},{6,70},{7,455},{8,72}... | collective-permute-start | bytes 786440 | tf_op jit(solution)/shard_map/ppermute | solution.py:53
  67.7 10.8 %collective-permute-start.5 = (f16[2,64,1024]{2,1,0:T(8,128)(2,1)S(1)}, f16[2,64,1024]{2,1,0:T(8,128)(2,1)S(1)}, u32[]{:S(2)}, u32[]{:S(2)}) collective-permute-start(f16[2,64,1024]{2,1,0:T(8,128)(2,1)S(1)} %fusion.10), channel_id=1, source_target_pairs={{0,448},{1,65},{2,450},{3,67},{4,452},{5,69},{6,454},{7,71},{8,456... | collective-permute-start | bytes 786440 | tf_op jit(solution)/shard_map/ppermute | solution.py:53
  70.9 12.4 %collective-permute-start.7 = (f16[2,64,1024]{2,1,0:T(8,128)(2,1)S(1)}, f16[2,64,1024]{2,1,0:T(8,128)(2,1)S(1)}, u32[]{:S(2)}, u32[]{:S(2)}) collective-permute-start(f16[2,64,1024]{2,1,0:T(8,128)(2,1)S(1)} %fusion.3), channel_id=1, source_target_pairs={{0,384},{1,129},{2,386},{3,131},{4,388},{5,133},{6,390},{7,135},{8... | collective-permute-start | bytes 786440 | tf_op jit(solution)/shard_map/ppermute | solution.py:53
  73.9 15.2 %collective-permute-start.6 = (f16[2,64,1024]{2,1,0:T(8,128)(2,1)S(1)}, f16[2,64,1024]{2,1,0:T(8,128)(2,1)S(1)}, u32[]{:S(2)}, u32[]{:S(2)}) collective-permute-start(f16[2,64,1024]{2,1,0:T(8,128)(2,1)S(1)} %fusion.6), channel_id=1, source_target_pairs={{0,128},{1,385},{2,130},{3,387},{4,132},{5,389},{6,134},{7,391},{8... | collective-permute-start | bytes 786440 | tf_op jit(solution)/shard_map/ppermute | solution.py:53
  78.6 13.6 %all-to-all-start.2 = ((f32[64,1,128]{2,1,0:T(1,128)}), f32[64,1,128]{2,1,0:T(1,128)S(1)}, u32[]{:S(2)}, u32[]{:S(2)}) async-start(f32[64,1,128]{2,1,0:T(1,128)} %bitcast.14), calls=%async_computation.2 | async-start | bytes 65536 | tf_op jit(solution)/shard_map/all_to_all | solution.py:292

commit v7 on v5

--- a/solution.py
+++ b/solution.py
@@ -210,7 +210,7 @@
     )(place, logits, terms)
 
 
-def finish_kernel(heads, per_device, place_ref, logits_ref, messages_ref, out_ref, attribution_ref):
+def finish_kernel(heads, per_device, place_ref, logits_ref, messages_ref, result_ref, attribution_ref, out_ref, semaphore):
     core = place_ref[1]
     every = messages_ref[:, 0, :]
     size = every.shape[1]
@@ -224,6 +224,8 @@
         for place in range(half // per_device):
             start = (place * NC + c) * per_device
             out_ref[start : start + per_device] = values[place * per_device : (place + 1) * per_device]
+    copy = pltpu.make_async_copy(out_ref, result_ref, semaphore)
+    copy.start()
     shape = (NV, per_device, size)
     token = lax.broadcasted_iota(jnp.int32, shape, 1)
     here = token == lax.broadcasted_iota(jnp.int32, shape, 2) // heads
@@ -239,6 +241,7 @@
         spread = spread.reshape(NV * per_device, size).astype(jnp.bfloat16)
         total += lax.dot_general(same, spread, (((1,), (1,)), ((), ())), preferred_element_type=jnp.float32)
     attribution_ref[...] = total
+    copy.wait()
 
 
 def finish(place, logits, messages, heads, per_device):
@@ -246,11 +249,12 @@
     return pl.pallas_call(
         functools.partial(finish_kernel, heads, per_device),
         in_specs=[SMEM, VMEM, VMEM],
-        out_specs=[VMEM, VMEM],
+        out_specs=[pl.BlockSpec(memory_space=pl.ANY), VMEM],
         out_shape=[
             jax.ShapeDtypeStruct((tokens, slab), jnp.bfloat16),
             jax.ShapeDtypeStruct((heads, NV * per_device), jnp.float32),
         ],
+        scratch_shapes=[pltpu.VMEM((tokens, slab), jnp.bfloat16), pltpu.SemaphoreType.DMA],
         cost_estimate=cost(0, 1),
         compiler_params=params(),
     )(place, logits, messages)

time: 110 us -> 110 us (level)
  no operation moved by 1% of the time
where the time goes in v7:
time: 110 us
  starting transfers between devices  44.2 us (40%)
  blocking collectives  30.8 us (28%)
  Pallas kernels  13.6 us (12%)
  waiting for transfers between devices  13.2 us (12%)
  local copies, waits for them, and re-layouts  6.12 us (6%)
    ppermute x7, starting transfers between devices, ring(): return lax.ppermute(values, ('head', 'vocab'), pairs)  28.6 us
    all_to_all x1, blocking collectives, share(): lax.all_to_all(copies, 'vocab', 0, 0, axis_index_groups=groups, tiled=True)  16.7 us
    all_to_all x1, blocking collectives, on_device(): messages = lax.all_to_all(message, 'vocab', 0, 0, tiled=True)  14 us
    ppermute x1, starting transfers between devices, on_device(): other = lax.ppermute(own, 'vocab', CORE_SWAP)  5.86 us
    ppermute x7, waiting for transfers between devices, ring(): return lax.ppermute(values, ('head', 'vocab'), pairs)  5.81 us
    all_to_all x1, starting transfers between devices, share(): lax.all_to_all(copies, 'vocab', 0, 0, axis_index_groups=groups, tiled=True)  5.09 us
    all_to_all x1, starting transfers between devices, on_device(): lax.all_to_all(terms, 'vocab', 0, 0, axis_index_groups=CORE_MAJOR, tiled=...  4.67 us
    all_to_all x1, waiting for transfers between devices, share(): lax.all_to_all(copies, 'vocab', 0, 0, axis_index_groups=groups, tiled=True)  4.08 us
  transfers between devices with their start and end apart: 10, of which 4 were waited for; matrix products, arithmetic and copies ran while one was open for 2% of the time, Pallas kernels for 8%

profile of v7, /device:TPU:1, one launch (start us, length us, event | category | flops | bytes accessed | tf_op | source)
XLA Modules:
  0.0 109.6 jit_solution(6636926771742174982)
XLA Ops:
  0.6 0.9 copy.9
  1.6 16.7 %all_to_all.20 = bf16[8,16,1024]{2,1,0:T(8,128)(2,1)S(1)} all-to-all(bf16[8,16,1024]{2,1,0:T(8,128)(2,1)S(1)} %broadcast_in_dim.14), channel_id=1, replica_groups={{0,2,4,6,8,10,12,14},{1,3,5,7,9,11,13,15},{16,18,20,22,24,26,28,30},{17..., dimensions={0} | all-to-all | bytes 524288 | tf_op jit(solution)/shard_map/all_to_all | solution.py:41
  18.3 1.1 %broadcast_in_dim.15 = bf16[4,8,16,1024]{3,2,1,0:T(8,128)(2,1)} broadcast(bf16[8,16,1024]{2,1,0:T(8,128)(2,1)S(1)} %all_to_all.20), dimensions={1,2,3} | broadcast | bytes 1310720 | tf_op jit(solution)/shard_map/broadcast_in_dim | solution.py:40
  19.5 5.1 %all-to-all-start.1 = ((bf16[4,8,16,1024]{3,2,1,0:T(8,128)(2,1)}), bf16[4,8,16,1024]{3,2,1,0:T(8,128)(2,1)S(1)}, u32[]{:S(2)}, u32[]{:S(2)}) async-start(bf16[4,8,16,1024]{3,2,1,0:T(8,128)(2,1)} %broadcast_in_dim.15), calls=%async_computation.1 | async-start | bytes 2097152 | tf_op jit(solution)/shard_map/all_to_all | solution.py:41
  24.6 1.1 copy.6.ids_ref
  25.7 1.0 copy-done.5
  26.7 3.9 %shard_map.50 = (bf16[512,1024]{1,0:T(8,128)(2,1)S(1)}, bf16[512,1024]{1,0:T(8,128)(2,1)S(1)}) custom-call(s32[3]{0:T(128)S(1)} %pad_add_fusion.place_ref, s32[1024,1]{1,0:T(8,128)S(1)} %copy-done.5, bf16[1024,1024]{1,0:T(8,128)(2,1)S(1)} %bitcast.43), custom_call_target="tpu_custom_call" | custom-call | flops 2147483648 | bytes 8388608 | tf_op jit(solution)/shard_map/pallas_call | solution.py:93
  30.6 1.0 copy-done.1
  31.6 1.0 copy-done.3
  32.6 4.1 %all-to-all-done.1 = bf16[4,8,16,1024]{3,2,1,0:T(8,128)(2,1)S(1)} async-done(((bf16[4,8,16,1024]{3,2,1,0:T(8,128)(2,1)}), bf16[4,8,16,1024]{3,2,1,0:T(8,128)(2,1)S(1)}, u32[]{:S(2)}, u32[]{:S(2)}) %all-to-all-start.1) | async-done | bytes 1048608 | tf_op jit(solution)/shard_map/all_to_all | solution.py:41
  36.6 5.9 %collective-permute-start = (bf16[512,1024]{1,0:T(8,128)(2,1)S(1)}, bf16[512,1024]{1,0:T(8,128)(2,1)S(1)}, u32[]{:S(2)}, u32[]{:S(2)}) collective-permute-start(bf16[512,1024]{1,0:T(8,128)(2,1)S(1)} %bitcast.40), channel_id=1, source_target_pairs={{0,1},{1,0},{2,3},{3,2},{4,5},{5,4},{6,7},{7,6},{8,9},{9,8},{10,11... | collective-permute-start | bytes 3145736 | tf_op jit(solution)/shard_map/ppermute | solution.py:278
  42.5 2.0 %shard_map.51.rest_0_ = f32[8,2,64,1024]{3,2,1,0:T(8,128)S(1)} custom-call(s32[3]{0:T(128)S(1)} %pad_add_fusion.place_ref, bf16[512,1024]{1,0:T(8,128)(2,1)S(1)} %bitcast.41, bf16[1024,1024]{1,0:T(8,128)(2,1)S(1)} %bitcast.44), custom_call_target="tpu_custom_call" | custom-call | flops 1073741824 | bytes 6291456 | tf_op jit(solution)/shard_map/pallas_call | solution.py:128
  44.5 0.2 collective-permute-done.rows_ref.other_ref
  44.8 2.0 %shard_map.52 = f32[8,2,64,1024]{3,2,1,0:T(8,128)S(1)} custom-call(s32[3]{0:T(128)S(1)} %pad_add_fusion.place_ref, bf16[512,1024]{1,0:T(8,128)(2,1)S(1)} %collective-permute-done.rows_ref.other_ref, bf16[1024,1024]{1,0:T(8,128)(2,1)S(1)} %bitcast.45, f32[8,2,64,1024]{3,2,1,0:T(8,128)S(1)} %shard_map.51.rest_0_), custom_call_target="tpu_custom_call", output_to_operand_aliasing={{}: (3, {})} | custom-call | flops 1073741824 | bytes 6291456 | tf_op jit(solution)/shard_map/pallas_call | solution.py:128
  46.9 4.0 %collective-permute-start.2 = (f16[2,64,1024]{2,1,0:T(8,128)(2,1)S(1)}, f16[2,64,1024]{2,1,0:T(8,128)(2,1)S(1)}, u32[]{:S(2)}, u32[]{:S(2)}) collective-permute-start(f16[2,64,1024]{2,1,0:T(8,128)(2,1)S(1)} %fusion.8), channel_id=1, source_target_pairs={{0,448},{1,65},{2,450},{3,67},{4,452},{5,69},{6,454},{7,71},{8,456... | collective-permute-start | bytes 786440 | tf_op jit(solution)/shard_map/ppermute | solution.py:53
  50.9 8.6 %collective-permute-start.3 = (f16[2,64,1024]{2,1,0:T(8,128)(2,1)S(1)}, f16[2,64,1024]{2,1,0:T(8,128)(2,1)S(1)}, u32[]{:S(2)}, u32[]{:S(2)}) collective-permute-start(f16[2,64,1024]{2,1,0:T(8,128)(2,1)S(1)} %fusion.7), channel_id=1, source_target_pairs={{0,64},{1,449},{2,66},{3,451},{4,68},{5,453},{6,70},{7,455},{8,72}... | collective-permute-start | bytes 786440 | tf_op jit(solution)/shard_map/ppermute | solution.py:53
  59.5 3.4 %collective-permute-start.1 = (f16[2,64,1024]{2,1,0:T(8,128)(2,1)S(1)}, f16[2,64,1024]{2,1,0:T(8,128)(2,1)S(1)}, u32[]{:S(2)}, u32[]{:S(2)}) collective-permute-start(f16[2,64,1024]{2,1,0:T(8,128)(2,1)S(1)} %fusion.11), channel_id=1, source_target_pairs={{0,128},{1,385},{2,130},{3,387},{4,132},{5,389},{6,134},{7,391},{8... | collective-permute-start | bytes 786440 | tf_op jit(solution)/shard_map/ppermute | solution.py:53
  62.9 2.2 %collective-permute-start.4 = (f16[2,64,1024]{2,1,0:T(8,128)(2,1)S(1)}, f16[2,64,1024]{2,1,0:T(8,128)(2,1)S(1)}, u32[]{:S(2)}, u32[]{:S(2)}) collective-permute-start(f16[2,64,1024]{2,1,0:T(8,128)(2,1)S(1)} %fusion.9), channel_id=1, source_target_pairs={{0,64},{1,449},{2,66},{3,451},{4,68},{5,453},{6,70},{7,455},{8,72}... | collective-permute-start | bytes 786440 | tf_op jit(solution)/shard_map/ppermute | solution.py:53
  65.2 2.6 %shard_map.53 = f32[2,32,1,128]{3,2,1,0:T(1,128)} custom-call(s32[3]{0:T(128)S(1)} %pad_add_fusion.place_ref, bf16[512,1024]{1,0:T(8,128)(2,1)S(1)} %bitcast.42, bf16[512,1024]{1,0:T(8,128)(2,1)S(1)} %collective-permute-done.rows_ref.other_ref, bf16[512,1024]{1,0:T(8,128)(2,1)S(1)} %copy-done.2, bf16[512,1024]{1,0:T(8,128)(2,1)S(1)} %copy-done.4), custom_call_target="tpu_custom_call" | custom-call | flops 1073741824 | bytes 4194304 | tf_op jit(solution)/shard_map/pallas_call | solution.py:169
  67.9 3.1 %collective-permute-start.5 = (f16[2,64,1024]{2,1,0:T(8,128)(2,1)S(1)}, f16[2,64,1024]{2,1,0:T(8,128)(2,1)S(1)}, u32[]{:S(2)}, u32[]{:S(2)}) collective-permute-start(f16[2,64,1024]{2,1,0:T(8,128)(2,1)S(1)} %fusion.10), channel_id=1, source_target_pairs={{0,448},{1,65},{2,450},{3,67},{4,452},{5,69},{6,454},{7,71},{8,456... | collective-permute-start | bytes 786440 | tf_op jit(solution)/shard_map/ppermute | solution.py:53
  71.0 0.1 fusion.3
  71.1 2.8 %collective-permute-start.7 = (f16[2,64,1024]{2,1,0:T(8,128)(2,1)S(1)}, f16[2,64,1024]{2,1,0:T(8,128)(2,1)S(1)}, u32[]{:S(2)}, u32[]{:S(2)}) collective-permute-start(f16[2,64,1024]{2,1,0:T(8,128)(2,1)S(1)} %fusion.3), channel_id=1, source_target_pairs={{0,384},{1,129},{2,386},{3,131},{4,388},{5,133},{6,390},{7,135},{8... | collective-permute-start | bytes 786440 | tf_op jit(solution)/shard_map/ppermute | solution.py:53
  73.9 0.2 fusion.6
  74.1 4.6 %collective-permute-start.6 = (f16[2,64,1024]{2,1,0:T(8,128)(2,1)S(1)}, f16[2,64,1024]{2,1,0:T(8,128)(2,1)S(1)}, u32[]{:S(2)}, u32[]{:S(2)}) collective-permute-start(f16[2,64,1024]{2,1,0:T(8,128)(2,1)S(1)} %fusion.6), channel_id=1, source_target_pairs={{0,128},{1,385},{2,130},{3,387},{4,132},{5,389},{6,134},{7,391},{8... | collective-permute-start | bytes 786440 | tf_op jit(solution)/shard_map/ppermute | solution.py:53
  78.7 0.1 fusion.1
  78.8 4.7 %all-to-all-start.2 = ((f32[64,1,128]{2,1,0:T(1,128)}), f32[64,1,128]{2,1,0:T(1,128)S(1)}, u32[]{:S(2)}, u32[]{:S(2)}) async-start(f32[64,1,128]{2,1,0:T(1,128)} %bitcast.14), calls=%async_computation.2 | async-start | bytes 65536 | tf_op jit(solution)/shard_map/all_to_all | solution.py:299
  83.5 5.8 %collective-permute-done.6 = f16[2,64,1024]{2,1,0:T(8,128)(2,1)S(1)} collective-permute-done((f16[2,64,1024]{2,1,0:T(8,128)(2,1)S(1)}, f16[2,64,1024]{2,1,0:T(8,128)(2,1)S(1)}, u32[]{:S(2)}, u32[]{:S(2)}) %collective-permute-start.6) | collective-permute-done | bytes 262176 | tf_op jit(solution)/shard_map/ppermute | solution.py:53
  89.3 0.1 multiply_add_fusion.logits_ref
  89.4 3.0 %all-to-all-done.2.terms_ref = f32[64,1,128]{2,1,0:T(1,128)S(1)} async-done(((f32[64,1,128]{2,1,0:T(1,128)}), f32[64,1,128]{2,1,0:T(1,128)S(1)}, u32[]{:S(2)}, u32[]{:S(2)}) %all-to-all-start.2) | async-done | bytes 32800 | tf_op jit(solution)/shard_map/all_to_all | solution.py:299
  92.5 0.9 shard_map.54
  93.4 14.0 %all_to_all.21.messages_ref = f32[64,2,128]{2,1,0:T(2,128)S(1)} all-to-all(f32[64,2,128]{2,1,0:T(2,128)S(1)} %shard_map.54), channel_id=1, replica_groups=mesh['head'=8,'vocab'=64] {'vocab'}, dimensions={0} | all-to-all | bytes 131072 | tf_op jit(solution)/shard_map/all_to_all | solution.py:304
  107.4 2.2 %shard_map.55 = (bf16[128,1024]{1,0:T(8,128)(2,1)}, f32[8,1024]{1,0:T(8,128)}) custom-call(s32[3]{0:T(128)S(1)} %pad_add_fusion.place_ref, f32[2,64,1024]{2,1,0:T(8,128)S(1)} %multiply_add_fusion.logits_ref, f32[64,2,128]{2,1,0:T(2,128)S(1)} %all_to_all.21.messages_ref), custom_call_target="tpu_custom_call" | custom-call | bytes 1048576 | tf_op jit(solution)/shard_map/pallas_call | solution.py:249
  (25 shorter events, 0.4 us)
Async XLA Ops:
  0.6 23.9 %copy-start.6 = (s32[1024]{0:T(1024)S(1)}, s32[1024]{0:T(1024)}, u32[]{:S(2)}) copy-start(s32[1024]{0:T(1024)} %param.5) | copy-start | bytes 12292
  0.6 25.0 %copy-start = (bf16[8,128,1024]{2,1,0:T(8,128)(2,1)S(1)}, bf16[8,128,1024]{2,1,0:T(8,128)(2,1)}, u32[]{:S(2)}) copy-start(bf16[8,128,1024]{2,1,0:T(8,128)(2,1)} %param.4) | copy-start | bytes 6291460
  19.5 17.2 %all-to-all-start.1 = ((bf16[4,8,16,1024]{3,2,1,0:T(8,128)(2,1)}), bf16[4,8,16,1024]{3,2,1,0:T(8,128)(2,1)S(1)}, u32[]{:S(2)}, u32[]{:S(2)}) async-start(bf16[4,8,16,1024]{3,2,1,0:T(8,128)(2,1)} %broadcast_in_dim.15), calls=%async_computation.1 | async-start | bytes 2097152 | tf_op jit(solution)/shard_map/all_to_all | solution.py:41
  25.7 1.0 copy-start.5
  30.6 1.0 copy-start.1
  31.6 1.0 copy-start.3
  36.6 8.1 %collective-permute-start = (bf16[512,1024]{1,0:T(8,128)(2,1)S(1)}, bf16[512,1024]{1,0:T(8,128)(2,1)S(1)}, u32[]{:S(2)}, u32[]{:S(2)}) collective-permute-start(bf16[512,1024]{1,0:T(8,128)(2,1)S(1)} %bitcast.40), channel_id=1, source_target_pairs={{0,1},{1,0},{2,3},{3,2},{4,5},{5,4},{6,7},{7,6},{8,9},{9,8},{10,11... | collective-permute-start | bytes 3145736 | tf_op jit(solution)/shard_map/ppermute | solution.py:278
  44.5 20.6 %copy-start.2 = (bf16[512,1024]{1,0:T(8,128)(2,1)S(1)}, bf16[512,1024]{1,0:T(8,128)(2,1)}, u32[]{:S(2)}) copy-start(bf16[512,1024]{1,0:T(8,128)(2,1)} %copy-done.1) | copy-start | bytes 3145732
  44.5 20.6 %copy-start.4 = (bf16[512,1024]{1,0:T(8,128)(2,1)S(1)}, bf16[512,1024]{1,0:T(8,128)(2,1)}, u32[]{:S(2)}) copy-start(bf16[512,1024]{1,0:T(8,128)(2,1)} %copy-done.3) | copy-start | bytes 3145732
  46.9 24.0 %collective-permute-start.2 = (f16[2,64,1024]{2,1,0:T(8,128)(2,1)S(1)}, f16[2,64,1024]{2,1,0:T(8,128)(2,1)S(1)}, u32[]{:S(2)}, u32[]{:S(2)}) collective-permute-start(f16[2,64,1024]{2,1,0:T(8,128)(2,1)S(1)} %fusion.8), channel_id=1, source_target_pairs={{0,448},{1,65},{2,450},{3,67},{4,452},{5,69},{6,454},{7,71},{8,456... | collective-permute-start | bytes 786440 | tf_op jit(solution)/shard_map/ppermute | solution.py:53
  50.9 23.0 %collective-permute-start.3 = (f16[2,64,1024]{2,1,0:T(8,128)(2,1)S(1)}, f16[2,64,1024]{2,1,0:T(8,128)(2,1)S(1)}, u32[]{:S(2)}, u32[]{:S(2)}) collective-permute-start(f16[2,64,1024]{2,1,0:T(8,128)(2,1)S(1)} %fusion.7), channel_id=1, source_target_pairs={{0,64},{1,449},{2,66},{3,451},{4,68},{5,453},{6,70},{7,455},{8,72}... | collective-permute-start | bytes 786440 | tf_op jit(solution)/shard_map/ppermute | solution.py:53
  59.5 14.4 %collective-permute-start.1 = (f16[2,64,1024]{2,1,0:T(8,128)(2,1)S(1)}, f16[2,64,1024]{2,1,0:T(8,128)(2,1)S(1)}, u32[]{:S(2)}, u32[]{:S(2)}) collective-permute-start(f16[2,64,1024]{2,1,0:T(8,128)(2,1)S(1)} %fusion.11), channel_id=1, source_target_pairs={{0,128},{1,385},{2,130},{3,387},{4,132},{5,389},{6,134},{7,391},{8... | collective-permute-start | bytes 786440 | tf_op jit(solution)/shard_map/ppermute | solution.py:53
  62.9 15.8 %collective-permute-start.4 = (f16[2,64,1024]{2,1,0:T(8,128)(2,1)S(1)}, f16[2,64,1024]{2,1,0:T(8,128)(2,1)S(1)}, u32[]{:S(2)}, u32[]{:S(2)}) collective-permute-start(f16[2,64,1024]{2,1,0:T(8,128)(2,1)S(1)} %fusion.9), channel_id=1, source_target_pairs={{0,64},{1,449},{2,66},{3,451},{4,68},{5,453},{6,70},{7,455},{8,72}... | collective-permute-start | bytes 786440 | tf_op jit(solution)/shard_map/ppermute | solution.py:53
  67.9 10.8 %collective-permute-start.5 = (f16[2,64,1024]{2,1,0:T(8,128)(2,1)S(1)}, f16[2,64,1024]{2,1,0:T(8,128)(2,1)S(1)}, u32[]{:S(2)}, u32[]{:S(2)}) collective-permute-start(f16[2,64,1024]{2,1,0:T(8,128)(2,1)S(1)} %fusion.10), channel_id=1, source_target_pairs={{0,448},{1,65},{2,450},{3,67},{4,452},{5,69},{6,454},{7,71},{8,456... | collective-permute-start | bytes 786440 | tf_op jit(solution)/shard_map/ppermute | solution.py:53
  71.1 12.4 %collective-permute-start.7 = (f16[2,64,1024]{2,1,0:T(8,128)(2,1)S(1)}, f16[2,64,1024]{2,1,0:T(8,128)(2,1)S(1)}, u32[]{:S(2)}, u32[]{:S(2)}) collective-permute-start(f16[2,64,1024]{2,1,0:T(8,128)(2,1)S(1)} %fusion.3), channel_id=1, source_target_pairs={{0,384},{1,129},{2,386},{3,131},{4,388},{5,133},{6,390},{7,135},{8... | collective-permute-start | bytes 786440 | tf_op jit(solution)/shard_map/ppermute | solution.py:53
  74.1 15.2 %collective-permute-start.6 = (f16[2,64,1024]{2,1,0:T(8,128)(2,1)S(1)}, f16[2,64,1024]{2,1,0:T(8,128)(2,1)S(1)}, u32[]{:S(2)}, u32[]{:S(2)}) collective-permute-start(f16[2,64,1024]{2,1,0:T(8,128)(2,1)S(1)} %fusion.6), channel_id=1, source_target_pairs={{0,128},{1,385},{2,130},{3,387},{4,132},{5,389},{6,134},{7,391},{8... | collective-permute-start | bytes 786440 | tf_op jit(solution)/shard_map/ppermute | solution.py:53
  78.8 13.7 %all-to-all-start.2 = ((f32[64,1,128]{2,1,0:T(1,128)}), f32[64,1,128]{2,1,0:T(1,128)S(1)}, u32[]{:S(2)}, u32[]{:S(2)}) async-start(f32[64,1,128]{2,1,0:T(1,128)} %bitcast.14), calls=%async_computation.2 | async-start | bytes 65536 | tf_op jit(solution)/shard_map/all_to_all | solution.py:299

commit v8 on v4

--- a/solution.py
+++ b/solution.py
@@ -274,10 +274,10 @@
     sums = partial_sums(place, own, weights)
     sums = partial_sums(place, tied(other, sums), weights, sums)
 
-    sent = coded(sums[0])
+    sent = coded(sums[2])
+    three = ring(sent, AHEAD)
+    sent = coded(tied(sums, sent)[0])
     four = ring(sent, AHEAD_TWO)
-    sent = coded(tied(sums, sent)[2])
-    three = ring(sent, AHEAD)
     sent = coded(tied(sums, sent)[1])
     five = ring(sent, BACK)
     sent = coded(tied(sums, sent)[6])

time: 110 us -> 110 us (level)
  transfers between devices with their start and end apart: 10 -> 10, of which waited for: 4 -> 5; matrix products, arithmetic and copies ran while one was open for 3% -> 3% of each run, Pallas kernels for 8% -> 8%
where the time goes in v8:
time: 110 us; the launch traced here: 109 us
  starting transfers between devices  44.2 us (40%)
  blocking collectives  30.8 us (28%)
  Pallas kernels  13.1 us (12%)
  waiting for transfers between devices  12 us (11%)
  local copies, waits for them, and re-layouts  6.1 us (6%)
  other arithmetic  1.88 us (2%)
    ppermute x7, starting transfers between devices, ring(): return lax.ppermute(values, ('head', 'vocab'), pairs)  28.6 us
    all_to_all x1, blocking collectives, share(): lax.all_to_all(copies, 'vocab', 0, 0, axis_index_groups=groups, tiled=True)  16.7 us
    all_to_all x1, blocking collectives, on_device(): messages = lax.all_to_all(message, 'vocab', 0, 0, tiled=True)  14 us
    ppermute x7, waiting for transfers between devices, ring(): return lax.ppermute(values, ('head', 'vocab'), pairs)  5.99 us
    ppermute x1, starting transfers between devices, on_device(): other = lax.ppermute(own, 'vocab', CORE_SWAP)  5.86 us
    all_to_all x1, starting transfers between devices, share(): lax.all_to_all(copies, 'vocab', 0, 0, axis_index_groups=groups, tiled=True)  5.09 us
    all_to_all x1, starting transfers between devices, on_device(): lax.all_to_all(terms, 'vocab', 0, 0, axis_index_groups=CORE_MAJOR, tiled=...  4.66 us
    all_to_all x1, waiting for transfers between devices, share(): lax.all_to_all(copies, 'vocab', 0, 0, axis_index_groups=groups, tiled=True)  4.09 us
  transfers between devices with their start and end apart: 10, of which 5 were waited for; matrix products, arithmetic and copies ran while one was open for 3% of the time, Pallas kernels for 8%

profile of v8, /device:TPU:1, one launch (start us, length us, event | category | flops | bytes accessed | tf_op | source)
XLA Modules:
  0.0 109.0 jit_solution(2890880330392217776)
XLA Ops:
  0.6 0.9 copy.9
  1.6 16.7 %all_to_all.20 = bf16[8,16,1024]{2,1,0:T(8,128)(2,1)S(1)} all-to-all(bf16[8,16,1024]{2,1,0:T(8,128)(2,1)S(1)} %broadcast_in_dim.14), channel_id=1, replica_groups={{0,2,4,6,8,10,12,14},{1,3,5,7,9,11,13,15},{16,18,20,22,24,26,28,30},{17..., dimensions={0} | all-to-all | bytes 524288 | tf_op jit(solution)/shard_map/all_to_all | solution.py:41
  18.3 1.1 %broadcast_in_dim.15 = bf16[4,8,16,1024]{3,2,1,0:T(8,128)(2,1)} broadcast(bf16[8,16,1024]{2,1,0:T(8,128)(2,1)S(1)} %all_to_all.20), dimensions={1,2,3} | broadcast | bytes 1310720 | tf_op jit(solution)/shard_map/broadcast_in_dim | solution.py:40
  19.4 5.1 %all-to-all-start.1 = ((bf16[4,8,16,1024]{3,2,1,0:T(8,128)(2,1)}), bf16[4,8,16,1024]{3,2,1,0:T(8,128)(2,1)S(1)}, u32[]{:S(2)}, u32[]{:S(2)}) async-start(bf16[4,8,16,1024]{3,2,1,0:T(8,128)(2,1)} %broadcast_in_dim.15), calls=%async_computation.1 | async-start | bytes 2097152 | tf_op jit(solution)/shard_map/all_to_all | solution.py:41
  24.5 1.0 copy.6.ids_ref
  25.7 1.0 copy-done.6
  26.7 3.9 %shard_map.50 = (bf16[512,1024]{1,0:T(8,128)(2,1)S(1)}, bf16[512,1024]{1,0:T(8,128)(2,1)S(1)}) custom-call(s32[3]{0:T(128)S(1)} %pad_add_fusion.place_ref, s32[1024,1]{1,0:T(8,128)S(1)} %copy-done.6, bf16[1024,1024]{1,0:T(8,128)(2,1)S(1)} %bitcast.47), custom_call_target="tpu_custom_call" | custom-call | flops 2147483648 | bytes 8388608 | tf_op jit(solution)/shard_map/pallas_call | solution.py:93
  30.6 1.0 copy-done.2
  31.6 1.0 copy-done.4
  32.5 4.1 %all-to-all-done.1 = bf16[4,8,16,1024]{3,2,1,0:T(8,128)(2,1)S(1)} async-done(((bf16[4,8,16,1024]{3,2,1,0:T(8,128)(2,1)}), bf16[4,8,16,1024]{3,2,1,0:T(8,128)(2,1)S(1)}, u32[]{:S(2)}, u32[]{:S(2)}) %all-to-all-start.1) | async-done | bytes 1048608 | tf_op jit(solution)/shard_map/all_to_all | solution.py:41
  36.6 5.9 %collective-permute-start = (bf16[512,1024]{1,0:T(8,128)(2,1)S(1)}, bf16[512,1024]{1,0:T(8,128)(2,1)S(1)}, u32[]{:S(2)}, u32[]{:S(2)}) collective-permute-start(bf16[512,1024]{1,0:T(8,128)(2,1)S(1)} %bitcast.44), channel_id=1, source_target_pairs={{0,1},{1,0},{2,3},{3,2},{4,5},{5,4},{6,7},{7,6},{8,9},{9,8},{10,11... | collective-permute-start | bytes 3145736 | tf_op jit(solution)/shard_map/ppermute | solution.py:273
  42.5 2.0 %shard_map.51.rest_0_ = f32[8,2,64,1024]{3,2,1,0:T(8,128)S(1)} custom-call(s32[3]{0:T(128)S(1)} %pad_add_fusion.place_ref, bf16[512,1024]{1,0:T(8,128)(2,1)S(1)} %bitcast.45, bf16[1024,1024]{1,0:T(8,128)(2,1)S(1)} %bitcast.48), custom_call_target="tpu_custom_call" | custom-call | flops 1073741824 | bytes 6291456 | tf_op jit(solution)/shard_map/pallas_call | solution.py:128
  44.5 0.2 collective-permute-done.rows_ref.other_ref
  44.8 2.0 %shard_map.52 = f32[8,2,64,1024]{3,2,1,0:T(8,128)S(1)} custom-call(s32[3]{0:T(128)S(1)} %pad_add_fusion.place_ref, bf16[512,1024]{1,0:T(8,128)(2,1)S(1)} %collective-permute-done.rows_ref.other_ref, bf16[1024,1024]{1,0:T(8,128)(2,1)S(1)} %bitcast.49, f32[8,2,64,1024]{3,2,1,0:T(8,128)S(1)} %shard_map.51.rest_0_), custom_call_target="tpu_custom_call", output_to_operand_aliasing={{}: (3, {})} | custom-call | flops 1073741824 | bytes 6291456 | tf_op jit(solution)/shard_map/pallas_call | solution.py:128
  46.9 4.0 %collective-permute-start.1 = (f16[2,64,1024]{2,1,0:T(8,128)(2,1)S(1)}, f16[2,64,1024]{2,1,0:T(8,128)(2,1)S(1)}, u32[]{:S(2)}, u32[]{:S(2)}) collective-permute-start(f16[2,64,1024]{2,1,0:T(8,128)(2,1)S(1)} %fusion.10), channel_id=1, source_target_pairs={{0,448},{1,65},{2,450},{3,67},{4,452},{5,69},{6,454},{7,71},{8,456... | collective-permute-start | bytes 786440 | tf_op jit(solution)/shard_map/ppermute | solution.py:53
  50.9 9.8 %collective-permute-start.2 = (f16[2,64,1024]{2,1,0:T(8,128)(2,1)S(1)}, f16[2,64,1024]{2,1,0:T(8,128)(2,1)S(1)}, u32[]{:S(2)}, u32[]{:S(2)}) collective-permute-start(f16[2,64,1024]{2,1,0:T(8,128)(2,1)S(1)} %fusion.9), channel_id=1, source_target_pairs={{0,128},{1,385},{2,130},{3,387},{4,132},{5,389},{6,134},{7,391},{8... | collective-permute-start | bytes 786440 | tf_op jit(solution)/shard_map/ppermute | solution.py:53
  60.7 2.2 %collective-permute-start.3 = (f16[2,64,1024]{2,1,0:T(8,128)(2,1)S(1)}, f16[2,64,1024]{2,1,0:T(8,128)(2,1)S(1)}, u32[]{:S(2)}, u32[]{:S(2)}) collective-permute-start(f16[2,64,1024]{2,1,0:T(8,128)(2,1)S(1)} %fusion.13), channel_id=1, source_target_pairs={{0,64},{1,449},{2,66},{3,451},{4,68},{5,453},{6,70},{7,455},{8,72}... | collective-permute-start | bytes 786440 | tf_op jit(solution)/shard_map/ppermute | solution.py:53
  62.9 2.2 %collective-permute-start.4 = (f16[2,64,1024]{2,1,0:T(8,128)(2,1)S(1)}, f16[2,64,1024]{2,1,0:T(8,128)(2,1)S(1)}, u32[]{:S(2)}, u32[]{:S(2)}) collective-permute-start(f16[2,64,1024]{2,1,0:T(8,128)(2,1)S(1)} %fusion.11), channel_id=1, source_target_pairs={{0,64},{1,449},{2,66},{3,451},{4,68},{5,453},{6,70},{7,455},{8,72}... | collective-permute-start | bytes 786440 | tf_op jit(solution)/shard_map/ppermute | solution.py:53
  65.2 2.6 %shard_map.53 = f32[2,32,1,128]{3,2,1,0:T(1,128)} custom-call(s32[3]{0:T(128)S(1)} %pad_add_fusion.place_ref, bf16[512,1024]{1,0:T(8,128)(2,1)S(1)} %bitcast.46, bf16[512,1024]{1,0:T(8,128)(2,1)S(1)} %collective-permute-done.rows_ref.other_ref, bf16[512,1024]{1,0:T(8,128)(2,1)S(1)} %copy-done.3, bf16[512,1024]{1,0:T(8,128)(2,1)S(1)} %copy-done.5), custom_call_target="tpu_custom_call" | custom-call | flops 1073741824 | bytes 4194304 | tf_op jit(solution)/shard_map/pallas_call | solution.py:169
  67.9 3.1 %collective-permute-start.5 = (f16[2,64,1024]{2,1,0:T(8,128)(2,1)S(1)}, f16[2,64,1024]{2,1,0:T(8,128)(2,1)S(1)}, u32[]{:S(2)}, u32[]{:S(2)}) collective-permute-start(f16[2,64,1024]{2,1,0:T(8,128)(2,1)S(1)} %fusion.12), channel_id=1, source_target_pairs={{0,448},{1,65},{2,450},{3,67},{4,452},{5,69},{6,454},{7,71},{8,456... | collective-permute-start | bytes 786440 | tf_op jit(solution)/shard_map/ppermute | solution.py:53
  71.0 0.2 fusion.6
  71.2 0.1 fusion.8
  71.3 2.8 %collective-permute-start.7 = (f16[2,64,1024]{2,1,0:T(8,128)(2,1)S(1)}, f16[2,64,1024]{2,1,0:T(8,128)(2,1)S(1)}, u32[]{:S(2)}, u32[]{:S(2)}) collective-permute-start(f16[2,64,1024]{2,1,0:T(8,128)(2,1)S(1)} %fusion.8), channel_id=1, source_target_pairs={{0,384},{1,129},{2,386},{3,131},{4,388},{5,133},{6,390},{7,135},{8... | collective-permute-start | bytes 786440 | tf_op jit(solution)/shard_map/ppermute | solution.py:53
  74.1 4.6 %collective-permute-start.6 = (f16[2,64,1024]{2,1,0:T(8,128)(2,1)S(1)}, f16[2,64,1024]{2,1,0:T(8,128)(2,1)S(1)}, u32[]{:S(2)}, u32[]{:S(2)}) collective-permute-start(f16[2,64,1024]{2,1,0:T(8,128)(2,1)S(1)} %fusion.6), channel_id=1, source_target_pairs={{0,128},{1,385},{2,130},{3,387},{4,132},{5,389},{6,134},{7,391},{8... | collective-permute-start | bytes 786440 | tf_op jit(solution)/shard_map/ppermute | solution.py:53
  78.7 4.7 %all-to-all-start.2 = ((f32[64,1,128]{2,1,0:T(1,128)}), f32[64,1,128]{2,1,0:T(1,128)S(1)}, u32[]{:S(2)}, u32[]{:S(2)}) async-start(f32[64,1,128]{2,1,0:T(1,128)} %bitcast.14), calls=%async_computation.2 | async-start | bytes 65536 | tf_op jit(solution)/shard_map/all_to_all | solution.py:294
  83.4 3.1 %collective-permute-done.7 = f16[2,64,1024]{2,1,0:T(8,128)(2,1)S(1)} collective-permute-done((f16[2,64,1024]{2,1,0:T(8,128)(2,1)S(1)}, f16[2,64,1024]{2,1,0:T(8,128)(2,1)S(1)}, u32[]{:S(2)}, u32[]{:S(2)}) %collective-permute-start.7) | collective-permute-done | bytes 262176 | tf_op jit(solution)/shard_map/ppermute | solution.py:53
  86.5 2.9 %collective-permute-done.6 = f16[2,64,1024]{2,1,0:T(8,128)(2,1)S(1)} collective-permute-done((f16[2,64,1024]{2,1,0:T(8,128)(2,1)S(1)}, f16[2,64,1024]{2,1,0:T(8,128)(2,1)S(1)}, u32[]{:S(2)}, u32[]{:S(2)}) %collective-permute-start.6) | collective-permute-done | bytes 262176 | tf_op jit(solution)/shard_map/ppermute | solution.py:53
  89.4 1.3 %fusion.3.logits_ref = f32[2,64,1024]{2,1,0:T(8,128)S(1)} fusion(f16[2,64,1024]{2,1,0:T(8,128)(2,1)S(1)} %collective-permute-done.7, f16[2,64,1024]{2,1,0:T(8,128)(2,1)S(1)} %collective-permute-done.6, f16[2,64,1024]{2,1,0:T(8,128)(2,1)S(1)} %collective-permute-done.5, f16[2,64,1024]{2,1,0:T(8,128)(2,1)S(1)} %collective-permute-done.4, ...), kind=kLoop, calls=%fused_computation.5 | loop fusion | flops 1572864 | bytes 2097152 | tf_op jit(solution)/shard_map/add | solution.py:297
  90.7 1.7 %all-to-all-done.2.terms_ref = f32[64,1,128]{2,1,0:T(1,128)S(1)} async-done(((f32[64,1,128]{2,1,0:T(1,128)}), f32[64,1,128]{2,1,0:T(1,128)S(1)}, u32[]{:S(2)}, u32[]{:S(2)}) %all-to-all-start.2) | async-done | bytes 32800 | tf_op jit(solution)/shard_map/all_to_all | solution.py:294
  92.3 0.9 shard_map.54
  93.3 14.0 %all_to_all.21.messages_ref = f32[64,2,128]{2,1,0:T(2,128)S(1)} all-to-all(f32[64,2,128]{2,1,0:T(2,128)S(1)} %shard_map.54), channel_id=1, replica_groups=mesh['head'=8,'vocab'=64] {'vocab'}, dimensions={0} | all-to-all | bytes 131072 | tf_op jit(solution)/shard_map/all_to_all | solution.py:300
  107.3 1.7 %shard_map.55 = (bf16[128,1024]{1,0:T(8,128)(2,1)}, f32[8,1024]{1,0:T(8,128)}) custom-call(s32[3]{0:T(128)S(1)} %pad_add_fusion.place_ref, f32[2,64,1024]{2,1,0:T(8,128)S(1)} %fusion.3.logits_ref, f32[64,2,128]{2,1,0:T(2,128)S(1)} %all_to_all.21.messages_ref), custom_call_target="tpu_custom_call" | custom-call | bytes 1048576 | tf_op jit(solution)/shard_map/pallas_call | solution.py:245
  (26 shorter events, 0.4 us)
Async XLA Ops:
  0.6 23.9 %copy-start.7 = (s32[1024]{0:T(1024)S(1)}, s32[1024]{0:T(1024)}, u32[]{:S(2)}) copy-start(s32[1024]{0:T(1024)} %param.5) | copy-start | bytes 12292
  0.6 25.0 %copy-start.1 = (bf16[8,128,1024]{2,1,0:T(8,128)(2,1)S(1)}, bf16[8,128,1024]{2,1,0:T(8,128)(2,1)}, u32[]{:S(2)}) copy-start(bf16[8,128,1024]{2,1,0:T(8,128)(2,1)} %param.4) | copy-start | bytes 6291460
  19.4 17.2 %all-to-all-start.1 = ((bf16[4,8,16,1024]{3,2,1,0:T(8,128)(2,1)}), bf16[4,8,16,1024]{3,2,1,0:T(8,128)(2,1)S(1)}, u32[]{:S(2)}, u32[]{:S(2)}) async-start(bf16[4,8,16,1024]{3,2,1,0:T(8,128)(2,1)} %broadcast_in_dim.15), calls=%async_computation.1 | async-start | bytes 2097152 | tf_op jit(solution)/shard_map/all_to_all | solution.py:41
  25.7 1.0 copy-start.6
  30.6 1.0 copy-start.2
  31.5 1.0 copy-start.4
  36.6 8.1 %collective-permute-start = (bf16[512,1024]{1,0:T(8,128)(2,1)S(1)}, bf16[512,1024]{1,0:T(8,128)(2,1)S(1)}, u32[]{:S(2)}, u32[]{:S(2)}) collective-permute-start(bf16[512,1024]{1,0:T(8,128)(2,1)S(1)} %bitcast.44), channel_id=1, source_target_pairs={{0,1},{1,0},{2,3},{3,2},{4,5},{5,4},{6,7},{7,6},{8,9},{9,8},{10,11... | collective-permute-start | bytes 3145736 | tf_op jit(solution)/shard_map/ppermute | solution.py:273
  44.5 20.6 %copy-start.3 = (bf16[512,1024]{1,0:T(8,128)(2,1)S(1)}, bf16[512,1024]{1,0:T(8,128)(2,1)}, u32[]{:S(2)}) copy-start(bf16[512,1024]{1,0:T(8,128)(2,1)} %copy-done.2) | copy-start | bytes 3145732
  44.5 20.6 %copy-start.5 = (bf16[512,1024]{1,0:T(8,128)(2,1)S(1)}, bf16[512,1024]{1,0:T(8,128)(2,1)}, u32[]{:S(2)}) copy-start(bf16[512,1024]{1,0:T(8,128)(2,1)} %copy-done.4) | copy-start | bytes 3145732
  46.7 24.4 %copy-start = (f32[8,2,64,1024]{3,2,1,0:T(8,128)}, f32[8,2,64,1024]{3,2,1,0:T(8,128)S(1)}, u32[]{:S(2)}) copy-start(f32[8,2,64,1024]{3,2,1,0:T(8,128)S(1)} %shard_map.52) | copy-start | bytes 12582916
  46.9 24.2 %collective-permute-start.1 = (f16[2,64,1024]{2,1,0:T(8,128)(2,1)S(1)}, f16[2,64,1024]{2,1,0:T(8,128)(2,1)S(1)}, u32[]{:S(2)}, u32[]{:S(2)}) collective-permute-start(f16[2,64,1024]{2,1,0:T(8,128)(2,1)S(1)} %fusion.10), channel_id=1, source_target_pairs={{0,448},{1,65},{2,450},{3,67},{4,452},{5,69},{6,454},{7,71},{8,456... | collective-permute-start | bytes 786440 | tf_op jit(solution)/shard_map/ppermute | solution.py:53
  50.9 20.0 %collective-permute-start.2 = (f16[2,64,1024]{2,1,0:T(8,128)(2,1)S(1)}, f16[2,64,1024]{2,1,0:T(8,128)(2,1)S(1)}, u32[]{:S(2)}, u32[]{:S(2)}) collective-permute-start(f16[2,64,1024]{2,1,0:T(8,128)(2,1)S(1)} %fusion.9), channel_id=1, source_target_pairs={{0,128},{1,385},{2,130},{3,387},{4,132},{5,389},{6,134},{7,391},{8... | collective-permute-start | bytes 786440 | tf_op jit(solution)/shard_map/ppermute | solution.py:53
  60.7 10.3 %collective-permute-start.3 = (f16[2,64,1024]{2,1,0:T(8,128)(2,1)S(1)}, f16[2,64,1024]{2,1,0:T(8,128)(2,1)S(1)}, u32[]{:S(2)}, u32[]{:S(2)}) collective-permute-start(f16[2,64,1024]{2,1,0:T(8,128)(2,1)S(1)} %fusion.13), channel_id=1, source_target_pairs={{0,64},{1,449},{2,66},{3,451},{4,68},{5,453},{6,70},{7,455},{8,72}... | collective-permute-start | bytes 786440 | tf_op jit(solution)/shard_map/ppermute | solution.py:53
  62.9 20.4 %collective-permute-start.4 = (f16[2,64,1024]{2,1,0:T(8,128)(2,1)S(1)}, f16[2,64,1024]{2,1,0:T(8,128)(2,1)S(1)}, u32[]{:S(2)}, u32[]{:S(2)}) collective-permute-start(f16[2,64,1024]{2,1,0:T(8,128)(2,1)S(1)} %fusion.11), channel_id=1, source_target_pairs={{0,64},{1,449},{2,66},{3,451},{4,68},{5,453},{6,70},{7,455},{8,72}... | collective-permute-start | bytes 786440 | tf_op jit(solution)/shard_map/ppermute | solution.py:53
  67.9 15.5 %collective-permute-start.5 = (f16[2,64,1024]{2,1,0:T(8,128)(2,1)S(1)}, f16[2,64,1024]{2,1,0:T(8,128)(2,1)S(1)}, u32[]{:S(2)}, u32[]{:S(2)}) collective-permute-start(f16[2,64,1024]{2,1,0:T(8,128)(2,1)S(1)} %fusion.12), channel_id=1, source_target_pairs={{0,448},{1,65},{2,450},{3,67},{4,452},{5,69},{6,454},{7,71},{8,456... | collective-permute-start | bytes 786440 | tf_op jit(solution)/shard_map/ppermute | solution.py:53
  71.3 15.2 %collective-permute-start.7 = (f16[2,64,1024]{2,1,0:T(8,128)(2,1)S(1)}, f16[2,64,1024]{2,1,0:T(8,128)(2,1)S(1)}, u32[]{:S(2)}, u32[]{:S(2)}) collective-permute-start(f16[2,64,1024]{2,1,0:T(8,128)(2,1)S(1)} %fusion.8), channel_id=1, source_target_pairs={{0,384},{1,129},{2,386},{3,131},{4,388},{5,133},{6,390},{7,135},{8... | collective-permute-start | bytes 786440 | tf_op jit(solution)/shard_map/ppermute | solution.py:53
  74.1 15.2 %collective-permute-start.6 = (f16[2,64,1024]{2,1,0:T(8,128)(2,1)S(1)}, f16[2,64,1024]{2,1,0:T(8,128)(2,1)S(1)}, u32[]{:S(2)}, u32[]{:S(2)}) collective-permute-start(f16[2,64,1024]{2,1,0:T(8,128)(2,1)S(1)} %fusion.6), channel_id=1, source_target_pairs={{0,128},{1,385},{2,130},{3,387},{4,132},{5,389},{6,134},{7,391},{8... | collective-permute-start | bytes 786440 | tf_op jit(solution)/shard_map/ppermute | solution.py:53
  78.7 13.6 %all-to-all-start.2 = ((f32[64,1,128]{2,1,0:T(1,128)}), f32[64,1,128]{2,1,0:T(1,128)S(1)}, u32[]{:S(2)}, u32[]{:S(2)}) async-start(f32[64,1,128]{2,1,0:T(1,128)} %bitcast.14), calls=%async_computation.2 | async-start | bytes 65536 | tf_op jit(solution)/shard_map/all_to_all | solution.py:294
